TPU v7x, 256 devices: a whole 4x4x8 slice. The times are simulated.
256 devices in a mesh: pair: 16 (over z, x_lo), chan: 16 (over x_hi, y, core).
Axes of the slice: x: 4 (x_hi: 2, x_lo: 2; x = x_hi * 2 + x_lo), y: 4, z: 8, core: 2. Of those that a mesh axis runs over, the one named last changes fastest.
Arguments:
- jones_start: float32 [8, 4, 128, 256], P(None, None, 'chan', 'pair'), may hold values from -4 to 4
- sky_model_products: bfloat16 [256, 8, 4, 128, 256], P('pair', None, None, 'chan'), may hold values from -6 to 6
- measured_correlations: bfloat16 [256, 8, 128, 256], P('pair', None, 'chan'), may hold values from -12 to 12
- retain_marker: int32 [256, 256], P('pair'), may hold values 0 or 1
- slot_rows: int32 [256], P('pair'), may hold values from -1 to 15, as said below
- slot_cols: int32 [256], P('pair'), may hold values from -1 to 15, as said below
Outputs:
- solutions: float32 [8, 4, 128, 256], P(None, None, 'chan', 'pair')
- duals: float32 [8, 4, 128, 256], P(None, None, 'chan', 'pair')
- consensus: float32 [8, 4, 4, 256], P(None, None, None, 'pair')
Inputs may be any that keep to these rules, and one draw needn't show every extreme that they name: A live slot holds one tile of the upper triangle of 16 x 16 station blocks, slot_rows <= slot_cols; every tile is held by exactly one slot; empty slots hold -1 in both lists and follow the live slots of their device; a device holds at most 16 live slots, and some device holds exactly 16. `slot_cols`: column block of the tile in the same slot as slot_rows, -1 in empty slots.
All inputs are finite; a program needn't handle non-finite values. No bound on the sum of `retain_marker` on one device may be relied on, other than what follows from the above.
Results may differ from a plain program's by a relative error of at most 0.0003.
Values may be sent and summed in bfloat16 or wider, within the bound.
No kernel may reach another device: no remote copies, remote signals or barrier semaphores. Data moves between devices by JAX's collectives and lax.ppermute only.
A program may use at most 128 MiB of HBM per device.

v0:
```python
import math

import jax
import jax.numpy as jnp
from jax import lax
from jax.sharding import PartitionSpec as P

STATIONS = 256
BLK = 16
NP = 4
ITERS = 2


RHO = 0.5
MU = 1.0
GROUP_SLOTS = 4


def entries(matrix):
    return [(matrix[2 * e], matrix[2 * e + 1]) for e in range(4)]


def stack_entries(items):
    return jnp.stack([piece for item in items for piece in item])


def cplx_mul(left, right):
    return (left[0] * right[0] - left[1] * right[1], left[0] * right[1] + left[1] * right[0])


def cplx_add(left, right):
    return (left[0] + right[0], left[1] + right[1])


def jones_mul(left, right):
    return [
        cplx_add(cplx_mul(left[0], right[0]), cplx_mul(left[1], right[2])),
        cplx_add(cplx_mul(left[0], right[1]), cplx_mul(left[1], right[3])),
        cplx_add(cplx_mul(left[2], right[0]), cplx_mul(left[3], right[2])),
        cplx_add(cplx_mul(left[2], right[1]), cplx_mul(left[3], right[3])),
    ]


def hermitian(matrix):
    return [
        (matrix[0][0], -matrix[0][1]),
        (matrix[2][0], -matrix[2][1]),
        (matrix[1][0], -matrix[1][1]),
        (matrix[3][0], -matrix[3][1]),
    ]


def poly_basis(total, first, count, terms):
    freqs = (first + jnp.arange(count)).astype(jnp.float32)
    orders = jnp.arange(terms)[:, None].astype(jnp.float32)
    waves = math.sqrt(2.0 / total) * jnp.cos(math.pi * orders * (freqs[None, :] + 0.5) / total)
    return jnp.where(orders == 0.0, math.sqrt(1.0 / total) * jnp.ones_like(waves), waves)


def project(field, basis):
    return jnp.einsum("mf,ckfs->ckms", basis, field, precision=lax.Precision.HIGHEST)


def expand(coeffs, basis):
    return jnp.einsum("mf,ckms->ckfs", basis, coeffs, precision=lax.Precision.HIGHEST)


def group_descent(jones_full, coher, observed, flag_rows, row_blocks, col_blocks):
    blk = BLK
    members = row_blocks.shape[0]
    dirs = coher.shape[2]
    chans = coher.shape[3]
    occupied = (row_blocks >= 0).astype(jnp.float32)
    row_safe = jnp.maximum(row_blocks, 0)
    col_safe = jnp.maximum(col_blocks, 0)
    upper_square = (jnp.arange(blk)[:, None] < jnp.arange(blk)[None, :]).astype(jnp.float32)
    same_block = (row_safe == col_safe)[:, None, None]
    keep_mask = flag_rows.astype(jnp.float32).reshape(members, blk, blk) * jnp.where(
        same_block, upper_square[None], 1.0
    )
    keep_mask = (keep_mask * occupied[:, None, None])[:, None, None]

    def take_block(block):
        return lax.dynamic_slice_in_dim(jones_full, block * blk, blk, 3)

    row_jones = jnp.moveaxis(jax.vmap(take_block)(row_safe), 1, 0)
    col_jones = jnp.moveaxis(jax.vmap(take_block)(col_safe), 1, 0)
    coher_view = jnp.moveaxis(coher, 1, 0).reshape(8, members, dirs, chans, blk, blk)
    coher_full = entries(coher_view.astype(jnp.float32))
    observed_view = jnp.moveaxis(observed, 1, 0).reshape(8, members, 1, chans, blk, blk)
    vis_full = entries(observed_view.astype(jnp.float32))
    left_jones = entries(row_jones[..., :, None])
    right_jones = entries(col_jones[..., None, :])
    left_coh = jones_mul(left_jones, coher_full)
    predicted = jones_mul(left_coh, hermitian(right_jones))
    residual = [
        (
            (seen[0] - jnp.sum(model[0], axis=1, keepdims=True)) * keep_mask,
            (seen[1] - jnp.sum(model[1], axis=1, keepdims=True)) * keep_mask,
        )
        for seen, model in zip(vis_full, predicted)
    ]
    row_terms = jones_mul(residual, jones_mul(right_jones, hermitian(coher_full)))
    col_terms = jones_mul(hermitian(residual), left_coh)
    row_part = stack_entries(
        [(jnp.sum(item[0], axis=-1), jnp.sum(item[1], axis=-1)) for item in row_terms]
    )
    col_part = stack_entries(
        [(jnp.sum(item[0], axis=-2), jnp.sum(item[1], axis=-2)) for item in col_terms]
    )
    return (row_part, col_part, row_safe, col_safe)


def local_descent(
    jones_full, sky_model_products, measured_correlations, retain_marker, slot_rows, slot_cols
):
    slot_count = slot_rows.shape[0]
    groups = slot_count // GROUP_SLOTS
    blocks = jones_full.shape[3] // BLK

    def group_reduce(array):
        return array.reshape((groups, GROUP_SLOTS) + array.shape[1:])

    def one_group(carry, group):
        coher, observed, flag_rows, row_blocks, col_blocks = group
        row_part, col_part, row_safe, col_safe = group_descent(
            jones_full, coher, observed, flag_rows, row_blocks, col_blocks
        )
        return (carry, (row_part, col_part, row_safe, col_safe))

    unused, outputs = lax.scan(
        one_group,
        0,
        (
            group_reduce(sky_model_products),
            group_reduce(measured_correlations),
            group_reduce(retain_marker),
            group_reduce(slot_rows),
            group_reduce(slot_cols),
        ),
    )
    row_parts, col_parts, row_safe, col_safe = outputs

    def flatten_parts(parts):
        moved = jnp.moveaxis(parts, 0, 1)
        return moved.reshape((8, slot_count) + moved.shape[3:])

    block_ids = jnp.arange(blocks)
    row_onehot = (row_safe.reshape(slot_count)[:, None] == block_ids[None, :]).astype(jnp.float32)
    col_onehot = (col_safe.reshape(slot_count)[:, None] == block_ids[None, :]).astype(jnp.float32)
    summed = jnp.einsum(
        "cgkfs,gb->ckfbs", flatten_parts(row_parts), row_onehot, precision=lax.Precision.HIGHEST
    )
    summed = summed + jnp.einsum(
        "cgkfs,gb->ckfbs", flatten_parts(col_parts), col_onehot, precision=lax.Precision.HIGHEST
    )
    return summed.reshape(jones_full.shape)


def share_consensus(field, basis):
    return lax.psum(project(field, basis), "chan")


def local(
    jones_start, sky_model_products, measured_correlations, retain_marker, slot_rows, slot_cols
):
    chan_width = jones_start.shape[2]
    basis = poly_basis(
        chan_width * lax.axis_size("chan"), lax.axis_index("chan") * chan_width, chan_width, NP
    )
    jones_full = lax.all_gather(jones_start, "pair", axis=3, tiled=True)
    jones_now = jones_start
    dual_now = jnp.zeros(jones_start.shape, jnp.float32)
    coeffs = share_consensus(jones_now, basis)
    for iteration in range(ITERS):
        if iteration > 0:
            jones_full = lax.all_gather(jones_now, "pair", axis=3, tiled=True)
        terms = local_descent(
            jones_full,
            sky_model_products,
            measured_correlations,
            retain_marker,
            slot_rows,
            slot_cols,
        )
        descent = lax.psum_scatter(terms, "pair", scatter_dimension=3, tiled=True)
        jones_now = jones_now + MU * (
            descent / STATIONS - dual_now - RHO * (jones_now - expand(coeffs, basis))
        )
        coeffs = share_consensus(jones_now + dual_now / RHO, basis)
        dual_now = dual_now + RHO * (jones_now - expand(coeffs, basis))
    return (jones_now, dual_now, coeffs)


def solution(mesh):
    placed = (
        P(None, None, "chan", "pair"),
        P("pair", None, None, "chan", None),
        P("pair", None, "chan", None),
        P("pair", None),
        P("pair"),
        P("pair"),
    )
    return jax.shard_map(
        local,
        mesh=mesh,
        in_specs=placed,
        out_specs=(
            P(None, None, "chan", "pair"),
            P(None, None, "chan", "pair"),
            P(None, None, None, "pair"),
        ),
        check_vma=False,
    )
```

profile of v0, /device:TPU:1, one launch (start us, length us, event | category | flops | bytes accessed | tf_op | source)
XLA Modules:
  0.0 1247.4 jit_solution(6951353166268425062)
XLA Ops:
  11.7 104.5 %all_gather.6 = f32[8,4,8,256]{2,0,1,3:T(8,128)} all-gather(f32[8,4,8,16]{2,0,1,3:T(8,128)S(1)} %copy.141), channel_id=1, replica_groups=mesh['pair'=16,'chan'=16] {'pair'}, dimensions={3}, use_global_device_ids=true | all-gather | bytes 278528 | tf_op jit(solution)/shard_map/all_gather | solution.py:171
  120.6 381.6 %while.32 = (s32[]{:T(128)}, f32[4,8,4,4,8,16]{5,4,3,2,0,1:T(8,128)}, f32[4,8,4,4,8,16]{5,4,3,2,0,1:T(8,128)}, s32[4,4]{1,0:T(4,128)}, s32[4,4]{1,0:T(4,128)}, /...) while((s32[]{:T(128)}, ...), condition=%wide.region_25.26_spmd, body=%wide.region_0.25_spmd.sunk | while | flops 10498630 | bytes 29081604 | solution.py:131
  163.4 6.6 fusion.155
  181.2 9.6 add_reduce_fusion.54
  258.7 6.6 fusion.155
  276.6 9.6 add_reduce_fusion.54
  354.0 6.6 fusion.155
  371.8 9.6 add_reduce_fusion.54
  449.3 6.6 fusion.155
  467.1 9.6 add_reduce_fusion.54
  513.5 7.1 reshape.807
  521.2 63.4 %psum.21 = f32[8,4,4,16]{3,2,1,0:T(4,128)S(1)} all-reduce(f32[8,4,4,16]{3,2,1,0:T(4,128)S(1)} %convolution_bitcast_fusion.5), channel_id=1, replica_groups=mesh['pair'=16,'chan'=16] {'chan'}, use_global_device_ids=true, to_apply=%region_27.28 | all-reduce | flops 2048 | bytes 16384 | tf_op jit(solution)/shard_map/psum | solution.py:161
  586.6 94.4 %all_gather.7 = f32[8,4,8,256]{2,0,1,3:T(8,128)} all-gather(f32[8,4,8,16]{2,0,1,3:T(8,128)S(1)} %copy.146), channel_id=1, replica_groups=mesh['pair'=16,'chan'=16] {'pair'}, dimensions={3}, use_global_device_ids=true | all-gather | bytes 278528 | tf_op jit(solution)/shard_map/all_gather | solution.py:177
  685.3 382.0 %while.33 = (s32[]{:T(128)}, f32[4,8,4,4,8,16]{5,4,3,2,0,1:T(8,128)}, f32[4,8,4,4,8,16]{5,4,3,2,0,1:T(8,128)}, s32[4,4]{1,0:T(4,128)}, s32[4,4]{1,0:T(4,128)}, /...) while((s32[]{:T(128)}, ...), condition=%wide.region_53.54_spmd, body=%wide.region_28.53_spmd.sunk | while | flops 10498630 | bytes 29081604 | solution.py:131
  728.4 6.6 fusion.163
  746.2 9.6 add_reduce_fusion.57
  823.8 6.6 fusion.163
  841.6 9.6 add_reduce_fusion.57
  919.2 6.6 fusion.163
  937.0 9.6 add_reduce_fusion.57
  1032.4 9.6 add_reduce_fusion.57
  1078.7 7.1 reshape.809
  1086.2 79.6 %psum.22 = f32[8,4,4,16]{3,2,1,0:T(4,128)S(1)} all-reduce(f32[8,4,4,16]{3,2,1,0:T(4,128)S(1)} %convolution_bitcast_fusion.4), channel_id=1, replica_groups=mesh['pair'=16,'chan'=16] {'chan'}, use_global_device_ids=true, to_apply=%region_55.56 | all-reduce | flops 2048 | bytes 16384 | tf_op jit(solution)/shard_map/psum | solution.py:161
  1168.0 71.0 %psum.23 = f32[8,4,4,16]{3,2,1,0:T(4,128)S(1)} all-reduce(f32[8,4,4,16]{3,2,1,0:T(4,128)S(1)} %convolution_bitcast_fusion.3), channel_id=1, replica_groups=mesh['pair'=16,'chan'=16] {'chan'}, use_global_device_ids=true, to_apply=%region_56.57 | all-reduce | flops 2048 | bytes 16384 | tf_op jit(solution)/shard_map/psum | solution.py:161
  (1165 shorter events, 677.1 us)
Async XLA Ops:
  7.2 577.4 %reduce-scatter.7.cloned.1.call-start = ((), (), s32[]{:S(2)}) async-start(), calls=%async_computation.2 | async-start | bytes 278528
  163.4 17.8 %copy-start.50 = (f32[4,4,8,16]{3,2,1,0:T(8,128)S(1)}, f32[4,4,8,16]{3,2,1,0:T(8,128)}, u32[]{:S(2)}) copy-start(f32[4,4,8,16]{3,2,1,0:T(8,128)} %copy.223) | copy-start | bytes 24580 | tf_op jit(solution)/shard_map/while
  163.4 17.8 %copy-start.52 = (f32[4,4,8,16]{3,2,1,0:T(8,128)S(1)}, f32[4,4,8,16]{3,2,1,0:T(8,128)}, u32[]{:S(2)}) copy-start(f32[4,4,8,16]{3,2,1,0:T(8,128)} %copy.225) | copy-start | bytes 24580 | tf_op jit(solution)/shard_map/while
  258.7 17.8 %copy-start.50 = (f32[4,4,8,16]{3,2,1,0:T(8,128)S(1)}, f32[4,4,8,16]{3,2,1,0:T(8,128)}, u32[]{:S(2)}) copy-start(f32[4,4,8,16]{3,2,1,0:T(8,128)} %copy.223) | copy-start | bytes 24580 | tf_op jit(solution)/shard_map/while
  258.7 17.8 %copy-start.52 = (f32[4,4,8,16]{3,2,1,0:T(8,128)S(1)}, f32[4,4,8,16]{3,2,1,0:T(8,128)}, u32[]{:S(2)}) copy-start(f32[4,4,8,16]{3,2,1,0:T(8,128)} %copy.225) | copy-start | bytes 24580 | tf_op jit(solution)/shard_map/while
  354.0 17.8 %copy-start.50 = (f32[4,4,8,16]{3,2,1,0:T(8,128)S(1)}, f32[4,4,8,16]{3,2,1,0:T(8,128)}, u32[]{:S(2)}) copy-start(f32[4,4,8,16]{3,2,1,0:T(8,128)} %copy.223) | copy-start | bytes 24580 | tf_op jit(solution)/shard_map/while
  354.0 17.8 %copy-start.52 = (f32[4,4,8,16]{3,2,1,0:T(8,128)S(1)}, f32[4,4,8,16]{3,2,1,0:T(8,128)}, u32[]{:S(2)}) copy-start(f32[4,4,8,16]{3,2,1,0:T(8,128)} %copy.225) | copy-start | bytes 24580 | tf_op jit(solution)/shard_map/while
  449.3 17.8 %copy-start.50 = (f32[4,4,8,16]{3,2,1,0:T(8,128)S(1)}, f32[4,4,8,16]{3,2,1,0:T(8,128)}, u32[]{:S(2)}) copy-start(f32[4,4,8,16]{3,2,1,0:T(8,128)} %copy.223) | copy-start | bytes 24580 | tf_op jit(solution)/shard_map/while
  449.3 17.8 %copy-start.52 = (f32[4,4,8,16]{3,2,1,0:T(8,128)S(1)}, f32[4,4,8,16]{3,2,1,0:T(8,128)}, u32[]{:S(2)}) copy-start(f32[4,4,8,16]{3,2,1,0:T(8,128)} %copy.225) | copy-start | bytes 24580 | tf_op jit(solution)/shard_map/while
  520.7 645.3 %reduce-scatter.9.cloned.1.call-start = ((), (), s32[]{:S(2)}) async-start(), calls=%async_computation.3 | async-start | bytes 278528
  520.7 160.2 %copy-start.67 = (pred[4]{0:T(512)(128)(4,1)}, pred[4]{0:T(512)(128)(4,1)S(1)}, u32[]{:S(2)}) copy-start(pred[4]{0:T(512)(128)(4,1)S(1)} %convert_compare_fusion) | copy-start | bytes 16
  520.8 160.2 %copy-start.69 = (f32[4]{0:T(128)}, f32[4]{0:T(128)S(1)}, u32[]{:S(2)}) copy-start(f32[4]{0:T(128)S(1)} %convert_multiply_fusion) | copy-start | bytes 52
  520.8 160.2 %copy-start.71 = (f32[8]{0:T(128)}, f32[8]{0:T(128)S(1)}, u32[]{:S(2)}) copy-start(f32[8]{0:T(128)S(1)} %convert_add_fusion) | copy-start | bytes 100
  586.3 94.7 %copy-start.56 = (f32[8,4,8,16]{3,2,1,0:T(8,128)}, f32[8,4,8,16]{3,2,1,0:T(8,128)S(1)}, u32[]{:S(2)}) copy-start(f32[8,4,8,16]{3,2,1,0:T(8,128)S(1)} %fusion.37) | copy-start | bytes 49156
  728.4 17.8 %copy-start.51 = (f32[4,4,8,16]{3,2,1,0:T(8,128)S(1)}, f32[4,4,8,16]{3,2,1,0:T(8,128)}, u32[]{:S(2)}) copy-start(f32[4,4,8,16]{3,2,1,0:T(8,128)} %copy.243) | copy-start | bytes 24580 | tf_op jit(solution)/shard_map/while
  728.4 17.8 %copy-start.53 = (f32[4,4,8,16]{3,2,1,0:T(8,128)S(1)}, f32[4,4,8,16]{3,2,1,0:T(8,128)}, u32[]{:S(2)}) copy-start(f32[4,4,8,16]{3,2,1,0:T(8,128)} %copy.245) | copy-start | bytes 24580 | tf_op jit(solution)/shard_map/while
  755.8 10.1 copy-start.48
  823.8 17.8 %copy-start.51 = (f32[4,4,8,16]{3,2,1,0:T(8,128)S(1)}, f32[4,4,8,16]{3,2,1,0:T(8,128)}, u32[]{:S(2)}) copy-start(f32[4,4,8,16]{3,2,1,0:T(8,128)} %copy.243) | copy-start | bytes 24580 | tf_op jit(solution)/shard_map/while
  823.8 17.8 %copy-start.53 = (f32[4,4,8,16]{3,2,1,0:T(8,128)S(1)}, f32[4,4,8,16]{3,2,1,0:T(8,128)}, u32[]{:S(2)}) copy-start(f32[4,4,8,16]{3,2,1,0:T(8,128)} %copy.245) | copy-start | bytes 24580 | tf_op jit(solution)/shard_map/while
  919.2 17.8 %copy-start.51 = (f32[4,4,8,16]{3,2,1,0:T(8,128)S(1)}, f32[4,4,8,16]{3,2,1,0:T(8,128)}, u32[]{:S(2)}) copy-start(f32[4,4,8,16]{3,2,1,0:T(8,128)} %copy.243) | copy-start | bytes 24580 | tf_op jit(solution)/shard_map/while
  919.2 17.8 %copy-start.53 = (f32[4,4,8,16]{3,2,1,0:T(8,128)S(1)}, f32[4,4,8,16]{3,2,1,0:T(8,128)}, u32[]{:S(2)}) copy-start(f32[4,4,8,16]{3,2,1,0:T(8,128)} %copy.245) | copy-start | bytes 24580 | tf_op jit(solution)/shard_map/while
  1014.6 17.8 %copy-start.51 = (f32[4,4,8,16]{3,2,1,0:T(8,128)S(1)}, f32[4,4,8,16]{3,2,1,0:T(8,128)}, u32[]{:S(2)}) copy-start(f32[4,4,8,16]{3,2,1,0:T(8,128)} %copy.243) | copy-start | bytes 24580 | tf_op jit(solution)/shard_map/while
  1014.6 17.8 %copy-start.53 = (f32[4,4,8,16]{3,2,1,0:T(8,128)S(1)}, f32[4,4,8,16]{3,2,1,0:T(8,128)}, u32[]{:S(2)}) copy-start(f32[4,4,8,16]{3,2,1,0:T(8,128)} %copy.245) | copy-start | bytes 24580 | tf_op jit(solution)/shard_map/while
  1167.7 72.5 %copy-start.59 = (f32[8,4,8,16]{3,2,1,0:T(8,128)}, f32[8,4,8,16]{3,2,1,0:T(8,128)S(1)}, u32[]{:S(2)}) copy-start(f32[8,4,8,16]{3,2,1,0:T(8,128)S(1)} %get-tuple-element.453) | copy-start | bytes 49156
  (231 other events, 1221.6 us)
Sparse Core Ops, SparseCore 0:
  520.8 61.5 reduce-scatter.6
  1086.0 79.9 reduce-scatter.8
where the time goes:
time: 1270 us; the launch traced here: 1250 us
  local copies, waits for them, and re-layouts  547 us (43%)
  blocking collectives  413 us (33%)
  other arithmetic  252 us (20%)
  matrix products  15.7 us (1%)
  between operations  14.7 us (1%)
    psum x3, blocking collectives, share_consensus(): return lax.psum(project(field, basis), 'chan')  214 us
    squeeze x160, local copies, waits for them, and re-layouts, entries(): return [(matrix[2 * e], matrix[2 * e + 1]) for e in range(4)]  187 us
    all_gather x1, blocking collectives, local(): jones_full = lax.all_gather(jones_start, 'pair', axis=3, tiled=True)  105 us
    all_gather x1, blocking collectives, local(): jones_full = lax.all_gather(jones_now, 'pair', axis=3, tiled=True)  94.4 us
    reduce_sum x8, other arithmetic, group_descent(): jnp.sum(model[0], axis=1, keepdims=True)  77 us
    slice x32, local copies, waits for them, and re-layouts, entries(): return [(matrix[2 * e], matrix[2 * e + 1]) for e in range(4)]  73.6 us
    mul x64, local copies, waits for them, and re-layouts, cplx_mul(): left[0] * right[0] - left[1] * right[1]  67.8 us
    gather x16, local copies, waits for them, and re-layouts, take_block(): return lax.dynamic_slice_in_dim(jones_full, block * blk, blk, 3)  52.8 us
  transfers between devices with their start and end apart: 2, of which 1 were waited for; matrix products, arithmetic and copies ran while one was open for 0% of the time, Pallas kernels for 0%

commit v1 on v0

v1 whole, which is shorter than its diff:
```python
import math

import jax
import jax.numpy as jnp
from jax import lax
from jax.experimental import pallas as pl
from jax.experimental.pallas import tpu as pltpu
from jax.sharding import PartitionSpec as P

STATIONS = 256
BLK = 16
NP = 4
RHO = 0.5
MU = 1.0
LANES = 128
CHANS = 8
DIRS = 4
VMEM_LIMIT = 40 * 1024 * 1024


def lane_iota():
    return lax.broadcasted_iota(jnp.int32, (CHANS, LANES), 1)


def pick(vec, index):
    return jnp.take_along_axis(vec, index, axis=1, mode="promise_in_bounds")


def basis_rows(chan, total):
    freq = (chan * CHANS + lax.broadcasted_iota(jnp.int32, (CHANS, LANES), 0)).astype(jnp.float32)
    rows = [jnp.full((CHANS, LANES), math.sqrt(1.0 / total), jnp.float32)]
    for m in range(1, NP):
        rows.append(math.sqrt(2.0 / total) * jnp.cos((math.pi * m) * (freq + 0.5) / total))
    return rows


def project_rows(field, basis):
    return [jnp.sum(basis[m] * field, axis=0, keepdims=True) for m in range(NP)]


def expand_rows(coeffs, basis):
    total = basis[0] * coeffs[0:1]
    for m in range(1, NP):
        total = total + basis[m] * coeffs[m : m + 1]
    return total


def acc_mul(acc, a, b, conj_a=False, conj_b=False, minus=False):
    rr, ii = a[0] * b[0], a[1] * b[1]
    ri, ir = a[0] * b[1], a[1] * b[0]
    sign_ii = -1 if conj_a == conj_b else 1
    sign_ri = -1 if conj_b else 1
    sign_ir = -1 if conj_a else 1
    if minus:
        sign_ii, sign_ri, sign_ir = -sign_ii, -sign_ri, -sign_ir
    sign_rr = -1 if minus else 1

    def put(base, value, sign):
        if base is None:
            return value if sign > 0 else -value
        return base + value if sign > 0 else base - value

    if acc is None:
        real = rr + ii if sign_ii == sign_rr else rr - ii
        if sign_ri == sign_ir:
            imag = ri + ir
        else:
            imag = ri - ir if sign_ri > 0 else ir - ri
        if minus:
            raise ValueError
        return (real, imag)
    return (
        put(put(acc[0], rr, sign_rr), ii, sign_ii),
        put(put(acc[1], ri, sign_ri), ir, sign_ir),
    )


def mat_mul(x, y, acc=None, x_herm=False, y_herm=False, minus=False):
    out = []
    for i in range(2):
        for j in range(2):
            item = None if acc is None else acc[2 * i + j]
            for l in range(2):
                left = x[2 * l + i] if x_herm else x[2 * i + l]
                right = y[2 * j + l] if y_herm else y[2 * l + j]
                item = acc_mul(item, left, right, x_herm, y_herm, minus)
            out.append(item)
    return out


def merge(vectors, dist, lane):
    low = (lane & dist) == 0
    swap = lane ^ dist
    out = []
    for first, second in zip(vectors[0::2], vectors[1::2]):
        kept = jnp.where(low, first, second)
        sent = jnp.where(low, second, first)
        out.append(kept + pick(sent, swap))
    return out


def pairs(list8):
    return [(list8[2 * e], list8[2 * e + 1]) for e in range(4)]


def flat(matrix):
    return [piece for item in matrix for piece in item]


def descent_kernel(rows_ref, cols_ref, jones_ref, coher_ref, seen_ref, marker_ref, out_ref, left_ref, res_ref):
    lane = lane_iota()
    u_lane = lane // BLK
    v_lane = lane % BLK
    out_ref[...] = jnp.zeros_like(out_ref)

    def coher_of(t, k, half):
        kk, odd = k // 2, k % 2
        parts = []
        for e in range(8):
            block = coher_ref[t, e, 16 * kk : 16 * kk + 16, LANES * half : LANES * half + LANES]
            parts.append(block.astype(jnp.float32)[8 * odd : 8 * odd + 8])
        return pairs(parts)

    def expand(block, k, base):
        vec = jones_ref[block, k]
        return pairs([pick(vec, base + e * BLK) for e in range(8)])

    def slot(t, carry):
        a = rows_ref[t]
        b = cols_ref[t]

        @pl.when(a >= 0)
        def _():
            for half in range(2):
                acc = []
                for e in range(4):
                    both = seen_ref[
                        t, 16 * e : 16 * e + 16, LANES * half : LANES * half + LANES
                    ].astype(jnp.float32)
                    acc.append((both[0:8], both[8:16]))
                for k in range(DIRS):
                    coher = coher_of(t, k, half)
                    left = mat_mul(expand(a, k, u_lane + 8 * half), coher)
                    for e, piece in enumerate(flat(left)):
                        left_ref[half, k, e] = piece
                    acc = mat_mul(left, expand(b, k, v_lane), acc, y_herm=True, minus=True)
                mark = marker_ref[t, :, LANES * half : LANES * half + LANES]
                keep = jnp.broadcast_to(mark.astype(jnp.float32), (CHANS, LANES))
                keep = jnp.where((a != b) | (u_lane + 8 * half < v_lane), keep, 0.0)
                for e, piece in enumerate(flat(acc)):
                    res_ref[half, e] = piece * keep
            for k in range(DIRS):
                right = expand(b, k, v_lane)
                row_list = []
                col_list = None
                for half in range(2):
                    res = pairs([res_ref[half, e] for e in range(8)])
                    coher = coher_of(t, k, half)
                    turned = mat_mul(coher, right, y_herm=True)
                    row_list += flat(mat_mul(res, turned, y_herm=True))
                    left = pairs([left_ref[half, k, e] for e in range(8)])
                    if half == 0:
                        col_list = mat_mul(res, left, x_herm=True)
                    else:
                        col_list = mat_mul(res, left, col_list, x_herm=True)
                for dist in (8, 4, 2, 1):
                    row_list = merge(row_list, dist, lane)
                cols = flat(col_list)
                for dist in (64, 32, 16):
                    cols = merge(cols, dist, lane)
                s = lane % BLK
                e = lane // BLK
                j = 8 * (s // 8) + e
                place = (j & 1) * 8 + ((j >> 1) & 1) * 4 + ((j >> 2) & 1) * 2 + ((j >> 3) & 1)
                row_sum = pick(row_list[0], (s % 8) * BLK + place)
                e_back = (e & 1) * 4 + (e & 2) + (e >> 2)
                col_sum = pick(cols[0], e_back * BLK + s)
                out_ref[a, k] = out_ref[a, k] + row_sum
                out_ref[b, k] = out_ref[b, k] + col_sum

        return carry

    lax.fori_loop(0, rows_ref.shape[0], slot, 0)


def local_descent(jones_full, coher, seen, marker, rows, cols):
    blocks = jones_full.shape[0]
    vmem = pl.BlockSpec(memory_space=pltpu.VMEM)
    smem = pl.BlockSpec(memory_space=pltpu.SMEM)
    return pl.pallas_call(
        descent_kernel,
        out_shape=jax.ShapeDtypeStruct((blocks, DIRS, CHANS, LANES), jnp.float32),
        in_specs=[smem, smem, vmem, vmem, vmem, vmem],
        out_specs=vmem,
        scratch_shapes=[
            pltpu.VMEM((2, DIRS, 8, CHANS, LANES), jnp.float32),
            pltpu.VMEM((2, 8, CHANS, LANES), jnp.float32),
        ],
        compiler_params=pltpu.CompilerParams(vmem_limit_bytes=VMEM_LIMIT),
        cost_estimate=pl.CostEstimate(
            flops=40_000_000, bytes_accessed=4_000_000, transcendentals=0
        ),
    )(rows, cols, jones_full, coher, seen, marker)


def to_dense_kernel(total, chan_ref, start_ref, sent_ref, part_ref):
    basis = basis_rows(chan_ref[0], total)
    for k in range(DIRS):
        field = jnp.concatenate([start_ref[e, k] for e in range(8)], axis=1)
        for n in range(sent_ref.shape[0]):
            sent_ref[n, k] = field
        part_ref[k] = jnp.concatenate(project_rows(field, basis), axis=0)


def descent_sum(terms_ref, k):
    parts = [terms_ref[n, k] for n in range(terms_ref.shape[0])]
    while len(parts) > 1:
        parts = [x + y for x, y in zip(parts[0::2], parts[1::2])]
    return parts[0]


def first_update_kernel(total, chan_ref, jones_ref, terms_ref, *refs):
    coeff_refs, (sent_ref, part_ref) = refs[:-2], refs[-2:]
    basis = basis_rows(chan_ref[0], total)
    for k in range(DIRS):
        coeffs = coeff_refs[0][k]
        for ref in coeff_refs[1:]:
            coeffs = coeffs + ref[k]
        now = jones_ref[0, k]
        now = now + MU * (
            descent_sum(terms_ref, k) / STATIONS - RHO * (now - expand_rows(coeffs, basis))
        )
        for n in range(sent_ref.shape[0]):
            sent_ref[n, k] = now
        part_ref[k] = jnp.concatenate(project_rows(now, basis), axis=0)


def second_sum_kernel(total, chan_ref, terms_ref, part_ref, descent_ref, sent_ref):
    basis = basis_rows(chan_ref[0], total)
    for k in range(DIRS):
        descent = descent_sum(terms_ref, k)
        descent_ref[k] = descent
        part = jnp.concatenate(
            [part_ref[k], jnp.concatenate(project_rows(descent, basis), axis=0)], axis=0
        )
        for n in range(sent_ref.shape[0]):
            sent_ref[n, k] = part


def finish_kernel(total, chan_ref, jones_ref, descent_ref, sums_ref, sol_ref, du_ref, co_ref):
    basis = basis_rows(chan_ref[0], total)
    for k in range(DIRS):
        both = descent_sum(sums_ref, k)
        coeffs = both[0:NP]
        now = jones_ref[0, k]
        dual = RHO * (now - expand_rows(coeffs, basis))
        now = now + MU * (descent_ref[k] / STATIONS - dual - dual)
        coeffs = coeffs + (MU / STATIONS) * both[NP : 2 * NP]
        dual = dual + RHO * (now - expand_rows(coeffs, basis))
        for e in range(8):
            part = slice(e * BLK, e * BLK + BLK)
            sol_ref[e, k] = now[:, part]
            du_ref[e, k] = dual[:, part]
            co_ref[e, k] = coeffs[:, part]


def small_call(kernel, total, chan, arrays, shapes):
    vmem = pl.BlockSpec(memory_space=pltpu.VMEM)
    smem = pl.BlockSpec(memory_space=pltpu.SMEM)

    def body(*refs):
        kernel(total, *refs)

    return pl.pallas_call(
        body,
        out_shape=[jax.ShapeDtypeStruct(s, jnp.float32) for s in shapes],
        in_specs=[smem] + [vmem] * len(arrays),
        out_specs=[vmem] * len(shapes),
    )(chan, *arrays)


def flipped(array, bits, count):
    return lax.ppermute(array, "chan", [(i, i ^ bits) for i in range(count)])


def chan_sum_parts(part, count):
    parts = [part]
    bits = [1 << i for i in range(count.bit_length() - 1)]
    order = [bits[0], bits[-1]] + bits[1:-1]
    for i in range(0, len(order), 2):
        total = sum(parts[1:], parts[0])
        chosen = order[i : i + 2]
        masks = chosen + ([chosen[0] | chosen[1]] if len(chosen) == 2 else [])
        parts = [total] + [flipped(total, m, count) for m in masks]
    return parts


def local(start, coher, seen, marker, rows, cols):
    pair_count = lax.axis_size("pair")
    chan_count = lax.axis_size("chan")
    total = CHANS * chan_count
    chan = lax.axis_index("chan").astype(jnp.int32).reshape(1)
    coher = coher.reshape(coher.shape[0], 8, DIRS * CHANS, BLK * BLK)
    seen = seen.reshape(seen.shape[0], 8 * CHANS, BLK * BLK)
    marker = marker.reshape(marker.shape[0], 1, BLK * BLK)
    block = (DIRS, CHANS, LANES)
    blocks = (pair_count,) + block
    poly = (DIRS, NP, LANES)
    sent, part = small_call(to_dense_kernel, total, chan, [start], [blocks, poly])
    full = lax.all_to_all(sent, "pair", 0, 0)
    coeff_parts = chan_sum_parts(part, chan_count)
    terms = local_descent(full, coher, seen, marker, rows, cols)
    terms = lax.all_to_all(terms, "pair", 0, 0)
    sent, part = small_call(
        first_update_kernel, total, chan, [sent, terms] + coeff_parts, [blocks, poly]
    )
    full = lax.all_to_all(sent, "pair", 0, 0)
    terms = local_descent(full, coher, seen, marker, rows, cols)
    terms = lax.all_to_all(terms, "pair", 0, 0)
    descent, sums = small_call(
        second_sum_kernel,
        total,
        chan,
        [terms, part],
        [block, (chan_count, DIRS, 2 * NP, LANES)],
    )
    sums = lax.all_to_all(sums, "chan", 0, 0)
    return small_call(
        finish_kernel,
        total,
        chan,
        [sent, descent, sums],
        [(8, DIRS, CHANS, BLK), (8, DIRS, CHANS, BLK), (8, DIRS, NP, BLK)],
    )


def solution(mesh):
    placed = (
        P(None, None, "chan", "pair"),
        P("pair", None, None, "chan", None),
        P("pair", None, "chan", None),
        P("pair", None),
        P("pair"),
        P("pair"),
    )
    return jax.shard_map(
        local,
        mesh=mesh,
        in_specs=placed,
        out_specs=(
            P(None, None, "chan", "pair"),
            P(None, None, "chan", "pair"),
            P(None, None, None, "pair"),
        ),
        check_vma=False,
    )
```

time: 1270 us -> 136 us (0.11); the launches traced: 1250 us -> 136 us
  local copies, waits for them, and re-layouts: 547 us -> 5.97 us
  blocking collectives: 413 us -> 47.9 us
  other arithmetic: 252 us -> 0.01 us
  Pallas kernels: 0 us -> 41.2 us
  starting transfers between devices: 0.08 us -> 22.6 us
  waiting for transfers between devices: 0.18 us -> 17.1 us
  matrix products: 15.7 us -> 0 us
  between operations: 14.7 us -> 0.73 us
    psum x3 -> x0, blocking collectives: 214 us -> none  [share_consensus(): return lax.psum(project(field, basis), 'chan')]
    all_gather x2 -> x0, blocking collectives: 199 us -> none  [the longest x1 105 us: local(): jones_full = lax.all_gather(jones_start, 'pair', axis=3, tiled=True)]
    squeeze x160 -> x0, local copies, waits for them, and re-layouts: 187 us -> none  [entries(): return [(matrix[2 * e], matrix[2 * e + 1]) for e in range(4)]]
    reduce_sum x24 -> x0, other arithmetic: 135 us -> none  [the longest x8 77 us: group_descent(): jnp.sum(model[0], axis=1, keepdims=True)]
    mul x96 -> x0, local copies, waits for them, and re-layouts: 112 us -> none  [the longest x64 67.8 us: cplx_mul(): left[0] * right[0] - left[1] * right[1]]
    slice x32 -> x0, local copies, waits for them, and re-layouts: 73.6 us -> none  [entries(): return [(matrix[2 * e], matrix[2 * e + 1]) for e in range(4)]]
    gather x16 -> x0, local copies, waits for them, and re-layouts: 52.8 us -> none  [take_block(): return lax.dynamic_slice_in_dim(jones_full, block * blk, blk, 3)]
    add x9 -> x1, other arithmetic: 50.9 us -> 0.01 us  [chan_sum_parts(): total = sum(parts[1:], parts[0])]
  transfers between devices with their start and end apart: 2 -> 8, of which waited for: 1 -> 5; matrix products, arithmetic and copies ran while one was open for 0% -> 1% of each run, Pallas kernels for 0% -> 0%
where the time goes in v1:
time: 136 us
  blocking collectives  47.9 us (35%)
  Pallas kernels  41.2 us (30%)
  starting transfers between devices  22.6 us (17%)
  waiting for transfers between devices  17.1 us (13%)
  local copies, waits for them, and re-layouts  5.97 us (4%)
    pallas_call x2, Pallas kernels, local_descent(): pl.pallas_call(descent_kernel, out_shape=jax.ShapeDtypeStruct((blocks, DI...  34 us
    all_to_all x1, blocking collectives, local(): sums = lax.all_to_all(sums, 'chan', 0, 0)  18 us
    all_to_all x1, blocking collectives, local(): full = lax.all_to_all(sent, 'pair', 0, 0)  16.9 us
    all_to_all x1, blocking collectives, local(): terms = lax.all_to_all(terms, 'pair', 0, 0)  12.9 us
    all_to_all x1, starting transfers between devices, local(): full = lax.all_to_all(sent, 'pair', 0, 0)  10.2 us
    all_to_all x1, waiting for transfers between devices, local(): full = lax.all_to_all(sent, 'pair', 0, 0)  9.76 us
    ppermute x6, starting transfers between devices, flipped(): return lax.ppermute(array, 'chan', [(i, i ^ bits) for i in range(count)])  8.94 us
    ppermute x6, waiting for transfers between devices, flipped(): return lax.ppermute(array, 'chan', [(i, i ^ bits) for i in range(count)])  7.31 us
  transfers between devices with their start and end apart: 8, of which 5 were waited for; matrix products, arithmetic and copies ran while one was open for 1% of the time, Pallas kernels for 0%

profile of v1, /device:TPU:1, one launch (start us, length us, event | category | flops | bytes accessed | tf_op | source)
XLA Modules:
  0.0 135.5 jit_solution(16559616887820521405)
XLA Ops:
  0.6 1.7 %shard_map.85 = (f32[16,4,8,128]{3,2,1,0:T(8,128)}, f32[4,4,128]{2,1,0:T(4,128)}) custom-call(s32[1]{0:T(128)} %bitcast.refs_0_, f32[8,4,8,16]{3,2,1,0:T(8,128)} %refs_1_.1), custom_call_target="tpu_custom_call" | custom-call | tf_op jit(solution)/shard_map/pallas_call | solution.py:274
  2.4 10.2 %all-to-all-start = ((f32[16,4,8,128]{3,2,1,0:T(8,128)}), f32[16,4,8,128]{3,2,1,0:T(8,128)S(1)}, u32[]{:S(2)}, u32[]{:S(2)}) async-start(f32[16,4,8,128]{3,2,1,0:T(8,128)} %get-tuple-element.9.refs_1_), calls=%async_computation | async-start | bytes 524288 | tf_op jit(solution)/shard_map/all_to_all | solution.py:310
  12.5 0.7 reshape.21.marker_ref
  13.3 9.8 %all-to-all-done.jones_ref = f32[16,4,8,128]{3,2,1,0:T(8,128)S(1)} async-done(((f32[16,4,8,128]{3,2,1,0:T(8,128)}), f32[16,4,8,128]{3,2,1,0:T(8,128)S(1)}, u32[]{:S(2)}, u32[]{:S(2)}) %all-to-all-start) | async-done | bytes 262176 | tf_op jit(solution)/shard_map/all_to_all | solution.py:310
  23.0 1.6 %copy-done = bf16[16,8,4,8,256]{4,3,2,1,0:T(8,128)(2,1)S(1)} copy-done((bf16[16,8,4,8,256]{4,3,2,1,0:T(8,128)(2,1)S(1)}, bf16[16,8,4,8,256]{4,3,2,1,0:T(8,128)(2,1)}, u32[]{:S(2)}) %copy-start) | copy-done | bytes 2097176
  24.6 1.0 copy-done.2
  25.7 0.7 copy-done.4
  26.3 0.7 copy-done.6
  27.0 17.4 %shard_map.86 = f32[16,4,8,128]{3,2,1,0:T(8,128)} custom-call(s32[16]{0:T(128)S(1)} %copy-done.4, s32[16]{0:T(128)S(1)} %copy-done.6, f32[16,4,8,128]{3,2,1,0:T(8,128)S(1)} %all-to-all-done.jones_ref, bf16[16,8,32,256]{3,2,1,0:T(8,128)(2,1)S(1)} %bitcast.8, bf16[16,64,256]{2,1,0:T(8,128)(2,1)S(1)} %bitcast.10, s32[16,1,256]{2,1,0:T(1,128)S(1)} %reshape.21.marker_ref), custom_call_target="tpu_custom_call" | custom-call | flops 40000000 | bytes 4000000 | tf_op jit(solution)/shard_map/pallas_call | solution.py:190
  44.4 3.5 %all-to-all-start.1 = ((f32[16,4,8,128]{3,2,1,0:T(8,128)}), f32[16,4,8,128]{3,2,1,0:T(8,128)S(1)}, u32[]{:S(2)}, u32[]{:S(2)}) async-start(f32[16,4,8,128]{3,2,1,0:T(8,128)} %shard_map.86), calls=%async_computation.1 | async-start | bytes 524288 | tf_op jit(solution)/shard_map/all_to_all | solution.py:313
  47.9 4.9 %collective-permute-start.2 = (f32[4,4,128]{2,1,0:T(4,128)S(1)}, f32[4,4,128]{2,1,0:T(4,128)S(1)}, u32[]{:S(2)}, u32[]{:S(2)}) collective-permute-start(f32[4,4,128]{2,1,0:T(4,128)S(1)} %copy-done.13), channel_id=1, source_target_pairs={{0,9},{1,8},{2,11},{3,10},{4,13},{5,12},{6,15},{7,14},{8,1},{9,0},... | collective-permute-start | bytes 24584 | tf_op jit(solution)/shard_map/ppermute | solution.py:283
  53.3 1.6 %collective-permute-done.2 = f32[4,4,128]{2,1,0:T(4,128)S(1)} collective-permute-done((f32[4,4,128]{2,1,0:T(4,128)S(1)}, f32[4,4,128]{2,1,0:T(4,128)S(1)}, u32[]{:S(2)}, u32[]{:S(2)}) %collective-permute-start.2) | collective-permute-done | bytes 8224 | tf_op jit(solution)/shard_map/ppermute | solution.py:283
  55.0 2.2 %collective-permute-done.1 = f32[4,4,128]{2,1,0:T(4,128)S(1)} collective-permute-done((f32[4,4,128]{2,1,0:T(4,128)S(1)}, f32[4,4,128]{2,1,0:T(4,128)S(1)}, u32[]{:S(2)}, u32[]{:S(2)}) %collective-permute-start.1) | collective-permute-done | bytes 8224 | tf_op jit(solution)/shard_map/ppermute | solution.py:283
  57.1 2.8 %collective-permute-start.5 = (f32[4,4,128]{2,1,0:T(4,128)S(1)}, f32[4,4,128]{2,1,0:T(4,128)S(1)}, u32[]{:S(2)}, u32[]{:S(2)}) collective-permute-start(f32[4,4,128]{2,1,0:T(4,128)S(1)} %bitcast.12), channel_id=1, source_target_pairs={{0,6},{1,7},{2,4},{3,5},{4,2},{5,3},{6,0},{7,1},{8,14},{9,15},{10,... | collective-permute-start | bytes 24584 | tf_op jit(solution)/shard_map/ppermute | solution.py:283
  61.0 3.2 %collective-permute-done.4.refs_5_ = f32[4,4,128]{2,1,0:T(4,128)S(1)} collective-permute-done((f32[4,4,128]{2,1,0:T(4,128)S(1)}, f32[4,4,128]{2,1,0:T(4,128)S(1)}, u32[]{:S(2)}, u32[]{:S(2)}) %collective-permute-start.4) | collective-permute-done | bytes 8224 | tf_op jit(solution)/shard_map/ppermute | solution.py:283
  64.2 0.6 copy-done.11
  64.8 0.7 copy-done.8
  65.5 1.9 %shard_map.87 = (f32[16,4,8,128]{3,2,1,0:T(8,128)}, f32[4,4,128]{2,1,0:T(4,128)}) custom-call(s32[1]{0:T(128)} %bitcast.refs_0_, f32[16,4,8,128]{3,2,1,0:T(8,128)} %get-tuple-element.9.refs_1_, f32[16,4,8,128]{3,2,1,0:T(8,128)} %copy-done.8, f32[4,4,128]{2,1,0:T(4,128)} %bitcast.15, f32[4,4,128]{2,1,0:T(4,128)} %copy-done.12, f32[4,4,128]{2,1,0:T(4,128)} %copy-done.11, ...), custom_call_target="tpu_custom_call" | custom-call | tf_op jit(solution)/shard_map/pallas_call | solution.py:274
  67.3 16.9 %all_to_all.25.jones_ref = f32[16,4,8,128]{3,2,1,0:T(8,128)S(1)} all-to-all(f32[16,4,8,128]{3,2,1,0:T(8,128)} %get-tuple-element.11.refs_1_), channel_id=1, replica_groups=mesh['pair'=16,'chan'=16] {'pair'}, dimensions={0} | all-to-all | bytes 524288 | tf_op jit(solution)/shard_map/all_to_all | solution.py:317
  84.3 16.6 %shard_map.88 = f32[16,4,8,128]{3,2,1,0:T(8,128)S(1)} custom-call(s32[16]{0:T(128)S(1)} %copy-done.5, s32[16]{0:T(128)S(1)} %copy-done.7, f32[16,4,8,128]{3,2,1,0:T(8,128)S(1)} %all_to_all.25.jones_ref, bf16[16,8,32,256]{3,2,1,0:T(8,128)(2,1)S(1)} %bitcast.9, bf16[16,64,256]{2,1,0:T(8,128)(2,1)S(1)} %bitcast.11, s32[16,1,256]{2,1,0:T(1,128)S(1)} %reshape.21.marker_ref), custom_call_target="tpu_custom_call" | custom-call | flops 40000000 | bytes 4000000 | tf_op jit(solution)/shard_map/pallas_call | solution.py:190
  100.9 12.9 %all_to_all.26.refs_1_ = f32[16,4,8,128]{3,2,1,0:T(8,128)} all-to-all(f32[16,4,8,128]{3,2,1,0:T(8,128)S(1)} %shard_map.88), channel_id=1, replica_groups=mesh['pair'=16,'chan'=16] {'pair'}, dimensions={0} | all-to-all | bytes 524288 | tf_op jit(solution)/shard_map/all_to_all | solution.py:319
  113.9 1.7 %shard_map.89 = (f32[4,8,128]{2,1,0:T(8,128)}, f32[16,4,8,128]{3,2,1,0:T(8,128)}) custom-call(s32[1]{0:T(128)} %bitcast.refs_0_, f32[16,4,8,128]{3,2,1,0:T(8,128)} %all_to_all.26.refs_1_, f32[4,4,128]{2,1,0:T(4,128)} %get-tuple-element.12.refs_2_), custom_call_target="tpu_custom_call" | custom-call | tf_op jit(solution)/shard_map/pallas_call | solution.py:274
  115.6 18.0 %all_to_all.27.refs_3_ = f32[16,4,8,128]{3,2,1,0:T(8,128)} all-to-all(f32[16,4,8,128]{3,2,1,0:T(8,128)} %get-tuple-element.14), channel_id=1, replica_groups=mesh['pair'=16,'chan'=16] {'chan'}, dimensions={0} | all-to-all | bytes 524288 | tf_op jit(solution)/shard_map/all_to_all | solution.py:327
  133.6 2.0 %shard_map.90 = (f32[8,4,8,16]{3,2,1,0:T(8,128)}, f32[8,4,8,16]{3,2,1,0:T(8,128)}, f32[8,4,4,16]{3,2,1,0:T(4,128)}) custom-call(s32[1]{0:T(128)} %bitcast.refs_0_, f32[16,4,8,128]{3,2,1,0:T(8,128)} %get-tuple-element.11.refs_1_, f32[4,8,128]{2,1,0:T(8,128)} %get-tuple-element.13.refs_2_, f32[16,4,8,128]{3,2,1,0:T(8,128)} %all_to_all.27.refs_3_), custom_call_target="tpu_custom_call" | custom-call | tf_op jit(solution)/shard_map/pallas_call | solution.py:274
  (31 shorter events, 1.6 us)
Async XLA Ops:
  2.4 45.5 %copy-start.13 = (f32[4,4,128]{2,1,0:T(4,128)S(1)}, f32[4,4,128]{2,1,0:T(4,128)}, u32[]{:S(2)}) copy-start(f32[4,4,128]{2,1,0:T(4,128)} %get-tuple-element.10) | copy-start | bytes 24580
  2.4 20.7 %all-to-all-start = ((f32[16,4,8,128]{3,2,1,0:T(8,128)}), f32[16,4,8,128]{3,2,1,0:T(8,128)S(1)}, u32[]{:S(2)}, u32[]{:S(2)}) async-start(f32[16,4,8,128]{3,2,1,0:T(8,128)} %get-tuple-element.9.refs_1_), calls=%async_computation | async-start | bytes 524288 | tf_op jit(solution)/shard_map/all_to_all | solution.py:310
  23.0 1.6 %copy-start = (bf16[16,8,4,8,256]{4,3,2,1,0:T(8,128)(2,1)S(1)}, bf16[16,8,4,8,256]{4,3,2,1,0:T(8,128)(2,1)}, u32[]{:S(2)}) copy-start(bf16[16,8,4,8,256]{4,3,2,1,0:T(8,128)(2,1)} %param.7) | copy-start | bytes 6291460
  24.6 1.0 copy-start.2
  25.7 0.7 copy-start.4
  26.3 0.7 copy-start.6
  27.0 57.3 %copy-start.1 = (bf16[16,8,4,8,256]{4,3,2,1,0:T(8,128)(2,1)S(1)}, bf16[16,8,4,8,256]{4,3,2,1,0:T(8,128)(2,1)}, u32[]{:S(2)}) copy-start(bf16[16,8,4,8,256]{4,3,2,1,0:T(8,128)(2,1)} %param.7) | copy-start | bytes 6291460
  27.0 57.3 %copy-start.3 = (bf16[16,8,8,256]{3,2,1,0:T(8,128)(2,1)S(1)}, bf16[16,8,8,256]{3,2,1,0:T(8,128)(2,1)}, u32[]{:S(2)}) copy-start(bf16[16,8,8,256]{3,2,1,0:T(8,128)(2,1)} %param.8) | copy-start | bytes 1572868
  27.0 57.3 %copy-start.5 = (s32[16]{0:T(128)S(1)}, s32[16]{0:T(128)}, u32[]{:S(2)}) copy-start(s32[16]{0:T(128)} %rows_ref.3) | copy-start | bytes 196
  27.0 57.3 %copy-start.7 = (s32[16]{0:T(128)S(1)}, s32[16]{0:T(128)}, u32[]{:S(2)}) copy-start(s32[16]{0:T(128)} %cols_ref.3) | copy-start | bytes 196
  44.4 19.8 %all-to-all-start.1 = ((f32[16,4,8,128]{3,2,1,0:T(8,128)}), f32[16,4,8,128]{3,2,1,0:T(8,128)S(1)}, u32[]{:S(2)}, u32[]{:S(2)}) async-start(f32[16,4,8,128]{3,2,1,0:T(8,128)} %shard_map.86), calls=%async_computation.1 | async-start | bytes 524288 | tf_op jit(solution)/shard_map/all_to_all | solution.py:313
  47.9 7.1 %collective-permute-start.2 = (f32[4,4,128]{2,1,0:T(4,128)S(1)}, f32[4,4,128]{2,1,0:T(4,128)S(1)}, u32[]{:S(2)}, u32[]{:S(2)}) collective-permute-start(f32[4,4,128]{2,1,0:T(4,128)S(1)} %copy-done.13), channel_id=1, source_target_pairs={{0,9},{1,8},{2,11},{3,10},{4,13},{5,12},{6,15},{7,14},{8,1},{9,0},... | collective-permute-start | bytes 24584 | tf_op jit(solution)/shard_map/ppermute | solution.py:283
  52.8 4.3 %collective-permute-start.1 = (f32[4,4,128]{2,1,0:T(4,128)S(1)}, f32[4,4,128]{2,1,0:T(4,128)S(1)}, u32[]{:S(2)}, u32[]{:S(2)}) collective-permute-start(f32[4,4,128]{2,1,0:T(4,128)S(1)} %copy-done.13), channel_id=1, source_target_pairs={{0,8},{1,9},{2,10},{3,11},{4,12},{5,13},{6,14},{7,15},{8,0},{9,1},... | collective-permute-start | bytes 24584 | tf_op jit(solution)/shard_map/ppermute | solution.py:283
  53.3 3.8 %collective-permute-start = (f32[4,4,128]{2,1,0:T(4,128)S(1)}, f32[4,4,128]{2,1,0:T(4,128)S(1)}, u32[]{:S(2)}, u32[]{:S(2)}) collective-permute-start(f32[4,4,128]{2,1,0:T(4,128)S(1)} %copy-done.13), channel_id=1, source_target_pairs={{0,1},{1,0},{2,3},{3,2},{4,5},{5,4},{6,7},{7,6},{8,9},{9,8},{10,11... | collective-permute-start | bytes 24584 | tf_op jit(solution)/shard_map/ppermute | solution.py:283
  57.1 7.1 %copy-start.9 = (f32[2,8,128]{2,1,0:T(8,128)}, f32[2,8,128]{2,1,0:T(8,128)S(1)}, u32[]{:S(2)}) copy-start(f32[2,8,128]{2,1,0:T(8,128)S(1)} %add_add_fusion) | copy-start | bytes 24580
  57.1 3.9 %collective-permute-start.5 = (f32[4,4,128]{2,1,0:T(4,128)S(1)}, f32[4,4,128]{2,1,0:T(4,128)S(1)}, u32[]{:S(2)}, u32[]{:S(2)}) collective-permute-start(f32[4,4,128]{2,1,0:T(4,128)S(1)} %bitcast.12), channel_id=1, source_target_pairs={{0,6},{1,7},{2,4},{3,5},{4,2},{5,3},{6,0},{7,1},{8,14},{9,15},{10,... | collective-permute-start | bytes 24584 | tf_op jit(solution)/shard_map/ppermute | solution.py:283
  60.0 4.2 %collective-permute-start.4 = (f32[4,4,128]{2,1,0:T(4,128)S(1)}, f32[4,4,128]{2,1,0:T(4,128)S(1)}, u32[]{:S(2)}, u32[]{:S(2)}) collective-permute-start(f32[4,4,128]{2,1,0:T(4,128)S(1)} %bitcast.13), channel_id=1, source_target_pairs={{0,4},{1,5},{2,6},{3,7},{4,0},{5,1},{6,2},{7,3},{8,12},{9,13},{10,... | collective-permute-start | bytes 24584 | tf_op jit(solution)/shard_map/ppermute | solution.py:283
  60.3 3.9 %collective-permute-start.3 = (f32[4,4,128]{2,1,0:T(4,128)S(1)}, f32[4,4,128]{2,1,0:T(4,128)S(1)}, u32[]{:S(2)}, u32[]{:S(2)}) collective-permute-start(f32[4,4,128]{2,1,0:T(4,128)S(1)} %bitcast.14), channel_id=1, source_target_pairs={{0,2},{1,3},{2,0},{3,1},{4,6},{5,7},{6,4},{7,5},{8,10},{9,11},{10,... | collective-permute-start | bytes 24584 | tf_op jit(solution)/shard_map/ppermute | solution.py:283
  61.0 3.2 %copy-start.10 = (f32[4,4,128]{2,1,0:T(4,128)}, f32[4,4,128]{2,1,0:T(4,128)S(1)}, u32[]{:S(2)}) copy-start(f32[4,4,128]{2,1,0:T(4,128)S(1)} %collective-permute-done.5.refs_6_) | copy-start | bytes 24580
  64.2 0.6 copy-start.11
  64.2 0.6 copy-start.12
  64.8 0.7 copy-start.8

commit v2 on v1

--- a/solution.py
+++ b/solution.py
@@ -15,15 +15,11 @@
 LANES = 128
 CHANS = 8
 DIRS = 4
-VMEM_LIMIT = 40 * 1024 * 1024
+VMEM_LIMIT = 32 * 1024 * 1024
 
 
 def lane_iota():
     return lax.broadcasted_iota(jnp.int32, (CHANS, LANES), 1)
-
-
-def pick(vec, index):
-    return jnp.take_along_axis(vec, index, axis=1, mode="promise_in_bounds")
 
 
 def basis_rows(chan, total):
@@ -88,15 +84,12 @@
     return out
 
 
-def merge(vectors, dist, lane):
-    low = (lane & dist) == 0
-    swap = lane ^ dist
-    out = []
-    for first, second in zip(vectors[0::2], vectors[1::2]):
-        kept = jnp.where(low, first, second)
-        sent = jnp.where(low, second, first)
-        out.append(kept + pick(sent, swap))
-    return out
+def mat_entry(x, y, i, j, item=None, x_herm=False, y_herm=False):
+    for l in range(2):
+        left = x[2 * l + i] if x_herm else x[2 * i + l]
+        right = y[2 * j + l] if y_herm else y[2 * l + j]
+        item = acc_mul(item, left, right, x_herm, y_herm)
+    return item
 
 
 def pairs(list8):
@@ -107,11 +100,82 @@
     return [piece for item in matrix for piece in item]
 
 
-def descent_kernel(rows_ref, cols_ref, jones_ref, coher_ref, seen_ref, marker_ref, out_ref, left_ref, res_ref):
+def one_hot(hit):
+    return jnp.where(hit, 1.0, 0.0).astype(jnp.bfloat16)
+
+
+def stage_kernel(rows_ref, cols_ref, marker_ref, keep_ref, spread_ref, sums_ref):
+    source = lax.broadcasted_iota(jnp.int32, (LANES, LANES), 0)
+    target = lax.broadcasted_iota(jnp.int32, (LANES, LANES), 1)
+    tables = [target % BLK, target // BLK, target // BLK + 8]
+    for n in range(24):
+        one = one_hot(source == (n // 3) * BLK + tables[n % 3])
+        spread_ref[0:LANES, n * LANES : n * LANES + LANES] = one
+        spread_ref[LANES : 2 * LANES, n * LANES : n * LANES + LANES] = one
+    for n in range(4):
+        sums_ref[0, n * LANES : n * LANES + LANES] = one_hot(target == 2 * n * BLK + source // BLK)
+        sums_ref[1, n * LANES : n * LANES + LANES] = one_hot(target == 2 * n * BLK + source % BLK)
+
     lane = lane_iota()
-    u_lane = lane // BLK
-    v_lane = lane % BLK
+    for t in range(rows_ref.shape[0]):
+        for half in range(2):
+            mark = marker_ref[t : t + 1, LANES * half : LANES * half + LANES].astype(jnp.float32)
+            keep = jnp.broadcast_to(mark, (CHANS, LANES))
+            off_diagonal = rows_ref[t] != cols_ref[t]
+            upper = lane // BLK + 8 * half < lane % BLK
+            keep = jnp.where((off_diagonal | upper) & (rows_ref[t] >= 0), keep, 0.0)
+            keep_ref[t, half] = keep
+
+
+def stage(marker, rows, cols):
+    slots = rows.shape[0]
+    vmem = pl.BlockSpec(memory_space=pltpu.VMEM)
+    smem = pl.BlockSpec(memory_space=pltpu.SMEM)
+    return pl.pallas_call(
+        stage_kernel,
+        out_shape=[
+            pltpu.VMEM((slots, 2, CHANS, LANES), jnp.float32),
+            pltpu.VMEM((2 * LANES, 24 * LANES), jnp.bfloat16),
+            pltpu.VMEM((2, 4 * LANES, LANES), jnp.bfloat16),
+        ],
+        in_specs=[smem, smem, vmem],
+        out_specs=[vmem] * 3,
+        cost_estimate=pl.CostEstimate(flops=1_000_000, bytes_accessed=2_000_000, transcendentals=0),
+    )(rows, cols, marker)
+
+
+def descent_kernel(
+    rows_ref, cols_ref, jones_ref, coher_hbm, seen_hbm, keep_ref, spread_ref, sums_ref, *refs
+):
+    outer, scratch = refs[:-9], refs[-9:]
+    if len(outer) > 1:
+        part_refs, (out_ref, sum_ref) = outer[:-2], outer[-2:]
+        sum_ref[...] = sum([ref[...] for ref in part_refs[1:]], part_refs[0][...])
+    else:
+        (out_ref,) = outer
+    coher_ref, seen_ref, wide_ref, left_ref, res_ref, row_ref, col_ref, coher_sem, seen_sem = scratch
+    slots = rows_ref.shape[0]
+    blocks = jones_ref.shape[0]
+
+    def copies(t):
+        return (
+            pltpu.make_async_copy(coher_hbm.at[t], coher_ref.at[t], coher_sem.at[t]),
+            pltpu.make_async_copy(seen_hbm.at[t], seen_ref.at[t], seen_sem.at[t]),
+        )
+
+    for t in range(slots):
+        for copy in copies(t):
+            copy.start()
     out_ref[...] = jnp.zeros_like(out_ref)
+
+    dense = jones_ref[...].reshape(blocks * DIRS * CHANS, LANES)
+    high = dense.astype(jnp.bfloat16)
+    low = (dense - high.astype(jnp.float32)).astype(jnp.bfloat16)
+    split = jnp.concatenate([high, low], axis=1)
+    for c in range(12):
+        part = slice(256 * c, 256 * c + 256)
+        wide = jnp.dot(split, spread_ref[:, part], preferred_element_type=jnp.float32)
+        wide_ref[:, :, part] = wide.reshape(blocks * DIRS, CHANS, 256)
 
     def coher_of(t, k, half):
         kk, odd = k // 2, k % 2
@@ -121,86 +185,117 @@
             parts.append(block.astype(jnp.float32)[8 * odd : 8 * odd + 8])
         return pairs(parts)
 
-    def expand(block, k, base):
-        vec = jones_ref[block, k]
-        return pairs([pick(vec, base + e * BLK) for e in range(8)])
-
-    def slot(t, carry):
-        a = rows_ref[t]
-        b = cols_ref[t]
-
-        @pl.when(a >= 0)
-        def _():
+    def expand(block, k, kind):
+        return pairs(
+            [
+                wide_ref[block * DIRS + k, :, (3 * e + kind) * LANES : (3 * e + kind + 1) * LANES]
+                for e in range(8)
+            ]
+        )
+
+    def put(ref, part, item):
+        ref[0:8, part * LANES : part * LANES + LANES] = item[0]
+        ref[8:16, part * LANES : part * LANES + LANES] = item[1]
+
+    def multiply(t, carry):
+        a = jnp.maximum(rows_ref[t], 0)
+        b = jnp.maximum(cols_ref[t], 0)
+        for copy in copies(t):
+            copy.wait()
+        for half in range(2):
+            acc = []
+            for e in range(4):
+                both = seen_ref[
+                    t, 16 * e : 16 * e + 16, LANES * half : LANES * half + LANES
+                ].astype(jnp.float32)
+                acc.append((both[0:8], both[8:16]))
+            for k in range(DIRS):
+                left = mat_mul(expand(a, k, 1 + half), coher_of(t, k, half))
+                for e, piece in enumerate(flat(left)):
+                    left_ref[half, k, e] = piece
+                acc = mat_mul(left, expand(b, k, 0), acc, y_herm=True, minus=True)
+            keep = keep_ref[t, half]
+            for e, piece in enumerate(flat(acc)):
+                res_ref[half, e] = piece * keep
+        for k in range(DIRS):
+            right = expand(b, k, 0)
+            cols = [None] * 4
             for half in range(2):
-                acc = []
+                res = pairs([res_ref[half, e] for e in range(8)])
+                turned = mat_mul(coher_of(t, k, half), right, y_herm=True)
                 for e in range(4):
-                    both = seen_ref[
-                        t, 16 * e : 16 * e + 16, LANES * half : LANES * half + LANES
-                    ].astype(jnp.float32)
-                    acc.append((both[0:8], both[8:16]))
-                for k in range(DIRS):
-                    coher = coher_of(t, k, half)
-                    left = mat_mul(expand(a, k, u_lane + 8 * half), coher)
-                    for e, piece in enumerate(flat(left)):
-                        left_ref[half, k, e] = piece
-                    acc = mat_mul(left, expand(b, k, v_lane), acc, y_herm=True, minus=True)
-                mark = marker_ref[t, :, LANES * half : LANES * half + LANES]
-                keep = jnp.broadcast_to(mark.astype(jnp.float32), (CHANS, LANES))
-                keep = jnp.where((a != b) | (u_lane + 8 * half < v_lane), keep, 0.0)
-                for e, piece in enumerate(flat(acc)):
-                    res_ref[half, e] = piece * keep
+                    item = mat_entry(res, turned, e // 2, e % 2, y_herm=True)
+                    put(row_ref.at[t, k, half], e, item)
+                left = pairs([left_ref[half, k, e] for e in range(8)])
+                for e in range(4):
+                    cols[e] = mat_entry(res, left, e // 2, e % 2, cols[e], x_herm=True)
+                    if half == 1:
+                        put(col_ref.at[t, k], e, cols[e])
+        return carry
+
+    lax.fori_loop(0, slots, multiply, 0)
+
+    group = 8
+
+    def total(values, sums):
+        high = values.astype(jnp.bfloat16)
+        low = (values - high.astype(jnp.float32)).astype(jnp.bfloat16)
+        out = jnp.dot(high, sums, preferred_element_type=jnp.float32)
+        return out + jnp.dot(low, sums, preferred_element_type=jnp.float32)
+
+    def settle(g, carry):
+        t0 = g * group
+        rows = total(row_ref[pl.ds(t0, group)].reshape(group * DIRS * 32, 4 * LANES), sums_ref[0])
+        cols = total(col_ref[pl.ds(t0, group)].reshape(group * DIRS * 16, 4 * LANES), sums_ref[1])
+        rows = rows.reshape(group, DIRS, 2, 2, CHANS, LANES)
+        cols = cols.reshape(group, DIRS, 2, CHANS, LANES)
+        for n in range(group):
+            a = jnp.maximum(rows_ref[t0 + n], 0)
+            b = jnp.maximum(cols_ref[t0 + n], 0)
             for k in range(DIRS):
-                right = expand(b, k, v_lane)
-                row_list = []
-                col_list = None
-                for half in range(2):
-                    res = pairs([res_ref[half, e] for e in range(8)])
-                    coher = coher_of(t, k, half)
-                    turned = mat_mul(coher, right, y_herm=True)
-                    row_list += flat(mat_mul(res, turned, y_herm=True))
-                    left = pairs([left_ref[half, k, e] for e in range(8)])
-                    if half == 0:
-                        col_list = mat_mul(res, left, x_herm=True)
-                    else:
-                        col_list = mat_mul(res, left, col_list, x_herm=True)
-                for dist in (8, 4, 2, 1):
-                    row_list = merge(row_list, dist, lane)
-                cols = flat(col_list)
-                for dist in (64, 32, 16):
-                    cols = merge(cols, dist, lane)
-                s = lane % BLK
-                e = lane // BLK
-                j = 8 * (s // 8) + e
-                place = (j & 1) * 8 + ((j >> 1) & 1) * 4 + ((j >> 2) & 1) * 2 + ((j >> 3) & 1)
-                row_sum = pick(row_list[0], (s % 8) * BLK + place)
-                e_back = (e & 1) * 4 + (e & 2) + (e >> 2)
-                col_sum = pick(cols[0], e_back * BLK + s)
-                out_ref[a, k] = out_ref[a, k] + row_sum
-                out_ref[b, k] = out_ref[b, k] + col_sum
-
+                row = [rows[n, k, 0, c] + pltpu.roll(rows[n, k, 1, c], 8, 1) for c in range(2)]
+                row = row[0] + pltpu.roll(row[1], BLK, 1)
+                out_ref[a, k] = out_ref[a, k] + row
+            for k in range(DIRS):
+                col = cols[n, k, 0] + pltpu.roll(cols[n, k, 1], BLK, 1)
+                out_ref[b, k] = out_ref[b, k] + col
         return carry
 
-    lax.fori_loop(0, rows_ref.shape[0], slot, 0)
-
-
-def local_descent(jones_full, coher, seen, marker, rows, cols):
+    lax.fori_loop(0, slots // group, settle, 0)
+
+
+def local_descent(jones_full, rows, cols, coher, seen, staged, parts):
     blocks = jones_full.shape[0]
+    slots = rows.shape[0]
     vmem = pl.BlockSpec(memory_space=pltpu.VMEM)
     smem = pl.BlockSpec(memory_space=pltpu.SMEM)
+    hbm = pl.BlockSpec(memory_space=pltpu.HBM)
+    tiles = [pltpu.with_memory_space_constraint(x, pltpu.HBM) for x in (coher, seen)]
+    staged = [pltpu.with_memory_space_constraint(x, pltpu.VMEM) for x in staged]
+    out_shape = [jax.ShapeDtypeStruct((blocks, DIRS, CHANS, LANES), jnp.float32)]
+    if len(parts) > 0:
+        out_shape.append(jax.ShapeDtypeStruct(parts[0].shape, jnp.float32))
     return pl.pallas_call(
         descent_kernel,
-        out_shape=jax.ShapeDtypeStruct((blocks, DIRS, CHANS, LANES), jnp.float32),
-        in_specs=[smem, smem, vmem, vmem, vmem, vmem],
-        out_specs=vmem,
+        out_shape=out_shape,
+        in_specs=[smem, smem, vmem, hbm, hbm] + [vmem] * (3 + len(parts)),
+        out_specs=[vmem] * len(out_shape),
         scratch_shapes=[
+            pltpu.VMEM(coher.shape, jnp.bfloat16),
+            pltpu.VMEM(seen.shape, jnp.bfloat16),
+            pltpu.VMEM((blocks * DIRS, CHANS, 24 * LANES), jnp.float32),
             pltpu.VMEM((2, DIRS, 8, CHANS, LANES), jnp.float32),
             pltpu.VMEM((2, 8, CHANS, LANES), jnp.float32),
+            pltpu.VMEM((slots, DIRS, 2, 16, 4 * LANES), jnp.float32),
+            pltpu.VMEM((slots, DIRS, 16, 4 * LANES), jnp.float32),
+            pltpu.SemaphoreType.DMA((slots,)),
+            pltpu.SemaphoreType.DMA((slots,)),
         ],
         compiler_params=pltpu.CompilerParams(vmem_limit_bytes=VMEM_LIMIT),
         cost_estimate=pl.CostEstimate(
             flops=40_000_000, bytes_accessed=4_000_000, transcendentals=0
         ),
-    )(rows, cols, jones_full, coher, seen, marker)
+    )(rows, cols, jones_full, *tiles, *staged, *parts)
 
 
 def to_dense_kernel(total, chan_ref, start_ref, sent_ref, part_ref):
@@ -283,16 +378,11 @@
     return lax.ppermute(array, "chan", [(i, i ^ bits) for i in range(count)])
 
 
-def chan_sum_parts(part, count):
-    parts = [part]
-    bits = [1 << i for i in range(count.bit_length() - 1)]
-    order = [bits[0], bits[-1]] + bits[1:-1]
-    for i in range(0, len(order), 2):
-        total = sum(parts[1:], parts[0])
-        chosen = order[i : i + 2]
-        masks = chosen + ([chosen[0] | chosen[1]] if len(chosen) == 2 else [])
-        parts = [total] + [flipped(total, m, count) for m in masks]
-    return parts
+def exchanged(part, bits, count):
+    masks = [0]
+    for bit in bits:
+        masks += [m ^ bit for m in masks]
+    return [part] + [flipped(part, m, count) for m in masks[1:]]
 
 
 def local(start, coher, seen, marker, rows, cols):
@@ -302,20 +392,22 @@
     chan = lax.axis_index("chan").astype(jnp.int32).reshape(1)
     coher = coher.reshape(coher.shape[0], 8, DIRS * CHANS, BLK * BLK)
     seen = seen.reshape(seen.shape[0], 8 * CHANS, BLK * BLK)
-    marker = marker.reshape(marker.shape[0], 1, BLK * BLK)
+    staged = stage(marker, rows, cols)
     block = (DIRS, CHANS, LANES)
     blocks = (pair_count,) + block
     poly = (DIRS, NP, LANES)
     sent, part = small_call(to_dense_kernel, total, chan, [start], [blocks, poly])
     full = lax.all_to_all(sent, "pair", 0, 0)
-    coeff_parts = chan_sum_parts(part, chan_count)
-    terms = local_descent(full, coher, seen, marker, rows, cols)
+    bits = [1 << i for i in range(chan_count.bit_length() - 1)]
+    parts = exchanged(part, bits[:1] + bits[3:], chan_count)
+    terms, part = local_descent(full, rows, cols, coher, seen, staged, parts)
+    coeff_parts = exchanged(part, bits[1:3], chan_count)
     terms = lax.all_to_all(terms, "pair", 0, 0)
     sent, part = small_call(
         first_update_kernel, total, chan, [sent, terms] + coeff_parts, [blocks, poly]
     )
     full = lax.all_to_all(sent, "pair", 0, 0)
-    terms = local_descent(full, coher, seen, marker, rows, cols)
+    (terms,) = local_descent(full, rows, cols, coher, seen, staged, [])
     terms = lax.all_to_all(terms, "pair", 0, 0)
     descent, sums = small_call(
         second_sum_kernel,

time: 136 us -> 115 us (0.85)
  Pallas kernels: 41.2 us -> 29.6 us
  waiting for transfers between devices: 17.1 us -> 12.1 us
  local copies, waits for them, and re-layouts: 5.97 us -> 2.73 us
    pallas_call x2 -> x3, Pallas kernels: 34 us -> 22.3 us  [the longest x2 21.1 us: local_descent(): pl.pallas_call(descent_kernel, out_shape=out_shape, in_specs=[smem, smem,...]
    all_to_all x1, waiting for transfers between devices: 9.76 us -> 2.22 us  [local(): full = lax.all_to_all(sent, 'pair', 0, 0)]
    all_to_all x1, waiting for transfers between devices: 0.01 us -> 3.02 us  [local(): terms = lax.all_to_all(terms, 'pair', 0, 0)]
    all_to_all x1, blocking collectives: 16.9 us -> 14.4 us  [local(): full = lax.all_to_all(sent, 'pair', 0, 0)]
    unnamed x28 -> x20, local copies, waits for them, and re-layouts: 5.24 us -> 2.73 us
    ppermute x6, starting transfers between devices: 8.94 us -> 7.4 us  [flipped(): return lax.ppermute(array, 'chan', [(i, i ^ bits) for i in range(count)])]
    all_to_all x1, blocking collectives: 18 us -> 19.4 us  [local(): sums = lax.all_to_all(sums, 'chan', 0, 0)]
  transfers between devices with their start and end apart: 8 -> 8, of which waited for: 5 -> 5; matrix products, arithmetic and copies ran while one was open for 1% -> 0% of each run, Pallas kernels for 0% -> 1%
where the time goes in v2:
time: 115 us; the launch traced here: 114 us
  blocking collectives  46.8 us (41%)
  Pallas kernels  29.6 us (26%)
  starting transfers between devices  22.3 us (19%)
  waiting for transfers between devices  12.1 us (11%)
  local copies, waits for them, and re-layouts  2.73 us (2%)
    pallas_call x2, Pallas kernels, local_descent(): pl.pallas_call(descent_kernel, out_shape=out_shape, in_specs=[smem, smem,...  21.1 us
    all_to_all x1, blocking collectives, local(): sums = lax.all_to_all(sums, 'chan', 0, 0)  19.4 us
    all_to_all x1, blocking collectives, local(): full = lax.all_to_all(sent, 'pair', 0, 0)  14.4 us
    all_to_all x1, blocking collectives, local(): terms = lax.all_to_all(terms, 'pair', 0, 0)  13 us
    all_to_all x1, starting transfers between devices, local(): full = lax.all_to_all(sent, 'pair', 0, 0)  10 us
    ppermute x6, starting transfers between devices, flipped(): return lax.ppermute(array, 'chan', [(i, i ^ bits) for i in range(count)])  7.4 us
    pallas_call x4, Pallas kernels, small_call(): pl.pallas_call(body, out_shape=[jax.ShapeDtypeStruct(s, jnp.float32) for...  7.32 us
    ppermute x6, waiting for transfers between devices, flipped(): return lax.ppermute(array, 'chan', [(i, i ^ bits) for i in range(count)])  6.86 us
  transfers between devices with their start and end apart: 8, of which 5 were waited for; matrix products, arithmetic and copies ran while one was open for 0% of the time, Pallas kernels for 1%

profile of v2, /device:TPU:1, one launch (start us, length us, event | category | flops | bytes accessed | tf_op | source)
XLA Modules:
  0.0 114.3 jit_solution(4444188039493731041)
XLA Ops:
  0.6 1.7 %shard_map.85 = (f32[16,4,8,128]{3,2,1,0:T(8,128)}, f32[4,4,128]{2,1,0:T(4,128)}) custom-call(s32[1]{0:T(128)} %bitcast.refs_0_, f32[8,4,8,16]{3,2,1,0:T(8,128)} %refs_1_.1), custom_call_target="tpu_custom_call" | custom-call | tf_op jit(solution)/shard_map/pallas_call | solution.py:369
  2.4 10.0 %all-to-all-start = ((f32[16,4,8,128]{3,2,1,0:T(8,128)}), f32[16,4,8,128]{3,2,1,0:T(8,128)S(1)}, u32[]{:S(2)}, u32[]{:S(2)}) async-start(f32[16,4,8,128]{3,2,1,0:T(8,128)} %get-tuple-element.14.refs_1_), calls=%async_computation | async-start | bytes 524288 | tf_op jit(solution)/shard_map/all_to_all | solution.py:400
  12.4 3.4 %collective-permute-start.2 = (f32[4,4,128]{2,1,0:T(4,128)}, f32[4,4,128]{2,1,0:T(4,128)S(1)}, u32[]{:S(2)}, u32[]{:S(2)}) collective-permute-start(f32[4,4,128]{2,1,0:T(4,128)} %get-tuple-element.18.refs_0_), channel_id=1, source_target_pairs={{0,9},{1,8},{2,11},{3,10},{4,13},{5,12},{6,15},{7,14},{8,1},{9,0},... | collective-permute-start | bytes 24584 | tf_op jit(solution)/shard_map/ppermute | solution.py:378
  15.8 0.5 collective-permute-start.1
  16.3 1.1 shard_map.86
  17.5 3.2 %collective-permute-done.1.refs_2_ = f32[4,4,128]{2,1,0:T(4,128)S(1)} collective-permute-done((f32[4,4,128]{2,1,0:T(4,128)}, f32[4,4,128]{2,1,0:T(4,128)S(1)}, u32[]{:S(2)}, u32[]{:S(2)}) %collective-permute-start.1) | collective-permute-done | bytes 8224 | tf_op jit(solution)/shard_map/ppermute | solution.py:378
  20.7 2.2 %all-to-all-done.jones_ref = f32[16,4,8,128]{3,2,1,0:T(8,128)S(1)} async-done(((f32[16,4,8,128]{3,2,1,0:T(8,128)}), f32[16,4,8,128]{3,2,1,0:T(8,128)S(1)}, u32[]{:S(2)}, u32[]{:S(2)}) %all-to-all-start) | async-done | bytes 262176 | tf_op jit(solution)/shard_map/all_to_all | solution.py:400
  22.9 0.7 copy-done.1
  23.6 0.7 copy-done.2
  24.3 0.7 copy-done.4
  24.9 10.9 %shard_map.87 = (f32[16,4,8,128]{3,2,1,0:T(8,128)}, f32[4,4,128]{2,1,0:T(4,128)S(1)}) custom-call(s32[16]{0:T(128)S(1)} %copy-done.2, s32[16]{0:T(128)S(1)} %copy-done.4, f32[16,4,8,128]{3,2,1,0:T(8,128)S(1)} %all-to-all-done.jones_ref, bf16[16,8,32,256]{3,2,1,0:T(8,128)(2,1)} %bitcast.3, bf16[16,64,256]{2,1,0:T(8,128)(2,1)} %bitcast.5, ...), custom_call_target="tpu_custom_call" | custom-call | flops 40000000 | bytes 4000000 | tf_op jit(solution)/shard_map/pallas_call | solution.py:278
  35.9 4.9 %all-to-all-start.1 = ((f32[16,4,8,128]{3,2,1,0:T(8,128)}), f32[16,4,8,128]{3,2,1,0:T(8,128)S(1)}, u32[]{:S(2)}, u32[]{:S(2)}) async-start(f32[16,4,8,128]{3,2,1,0:T(8,128)} %get-tuple-element.19), calls=%async_computation.1 | async-start | bytes 524288 | tf_op jit(solution)/shard_map/all_to_all | solution.py:405
  40.8 2.8 %collective-permute-start.5 = (f32[4,4,128]{2,1,0:T(4,128)S(1)}, f32[4,4,128]{2,1,0:T(4,128)S(1)}, u32[]{:S(2)}, u32[]{:S(2)}) collective-permute-start(f32[4,4,128]{2,1,0:T(4,128)S(1)} %get-tuple-element.20.refs_3_), channel_id=1, source_target_pairs={{0,6},{1,7},{2,4},{3,5},{4,2},{5,3},{6,0},{7,1},{8,14},{9,15},{10,... | collective-permute-start | bytes 24584 | tf_op jit(solution)/shard_map/ppermute | solution.py:378
  44.3 0.4 collective-permute-done.5.refs_6_
  44.6 3.3 %collective-permute-done.4.refs_5_ = f32[4,4,128]{2,1,0:T(4,128)S(1)} collective-permute-done((f32[4,4,128]{2,1,0:T(4,128)S(1)}, f32[4,4,128]{2,1,0:T(4,128)S(1)}, u32[]{:S(2)}, u32[]{:S(2)}) %collective-permute-start.4) | collective-permute-done | bytes 8224 | tf_op jit(solution)/shard_map/ppermute | solution.py:378
  47.9 3.0 %all-to-all-done.1.refs_2_ = f32[16,4,8,128]{3,2,1,0:T(8,128)S(1)} async-done(((f32[16,4,8,128]{3,2,1,0:T(8,128)}), f32[16,4,8,128]{3,2,1,0:T(8,128)S(1)}, u32[]{:S(2)}, u32[]{:S(2)}) %all-to-all-start.1) | async-done | bytes 262176 | tf_op jit(solution)/shard_map/all_to_all | solution.py:405
  50.9 0.7 copy-done.6
  51.6 1.9 %shard_map.88 = (f32[16,4,8,128]{3,2,1,0:T(8,128)}, f32[4,4,128]{2,1,0:T(4,128)}) custom-call(s32[1]{0:T(128)} %bitcast.refs_0_, f32[16,4,8,128]{3,2,1,0:T(8,128)} %get-tuple-element.14.refs_1_, f32[16,4,8,128]{3,2,1,0:T(8,128)} %copy-done.6, f32[4,4,128]{2,1,0:T(4,128)} %copy-done, f32[4,4,128]{2,1,0:T(4,128)} %copy-done.9, f32[4,4,128]{2,1,0:T(4,128)} %copy-done.8, ...), custom_call_target="tpu_custom_call" | custom-call | tf_op jit(solution)/shard_map/pallas_call | solution.py:369
  53.5 14.4 %all_to_all.25.jones_ref = f32[16,4,8,128]{3,2,1,0:T(8,128)S(1)} all-to-all(f32[16,4,8,128]{3,2,1,0:T(8,128)} %get-tuple-element.21.refs_1_), channel_id=1, replica_groups=mesh['pair'=16,'chan'=16] {'pair'}, dimensions={0} | all-to-all | bytes 524288 | tf_op jit(solution)/shard_map/all_to_all | solution.py:409
  67.9 10.2 %shard_map.89 = f32[16,4,8,128]{3,2,1,0:T(8,128)S(1)} custom-call(s32[16]{0:T(128)S(1)} %copy-done.3, s32[16]{0:T(128)S(1)} %copy-done.5, f32[16,4,8,128]{3,2,1,0:T(8,128)S(1)} %all_to_all.25.jones_ref, bf16[16,8,32,256]{3,2,1,0:T(8,128)(2,1)} %bitcast.4, bf16[16,64,256]{2,1,0:T(8,128)(2,1)} %bitcast.6, f32[16,2,8,128]{3,2,1,0:T(8,128)S(1)} %get-tuple-element.15.keep_ref, ...), custom_call_target="tpu_custom_call" | custom-call | flops 40000000 | bytes 4000000 | tf_op jit(solution)/shard_map/pallas_call | solution.py:278
  78.1 13.0 %all_to_all.26.refs_1_ = f32[16,4,8,128]{3,2,1,0:T(8,128)} all-to-all(f32[16,4,8,128]{3,2,1,0:T(8,128)S(1)} %shard_map.89), channel_id=1, replica_groups=mesh['pair'=16,'chan'=16] {'pair'}, dimensions={0} | all-to-all | bytes 524288 | tf_op jit(solution)/shard_map/all_to_all | solution.py:411
  91.2 1.8 %shard_map.90 = (f32[4,8,128]{2,1,0:T(8,128)}, f32[16,4,8,128]{3,2,1,0:T(8,128)}) custom-call(s32[1]{0:T(128)} %bitcast.refs_0_, f32[16,4,8,128]{3,2,1,0:T(8,128)} %all_to_all.26.refs_1_, f32[4,4,128]{2,1,0:T(4,128)} %get-tuple-element.22.refs_2_), custom_call_target="tpu_custom_call" | custom-call | tf_op jit(solution)/shard_map/pallas_call | solution.py:369
  92.9 19.4 %all_to_all.27.refs_3_ = f32[16,4,8,128]{3,2,1,0:T(8,128)} all-to-all(f32[16,4,8,128]{3,2,1,0:T(8,128)} %get-tuple-element.24), channel_id=1, replica_groups=mesh['pair'=16,'chan'=16] {'chan'}, dimensions={0} | all-to-all | bytes 524288 | tf_op jit(solution)/shard_map/all_to_all | solution.py:419
  112.3 2.0 %shard_map.91 = (f32[8,4,8,16]{3,2,1,0:T(8,128)}, f32[8,4,8,16]{3,2,1,0:T(8,128)}, f32[8,4,4,16]{3,2,1,0:T(4,128)}) custom-call(s32[1]{0:T(128)} %bitcast.refs_0_, f32[16,4,8,128]{3,2,1,0:T(8,128)} %get-tuple-element.21.refs_1_, f32[4,8,128]{2,1,0:T(8,128)} %get-tuple-element.23.refs_2_, f32[16,4,8,128]{3,2,1,0:T(8,128)} %all_to_all.27.refs_3_), custom_call_target="tpu_custom_call" | custom-call | tf_op jit(solution)/shard_map/pallas_call | solution.py:369
  (22 shorter events, 0.7 us)
Async XLA Ops:
  2.4 20.6 %all-to-all-start = ((f32[16,4,8,128]{3,2,1,0:T(8,128)}), f32[16,4,8,128]{3,2,1,0:T(8,128)S(1)}, u32[]{:S(2)}, u32[]{:S(2)}) async-start(f32[16,4,8,128]{3,2,1,0:T(8,128)} %get-tuple-element.14.refs_1_), calls=%async_computation | async-start | bytes 524288 | tf_op jit(solution)/shard_map/all_to_all | solution.py:400
  12.4 5.0 %collective-permute-start.2 = (f32[4,4,128]{2,1,0:T(4,128)}, f32[4,4,128]{2,1,0:T(4,128)S(1)}, u32[]{:S(2)}, u32[]{:S(2)}) collective-permute-start(f32[4,4,128]{2,1,0:T(4,128)} %get-tuple-element.18.refs_0_), channel_id=1, source_target_pairs={{0,9},{1,8},{2,11},{3,10},{4,13},{5,12},{6,15},{7,14},{8,1},{9,0},... | collective-permute-start | bytes 24584 | tf_op jit(solution)/shard_map/ppermute | solution.py:378
  15.8 4.9 %collective-permute-start.1 = (f32[4,4,128]{2,1,0:T(4,128)}, f32[4,4,128]{2,1,0:T(4,128)S(1)}, u32[]{:S(2)}, u32[]{:S(2)}) collective-permute-start(f32[4,4,128]{2,1,0:T(4,128)} %get-tuple-element.18.refs_0_), channel_id=1, source_target_pairs={{0,8},{1,9},{2,10},{3,11},{4,12},{5,13},{6,14},{7,15},{8,0},{9,1},... | collective-permute-start | bytes 24584 | tf_op jit(solution)/shard_map/ppermute | solution.py:378
  16.3 4.4 %collective-permute-start = (f32[4,4,128]{2,1,0:T(4,128)}, f32[4,4,128]{2,1,0:T(4,128)S(1)}, u32[]{:S(2)}, u32[]{:S(2)}) collective-permute-start(f32[4,4,128]{2,1,0:T(4,128)} %get-tuple-element.18.refs_0_), channel_id=1, source_target_pairs={{0,1},{1,0},{2,3},{3,2},{4,5},{5,4},{6,7},{7,6},{8,9},{9,8},{10,11... | collective-permute-start | bytes 24584 | tf_op jit(solution)/shard_map/ppermute | solution.py:378
  22.9 0.7 copy-start.1
  23.6 0.7 copy-start.2
  24.3 0.7 copy-start.4
  24.9 43.0 %copy-start.3 = (s32[16]{0:T(128)S(1)}, s32[16]{0:T(128)}, u32[]{:S(2)}) copy-start(s32[16]{0:T(128)} %rows_ref.5) | copy-start | bytes 196
  24.9 43.0 %copy-start.5 = (s32[16]{0:T(128)S(1)}, s32[16]{0:T(128)}, u32[]{:S(2)}) copy-start(s32[16]{0:T(128)} %cols_ref.5) | copy-start | bytes 196
  35.9 15.0 %copy-start = (f32[4,4,128]{2,1,0:T(4,128)}, f32[4,4,128]{2,1,0:T(4,128)S(1)}, u32[]{:S(2)}) copy-start(f32[4,4,128]{2,1,0:T(4,128)S(1)} %get-tuple-element.20.refs_3_) | copy-start | bytes 24580
  35.9 15.0 %all-to-all-start.1 = ((f32[16,4,8,128]{3,2,1,0:T(8,128)}), f32[16,4,8,128]{3,2,1,0:T(8,128)S(1)}, u32[]{:S(2)}, u32[]{:S(2)}) async-start(f32[16,4,8,128]{3,2,1,0:T(8,128)} %get-tuple-element.19), calls=%async_computation.1 | async-start | bytes 524288 | tf_op jit(solution)/shard_map/all_to_all | solution.py:405
  40.8 3.9 %collective-permute-start.5 = (f32[4,4,128]{2,1,0:T(4,128)S(1)}, f32[4,4,128]{2,1,0:T(4,128)S(1)}, u32[]{:S(2)}, u32[]{:S(2)}) collective-permute-start(f32[4,4,128]{2,1,0:T(4,128)S(1)} %get-tuple-element.20.refs_3_), channel_id=1, source_target_pairs={{0,6},{1,7},{2,4},{3,5},{4,2},{5,3},{6,0},{7,1},{8,14},{9,15},{10,... | collective-permute-start | bytes 24584 | tf_op jit(solution)/shard_map/ppermute | solution.py:378
  43.6 4.3 %collective-permute-start.4 = (f32[4,4,128]{2,1,0:T(4,128)S(1)}, f32[4,4,128]{2,1,0:T(4,128)S(1)}, u32[]{:S(2)}, u32[]{:S(2)}) collective-permute-start(f32[4,4,128]{2,1,0:T(4,128)S(1)} %get-tuple-element.20.refs_3_), channel_id=1, source_target_pairs={{0,4},{1,5},{2,6},{3,7},{4,0},{5,1},{6,2},{7,3},{8,12},{9,13},{10,... | collective-permute-start | bytes 24584 | tf_op jit(solution)/shard_map/ppermute | solution.py:378
  43.9 4.0 %collective-permute-start.3 = (f32[4,4,128]{2,1,0:T(4,128)S(1)}, f32[4,4,128]{2,1,0:T(4,128)S(1)}, u32[]{:S(2)}, u32[]{:S(2)}) collective-permute-start(f32[4,4,128]{2,1,0:T(4,128)S(1)} %get-tuple-element.20.refs_3_), channel_id=1, source_target_pairs={{0,2},{1,3},{2,0},{3,1},{4,6},{5,7},{6,4},{7,5},{8,10},{9,11},{10,... | collective-permute-start | bytes 24584 | tf_op jit(solution)/shard_map/ppermute | solution.py:378
  44.6 6.3 %copy-start.7 = (f32[4,4,128]{2,1,0:T(4,128)}, f32[4,4,128]{2,1,0:T(4,128)S(1)}, u32[]{:S(2)}) copy-start(f32[4,4,128]{2,1,0:T(4,128)S(1)} %collective-permute-done.5.refs_6_) | copy-start | bytes 24580
  47.9 3.0 %copy-start.8 = (f32[4,4,128]{2,1,0:T(4,128)}, f32[4,4,128]{2,1,0:T(4,128)S(1)}, u32[]{:S(2)}) copy-start(f32[4,4,128]{2,1,0:T(4,128)S(1)} %collective-permute-done.4.refs_5_) | copy-start | bytes 24580
  47.9 3.0 %copy-start.9 = (f32[4,4,128]{2,1,0:T(4,128)}, f32[4,4,128]{2,1,0:T(4,128)S(1)}, u32[]{:S(2)}) copy-start(f32[4,4,128]{2,1,0:T(4,128)S(1)} %collective-permute-done.3.refs_4_) | copy-start | bytes 24580
  50.9 0.7 copy-start.6

commit v3 on v2

--- a/solution.py
+++ b/solution.py
@@ -16,6 +16,11 @@
 CHANS = 8
 DIRS = 4
 VMEM_LIMIT = 32 * 1024 * 1024
+SMALL_LIMIT = 8 * 1024 * 1024
+
+
+def in_hbm(array):
+    return pltpu.with_memory_space_constraint(array, pltpu.HBM)
 
 
 def lane_iota():
@@ -140,8 +145,9 @@
         ],
         in_specs=[smem, smem, vmem],
         out_specs=[vmem] * 3,
+        compiler_params=pltpu.CompilerParams(vmem_limit_bytes=SMALL_LIMIT),
         cost_estimate=pl.CostEstimate(flops=1_000_000, bytes_accessed=2_000_000, transcendentals=0),
-    )(rows, cols, marker)
+    )(in_hbm(rows), in_hbm(cols), in_hbm(marker))
 
 
 def descent_kernel(
@@ -270,7 +276,6 @@
     vmem = pl.BlockSpec(memory_space=pltpu.VMEM)
     smem = pl.BlockSpec(memory_space=pltpu.SMEM)
     hbm = pl.BlockSpec(memory_space=pltpu.HBM)
-    tiles = [pltpu.with_memory_space_constraint(x, pltpu.HBM) for x in (coher, seen)]
     staged = [pltpu.with_memory_space_constraint(x, pltpu.VMEM) for x in staged]
     out_shape = [jax.ShapeDtypeStruct((blocks, DIRS, CHANS, LANES), jnp.float32)]
     if len(parts) > 0:
@@ -295,7 +300,7 @@
         cost_estimate=pl.CostEstimate(
             flops=40_000_000, bytes_accessed=4_000_000, transcendentals=0
         ),
-    )(rows, cols, jones_full, *tiles, *staged, *parts)
+    )(in_hbm(rows), in_hbm(cols), jones_full, in_hbm(coher), in_hbm(seen), *staged, *parts)
 
 
 def to_dense_kernel(total, chan_ref, start_ref, sent_ref, part_ref):
@@ -371,7 +376,8 @@
         out_shape=[jax.ShapeDtypeStruct(s, jnp.float32) for s in shapes],
         in_specs=[smem] + [vmem] * len(arrays),
         out_specs=[vmem] * len(shapes),
-    )(chan, *arrays)
+        compiler_params=pltpu.CompilerParams(vmem_limit_bytes=SMALL_LIMIT),
+    )(in_hbm(chan), *arrays)
 
 
 def flipped(array, bits, count):

time: 115 us -> 107 us (0.930)
  Pallas kernels: 29.6 us -> 25.4 us
  local copies, waits for them, and re-layouts: 2.73 us -> 0.9 us
  blocking collectives: 46.8 us -> 45.4 us
    pallas_call x4, Pallas kernels: 7.32 us -> 2.87 us  [small_call(): pl.pallas_call(body, out_shape=[jax.ShapeDtypeStruct(s, jnp.float32) for...]
    unnamed x20 -> x2, local copies, waits for them, and re-layouts: 2.73 us -> 0.9 us
  transfers between devices with their start and end apart: 8 -> 8, of which waited for: 5 -> 6; matrix products, arithmetic and copies ran while one was open for 0% -> 0% of each run, Pallas kernels for 1% -> 1%
where the time goes in v3:
time: 107 us; the launch traced here: 106 us
  blocking collectives  45.4 us (42%)
  Pallas kernels  25.4 us (24%)
  starting transfers between devices  22.2 us (21%)
  waiting for transfers between devices  12 us (11%)
    pallas_call x2, Pallas kernels, local_descent(): pl.pallas_call(descent_kernel, out_shape=out_shape, in_specs=[smem, smem,...  21.4 us
    all_to_all x1, blocking collectives, local(): sums = lax.all_to_all(sums, 'chan', 0, 0)  19.4 us
    all_to_all x1, blocking collectives, local(): full = lax.all_to_all(sent, 'pair', 0, 0)  13.8 us
    all_to_all x1, blocking collectives, local(): terms = lax.all_to_all(terms, 'pair', 0, 0)  12.2 us
    all_to_all x1, starting transfers between devices, local(): full = lax.all_to_all(sent, 'pair', 0, 0)  10 us
    ppermute x6, starting transfers between devices, flipped(): return lax.ppermute(array, 'chan', [(i, i ^ bits) for i in range(count)])  7.4 us
    ppermute x6, waiting for transfers between devices, flipped(): return lax.ppermute(array, 'chan', [(i, i ^ bits) for i in range(count)])  6.35 us
    all_to_all x1, starting transfers between devices, local(): terms = lax.all_to_all(terms, 'pair', 0, 0)  4.71 us
  transfers between devices with their start and end apart: 8, of which 6 were waited for; matrix products, arithmetic and copies ran while one was open for 0% of the time, Pallas kernels for 1%

profile of v3, /device:TPU:1, one launch (start us, length us, event | category | flops | bytes accessed | tf_op | source)
XLA Modules:
  0.0 106.5 jit_solution(4735837573823980109)
XLA Ops:
  0.6 0.9 copy-done
  1.5 0.8 shard_map.85
  2.4 10.0 %all-to-all-start = ((f32[16,4,8,128]{3,2,1,0:T(8,128)}), f32[16,4,8,128]{3,2,1,0:T(8,128)S(1)}, u32[]{:S(2)}, u32[]{:S(2)}) async-start(f32[16,4,8,128]{3,2,1,0:T(8,128)} %get-tuple-element.14.refs_1_), calls=%async_computation | async-start | bytes 524288 | tf_op jit(solution)/shard_map/all_to_all | solution.py:406
  12.4 3.4 %collective-permute-start.2 = (f32[4,4,128]{2,1,0:T(4,128)S(1)}, f32[4,4,128]{2,1,0:T(4,128)S(1)}, u32[]{:S(2)}, u32[]{:S(2)}) collective-permute-start(f32[4,4,128]{2,1,0:T(4,128)S(1)} %get-tuple-element.18.refs_0_), channel_id=1, source_target_pairs={{0,9},{1,8},{2,11},{3,10},{4,13},{5,12},{6,15},{7,14},{8,1},{9,0},... | collective-permute-start | bytes 24584 | tf_op jit(solution)/shard_map/ppermute | solution.py:384
  15.8 0.5 collective-permute-start.1
  16.3 1.1 %shard_map.86 = (f32[16,2,8,128]{3,2,1,0:T(8,128)S(1)}, bf16[256,3072]{1,0:T(8,128)(2,1)S(1)}, bf16[2,512,128]{2,1,0:T(8,128)(2,1)S(1)}) custom-call(s32[16]{0:T(128)} %rows_ref.5, s32[16]{0:T(128)} %cols_ref.5, s32[16,256]{1,0:T(8,128)} %marker_ref.1), custom_call_target="tpu_custom_call" | custom-call | flops 1000000 | bytes 2000000 | tf_op jit(solution)/shard_map/pallas_call | solution.py:139
  17.4 0.3 collective-permute-done.2.refs_3_
  17.7 2.4 %collective-permute-done.1.refs_2_ = f32[4,4,128]{2,1,0:T(4,128)S(1)} collective-permute-done((f32[4,4,128]{2,1,0:T(4,128)S(1)}, f32[4,4,128]{2,1,0:T(4,128)S(1)}, u32[]{:S(2)}, u32[]{:S(2)}) %collective-permute-start.1) | collective-permute-done | bytes 8224 | tf_op jit(solution)/shard_map/ppermute | solution.py:384
  20.2 2.7 %all-to-all-done.jones_ref = f32[16,4,8,128]{3,2,1,0:T(8,128)S(1)} async-done(((f32[16,4,8,128]{3,2,1,0:T(8,128)}), f32[16,4,8,128]{3,2,1,0:T(8,128)S(1)}, u32[]{:S(2)}, u32[]{:S(2)}) %all-to-all-start) | async-done | bytes 262176 | tf_op jit(solution)/shard_map/all_to_all | solution.py:406
  22.9 11.0 %shard_map.87 = (f32[16,4,8,128]{3,2,1,0:T(8,128)}, f32[4,4,128]{2,1,0:T(4,128)S(1)}) custom-call(s32[16]{0:T(128)} %rows_ref.5, s32[16]{0:T(128)} %cols_ref.5, f32[16,4,8,128]{3,2,1,0:T(8,128)S(1)} %all-to-all-done.jones_ref, bf16[16,8,32,256]{3,2,1,0:T(8,128)(2,1)} %bitcast.3, bf16[16,64,256]{2,1,0:T(8,128)(2,1)} %bitcast.5, ...), custom_call_target="tpu_custom_call" | custom-call | flops 40000000 | bytes 4000000 | tf_op jit(solution)/shard_map/pallas_call | solution.py:283
  33.9 4.7 %all-to-all-start.1 = ((f32[16,4,8,128]{3,2,1,0:T(8,128)}), f32[16,4,8,128]{3,2,1,0:T(8,128)S(1)}, u32[]{:S(2)}, u32[]{:S(2)}) async-start(f32[16,4,8,128]{3,2,1,0:T(8,128)} %get-tuple-element.19), calls=%async_computation.1 | async-start | bytes 524288 | tf_op jit(solution)/shard_map/all_to_all | solution.py:411
  38.7 2.8 %collective-permute-start.5 = (f32[4,4,128]{2,1,0:T(4,128)S(1)}, f32[4,4,128]{2,1,0:T(4,128)S(1)}, u32[]{:S(2)}, u32[]{:S(2)}) collective-permute-start(f32[4,4,128]{2,1,0:T(4,128)S(1)} %get-tuple-element.20.refs_3_), channel_id=1, source_target_pairs={{0,6},{1,7},{2,4},{3,5},{4,2},{5,3},{6,0},{7,1},{8,14},{9,15},{10,... | collective-permute-start | bytes 24584 | tf_op jit(solution)/shard_map/ppermute | solution.py:384
  41.5 0.3 collective-permute-start.4
  41.8 0.3 collective-permute-start.3
  42.2 0.4 collective-permute-done.5.refs_6_
  42.5 3.3 %collective-permute-done.4.refs_5_ = f32[4,4,128]{2,1,0:T(4,128)S(1)} collective-permute-done((f32[4,4,128]{2,1,0:T(4,128)S(1)}, f32[4,4,128]{2,1,0:T(4,128)S(1)}, u32[]{:S(2)}, u32[]{:S(2)}) %collective-permute-start.4) | collective-permute-done | bytes 8224 | tf_op jit(solution)/shard_map/ppermute | solution.py:384
  45.8 2.9 %all-to-all-done.1.refs_2_ = f32[16,4,8,128]{3,2,1,0:T(8,128)S(1)} async-done(((f32[16,4,8,128]{3,2,1,0:T(8,128)}), f32[16,4,8,128]{3,2,1,0:T(8,128)S(1)}, u32[]{:S(2)}, u32[]{:S(2)}) %all-to-all-start.1) | async-done | bytes 262176 | tf_op jit(solution)/shard_map/all_to_all | solution.py:411
  48.7 1.0 shard_map.88
  49.7 13.8 %all_to_all.25.jones_ref = f32[16,4,8,128]{3,2,1,0:T(8,128)S(1)} all-to-all(f32[16,4,8,128]{3,2,1,0:T(8,128)S(1)} %get-tuple-element.21.refs_1_), channel_id=1, replica_groups=mesh['pair'=16,'chan'=16] {'pair'}, dimensions={0} | all-to-all | bytes 524288 | tf_op jit(solution)/shard_map/all_to_all | solution.py:415
  63.5 10.3 %shard_map.89 = f32[16,4,8,128]{3,2,1,0:T(8,128)S(1)} custom-call(s32[16]{0:T(128)} %rows_ref.5, s32[16]{0:T(128)} %cols_ref.5, f32[16,4,8,128]{3,2,1,0:T(8,128)S(1)} %all_to_all.25.jones_ref, bf16[16,8,32,256]{3,2,1,0:T(8,128)(2,1)} %bitcast.4, bf16[16,64,256]{2,1,0:T(8,128)(2,1)} %bitcast.6, f32[16,2,8,128]{3,2,1,0:T(8,128)S(1)} %get-tuple-element.15.keep_ref, ...), custom_call_target="tpu_custom_call" | custom-call | flops 40000000 | bytes 4000000 | tf_op jit(solution)/shard_map/pallas_call | solution.py:283
  73.9 12.2 %all_to_all.26.refs_1_ = f32[16,4,8,128]{3,2,1,0:T(8,128)S(1)} all-to-all(f32[16,4,8,128]{3,2,1,0:T(8,128)S(1)} %shard_map.89), channel_id=1, replica_groups=mesh['pair'=16,'chan'=16] {'pair'}, dimensions={0} | all-to-all | bytes 524288 | tf_op jit(solution)/shard_map/all_to_all | solution.py:417
  86.1 0.1 shard_map.90
  86.2 19.4 %all_to_all.27.refs_3_ = f32[16,4,8,128]{3,2,1,0:T(8,128)S(1)} all-to-all(f32[16,4,8,128]{3,2,1,0:T(8,128)S(1)} %get-tuple-element.24), channel_id=1, replica_groups=mesh['pair'=16,'chan'=16] {'chan'}, dimensions={0} | all-to-all | bytes 524288 | tf_op jit(solution)/shard_map/all_to_all | solution.py:425
  105.6 0.9 shard_map.91
  (4 shorter events, 0.0 us)
Async XLA Ops:
  0.6 0.9 copy-start
  2.4 20.6 %all-to-all-start = ((f32[16,4,8,128]{3,2,1,0:T(8,128)}), f32[16,4,8,128]{3,2,1,0:T(8,128)S(1)}, u32[]{:S(2)}, u32[]{:S(2)}) async-start(f32[16,4,8,128]{3,2,1,0:T(8,128)} %get-tuple-element.14.refs_1_), calls=%async_computation | async-start | bytes 524288 | tf_op jit(solution)/shard_map/all_to_all | solution.py:406
  12.4 5.3 %collective-permute-start.2 = (f32[4,4,128]{2,1,0:T(4,128)S(1)}, f32[4,4,128]{2,1,0:T(4,128)S(1)}, u32[]{:S(2)}, u32[]{:S(2)}) collective-permute-start(f32[4,4,128]{2,1,0:T(4,128)S(1)} %get-tuple-element.18.refs_0_), channel_id=1, source_target_pairs={{0,9},{1,8},{2,11},{3,10},{4,13},{5,12},{6,15},{7,14},{8,1},{9,0},... | collective-permute-start | bytes 24584 | tf_op jit(solution)/shard_map/ppermute | solution.py:384
  15.8 4.4 %collective-permute-start.1 = (f32[4,4,128]{2,1,0:T(4,128)S(1)}, f32[4,4,128]{2,1,0:T(4,128)S(1)}, u32[]{:S(2)}, u32[]{:S(2)}) collective-permute-start(f32[4,4,128]{2,1,0:T(4,128)S(1)} %get-tuple-element.18.refs_0_), channel_id=1, source_target_pairs={{0,8},{1,9},{2,10},{3,11},{4,12},{5,13},{6,14},{7,15},{8,0},{9,1},... | collective-permute-start | bytes 24584 | tf_op jit(solution)/shard_map/ppermute | solution.py:384
  16.3 3.9 %collective-permute-start = (f32[4,4,128]{2,1,0:T(4,128)S(1)}, f32[4,4,128]{2,1,0:T(4,128)S(1)}, u32[]{:S(2)}, u32[]{:S(2)}) collective-permute-start(f32[4,4,128]{2,1,0:T(4,128)S(1)} %get-tuple-element.18.refs_0_), channel_id=1, source_target_pairs={{0,1},{1,0},{2,3},{3,2},{4,5},{5,4},{6,7},{7,6},{8,9},{9,8},{10,11... | collective-permute-start | bytes 24584 | tf_op jit(solution)/shard_map/ppermute | solution.py:384
  33.9 14.7 %all-to-all-start.1 = ((f32[16,4,8,128]{3,2,1,0:T(8,128)}), f32[16,4,8,128]{3,2,1,0:T(8,128)S(1)}, u32[]{:S(2)}, u32[]{:S(2)}) async-start(f32[16,4,8,128]{3,2,1,0:T(8,128)} %get-tuple-element.19), calls=%async_computation.1 | async-start | bytes 524288 | tf_op jit(solution)/shard_map/all_to_all | solution.py:411
  38.7 3.9 %collective-permute-start.5 = (f32[4,4,128]{2,1,0:T(4,128)S(1)}, f32[4,4,128]{2,1,0:T(4,128)S(1)}, u32[]{:S(2)}, u32[]{:S(2)}) collective-permute-start(f32[4,4,128]{2,1,0:T(4,128)S(1)} %get-tuple-element.20.refs_3_), channel_id=1, source_target_pairs={{0,6},{1,7},{2,4},{3,5},{4,2},{5,3},{6,0},{7,1},{8,14},{9,15},{10,... | collective-permute-start | bytes 24584 | tf_op jit(solution)/shard_map/ppermute | solution.py:384
  41.5 4.3 %collective-permute-start.4 = (f32[4,4,128]{2,1,0:T(4,128)S(1)}, f32[4,4,128]{2,1,0:T(4,128)S(1)}, u32[]{:S(2)}, u32[]{:S(2)}) collective-permute-start(f32[4,4,128]{2,1,0:T(4,128)S(1)} %get-tuple-element.20.refs_3_), channel_id=1, source_target_pairs={{0,4},{1,5},{2,6},{3,7},{4,0},{5,1},{6,2},{7,3},{8,12},{9,13},{10,... | collective-permute-start | bytes 24584 | tf_op jit(solution)/shard_map/ppermute | solution.py:384
  41.8 4.0 %collective-permute-start.3 = (f32[4,4,128]{2,1,0:T(4,128)S(1)}, f32[4,4,128]{2,1,0:T(4,128)S(1)}, u32[]{:S(2)}, u32[]{:S(2)}) collective-permute-start(f32[4,4,128]{2,1,0:T(4,128)S(1)} %get-tuple-element.20.refs_3_), channel_id=1, source_target_pairs={{0,2},{1,3},{2,0},{3,1},{4,6},{5,7},{6,4},{7,5},{8,10},{9,11},{10,... | collective-permute-start | bytes 24584 | tf_op jit(solution)/shard_map/ppermute | solution.py:384

commit v4 on v3

--- a/solution.py
+++ b/solution.py
@@ -109,7 +109,10 @@
     return jnp.where(hit, 1.0, 0.0).astype(jnp.bfloat16)
 
 
-def stage_kernel(rows_ref, cols_ref, marker_ref, keep_ref, spread_ref, sums_ref):
+def stage_kernel(rows_ref, cols_ref, marker_ref, *refs):
+    part_refs, (keep_ref, spread_ref, sums_ref, total_ref) = refs[:-4], refs[-4:]
+    parts = [ref[n] for ref in part_refs for n in range(ref.shape[0])]
+    total_ref[...] = sum(parts[1:], parts[0])
     source = lax.broadcasted_iota(jnp.int32, (LANES, LANES), 0)
     target = lax.broadcasted_iota(jnp.int32, (LANES, LANES), 1)
     tables = [target % BLK, target // BLK, target // BLK + 8]
@@ -132,7 +135,7 @@
             keep_ref[t, half] = keep
 
 
-def stage(marker, rows, cols):
+def stage(marker, rows, cols, parts):
     slots = rows.shape[0]
     vmem = pl.BlockSpec(memory_space=pltpu.VMEM)
     smem = pl.BlockSpec(memory_space=pltpu.SMEM)
@@ -142,24 +145,35 @@
             pltpu.VMEM((slots, 2, CHANS, LANES), jnp.float32),
             pltpu.VMEM((2 * LANES, 24 * LANES), jnp.bfloat16),
             pltpu.VMEM((2, 4 * LANES, LANES), jnp.bfloat16),
+            jax.ShapeDtypeStruct(parts[0].shape[1:], jnp.float32),
         ],
-        in_specs=[smem, smem, vmem],
-        out_specs=[vmem] * 3,
+        in_specs=[smem, smem, vmem] + [vmem] * len(parts),
+        out_specs=[vmem] * 4,
         compiler_params=pltpu.CompilerParams(vmem_limit_bytes=SMALL_LIMIT),
         cost_estimate=pl.CostEstimate(flops=1_000_000, bytes_accessed=2_000_000, transcendentals=0),
-    )(in_hbm(rows), in_hbm(cols), in_hbm(marker))
+    )(in_hbm(rows), in_hbm(cols), in_hbm(marker), *parts)
 
 
 def descent_kernel(
-    rows_ref, cols_ref, jones_ref, coher_hbm, seen_hbm, keep_ref, spread_ref, sums_ref, *refs
+    rows_ref,
+    cols_ref,
+    jones_ref,
+    coher_hbm,
+    seen_hbm,
+    keep_ref,
+    spread_ref,
+    sums_ref,
+    out_ref,
+    coher_ref,
+    seen_ref,
+    wide_ref,
+    left_ref,
+    res_ref,
+    row_ref,
+    col_ref,
+    coher_sem,
+    seen_sem,
 ):
-    outer, scratch = refs[:-9], refs[-9:]
-    if len(outer) > 1:
-        part_refs, (out_ref, sum_ref) = outer[:-2], outer[-2:]
-        sum_ref[...] = sum([ref[...] for ref in part_refs[1:]], part_refs[0][...])
-    else:
-        (out_ref,) = outer
-    coher_ref, seen_ref, wide_ref, left_ref, res_ref, row_ref, col_ref, coher_sem, seen_sem = scratch
     slots = rows_ref.shape[0]
     blocks = jones_ref.shape[0]
 
@@ -270,21 +284,18 @@
     lax.fori_loop(0, slots // group, settle, 0)
 
 
-def local_descent(jones_full, rows, cols, coher, seen, staged, parts):
+def local_descent(jones_full, rows, cols, coher, seen, staged):
     blocks = jones_full.shape[0]
     slots = rows.shape[0]
     vmem = pl.BlockSpec(memory_space=pltpu.VMEM)
     smem = pl.BlockSpec(memory_space=pltpu.SMEM)
     hbm = pl.BlockSpec(memory_space=pltpu.HBM)
     staged = [pltpu.with_memory_space_constraint(x, pltpu.VMEM) for x in staged]
-    out_shape = [jax.ShapeDtypeStruct((blocks, DIRS, CHANS, LANES), jnp.float32)]
-    if len(parts) > 0:
-        out_shape.append(jax.ShapeDtypeStruct(parts[0].shape, jnp.float32))
     return pl.pallas_call(
         descent_kernel,
-        out_shape=out_shape,
-        in_specs=[smem, smem, vmem, hbm, hbm] + [vmem] * (3 + len(parts)),
-        out_specs=[vmem] * len(out_shape),
+        out_shape=jax.ShapeDtypeStruct((blocks, DIRS, CHANS, LANES), jnp.float32),
+        in_specs=[smem, smem, vmem, hbm, hbm] + [vmem] * 3,
+        out_specs=vmem,
         scratch_shapes=[
             pltpu.VMEM(coher.shape, jnp.bfloat16),
             pltpu.VMEM(seen.shape, jnp.bfloat16),
@@ -300,13 +311,14 @@
         cost_estimate=pl.CostEstimate(
             flops=40_000_000, bytes_accessed=4_000_000, transcendentals=0
         ),
-    )(in_hbm(rows), in_hbm(cols), jones_full, in_hbm(coher), in_hbm(seen), *staged, *parts)
-
-
-def to_dense_kernel(total, chan_ref, start_ref, sent_ref, part_ref):
+    )(in_hbm(rows), in_hbm(cols), jones_full, in_hbm(coher), in_hbm(seen), *staged)
+
+
+def to_dense_kernel(total, chan_ref, start_ref, dense_ref, sent_ref, part_ref):
     basis = basis_rows(chan_ref[0], total)
     for k in range(DIRS):
         field = jnp.concatenate([start_ref[e, k] for e in range(8)], axis=1)
+        dense_ref[k] = field
         for n in range(sent_ref.shape[0]):
             sent_ref[n, k] = field
         part_ref[k] = jnp.concatenate(project_rows(field, basis), axis=0)
@@ -320,16 +332,17 @@
 
 
 def first_update_kernel(total, chan_ref, jones_ref, terms_ref, *refs):
-    coeff_refs, (sent_ref, part_ref) = refs[:-2], refs[-2:]
+    coeff_refs, (dense_ref, sent_ref, part_ref) = refs[:-3], refs[-3:]
     basis = basis_rows(chan_ref[0], total)
     for k in range(DIRS):
         coeffs = coeff_refs[0][k]
         for ref in coeff_refs[1:]:
             coeffs = coeffs + ref[k]
-        now = jones_ref[0, k]
+        now = jones_ref[k]
         now = now + MU * (
             descent_sum(terms_ref, k) / STATIONS - RHO * (now - expand_rows(coeffs, basis))
         )
+        dense_ref[k] = now
         for n in range(sent_ref.shape[0]):
             sent_ref[n, k] = now
         part_ref[k] = jnp.concatenate(project_rows(now, basis), axis=0)
@@ -352,7 +365,7 @@
     for k in range(DIRS):
         both = descent_sum(sums_ref, k)
         coeffs = both[0:NP]
-        now = jones_ref[0, k]
+        now = jones_ref[k]
         dual = RHO * (now - expand_rows(coeffs, basis))
         now = now + MU * (descent_ref[k] / STATIONS - dual - dual)
         coeffs = coeffs + (MU / STATIONS) * both[NP : 2 * NP]
@@ -398,22 +411,22 @@
     chan = lax.axis_index("chan").astype(jnp.int32).reshape(1)
     coher = coher.reshape(coher.shape[0], 8, DIRS * CHANS, BLK * BLK)
     seen = seen.reshape(seen.shape[0], 8 * CHANS, BLK * BLK)
-    staged = stage(marker, rows, cols)
     block = (DIRS, CHANS, LANES)
     blocks = (pair_count,) + block
     poly = (DIRS, NP, LANES)
-    sent, part = small_call(to_dense_kernel, total, chan, [start], [blocks, poly])
+    jones, sent, part = small_call(to_dense_kernel, total, chan, [start], [block, blocks, poly])
     full = lax.all_to_all(sent, "pair", 0, 0)
     bits = [1 << i for i in range(chan_count.bit_length() - 1)]
-    parts = exchanged(part, bits[:1] + bits[3:], chan_count)
-    terms, part = local_descent(full, rows, cols, coher, seen, staged, parts)
+    parts = exchanged(part[None], bits[:1] + bits[3:], chan_count)
+    *staged, part = stage(marker, rows, cols, parts)
+    terms = local_descent(full, rows, cols, coher, seen, staged)
     coeff_parts = exchanged(part, bits[1:3], chan_count)
     terms = lax.all_to_all(terms, "pair", 0, 0)
-    sent, part = small_call(
-        first_update_kernel, total, chan, [sent, terms] + coeff_parts, [blocks, poly]
+    jones, sent, part = small_call(
+        first_update_kernel, total, chan, [jones, terms] + coeff_parts, [block, blocks, poly]
     )
     full = lax.all_to_all(sent, "pair", 0, 0)
-    (terms,) = local_descent(full, rows, cols, coher, seen, staged, [])
+    terms = local_descent(full, rows, cols, coher, seen, staged)
     terms = lax.all_to_all(terms, "pair", 0, 0)
     descent, sums = small_call(
         second_sum_kernel,
@@ -427,7 +440,7 @@
         finish_kernel,
         total,
         chan,
-        [sent, descent, sums],
+        [jones, descent, sums],
         [(8, DIRS, CHANS, BLK), (8, DIRS, CHANS, BLK), (8, DIRS, NP, BLK)],
     )
 

time: 107 us -> 106 us (level)
  blocking collectives: 45.4 us -> 43.5 us
  starting transfers between devices: 22.2 us -> 23.3 us
    all_to_all x1, starting transfers between devices: 4.71 us -> 5.86 us  [local(): terms = lax.all_to_all(terms, 'pair', 0, 0)]
    all_to_all x1, waiting for transfers between devices: 2.73 us -> 1.59 us  [local(): full = lax.all_to_all(sent, 'pair', 0, 0)]
    all_to_all x1, blocking collectives: 19.4 us -> 18.3 us  [local(): sums = lax.all_to_all(sums, 'chan', 0, 0)]
where the time goes in v4:
time: 106 us
  blocking collectives  43.5 us (41%)
  Pallas kernels  24.5 us (23%)
  starting transfers between devices  23.3 us (22%)
  waiting for transfers between devices  12.9 us (12%)
    pallas_call x2, Pallas kernels, local_descent(): pl.pallas_call(descent_kernel, out_shape=jax.ShapeDtypeStruct((blocks, DI...  21.4 us
    all_to_all x1, blocking collectives, local(): sums = lax.all_to_all(sums, 'chan', 0, 0)  18.3 us
    all_to_all x1, blocking collectives, local(): full = lax.all_to_all(sent, 'pair', 0, 0)  12.9 us
    all_to_all x1, blocking collectives, local(): terms = lax.all_to_all(terms, 'pair', 0, 0)  12.3 us
    all_to_all x1, starting transfers between devices, local(): full = lax.all_to_all(sent, 'pair', 0, 0)  10 us
    ppermute x6, starting transfers between devices, flipped(): return lax.ppermute(array, 'chan', [(i, i ^ bits) for i in range(count)])  7.4 us
    ppermute x6, waiting for transfers between devices, flipped(): return lax.ppermute(array, 'chan', [(i, i ^ bits) for i in range(count)])  7.35 us
    all_to_all x1, starting transfers between devices, local(): terms = lax.all_to_all(terms, 'pair', 0, 0)  5.86 us
  transfers between devices with their start and end apart: 8, of which 6 were waited for; matrix products, arithmetic and copies ran while one was open for 0% of the time, Pallas kernels for 1%

profile of v4, /device:TPU:1, one launch (start us, length us, event | category | flops | bytes accessed | tf_op | source)
XLA Modules:
  0.0 105.7 jit_solution(1415818786686935556)
XLA Ops:
  0.6 0.9 copy-done
  1.5 0.8 shard_map.85
  2.4 10.0 %all-to-all-start = ((f32[16,4,8,128]{3,2,1,0:T(8,128)}), f32[16,4,8,128]{3,2,1,0:T(8,128)S(1)}, u32[]{:S(2)}, u32[]{:S(2)}) async-start(f32[16,4,8,128]{3,2,1,0:T(8,128)} %get-tuple-element.16), calls=%async_computation | async-start | bytes 524288 | tf_op jit(solution)/shard_map/all_to_all | solution.py:418
  12.4 3.4 %collective-permute-start.2 = (f32[1,4,4,128]{3,2,1,0:T(4,128)S(1)}, f32[1,4,4,128]{3,2,1,0:T(4,128)S(1)}, u32[]{:S(2)}, u32[]{:S(2)}) collective-permute-start(f32[1,4,4,128]{3,2,1,0:T(4,128)S(1)} %bitcast.4), channel_id=1, source_target_pairs={{0,9},{1,8},{2,11},{3,10},{4,13},{5,12},{6,15},{7,14},{8,1},{9,0},... | collective-permute-start | bytes 24584 | tf_op jit(solution)/shard_map/ppermute | solution.py:397
  15.8 0.5 collective-permute-start.1
  16.3 1.4 %collective-permute-done.2.refs_3_ = f32[1,4,4,128]{3,2,1,0:T(4,128)S(1)} collective-permute-done((f32[1,4,4,128]{3,2,1,0:T(4,128)S(1)}, f32[1,4,4,128]{3,2,1,0:T(4,128)S(1)}, u32[]{:S(2)}, u32[]{:S(2)}) %collective-permute-start.2) | collective-permute-done | bytes 8224 | tf_op jit(solution)/shard_map/ppermute | solution.py:397
  17.7 2.4 %collective-permute-done.1.refs_2_ = f32[1,4,4,128]{3,2,1,0:T(4,128)S(1)} collective-permute-done((f32[1,4,4,128]{3,2,1,0:T(4,128)S(1)}, f32[1,4,4,128]{3,2,1,0:T(4,128)S(1)}, u32[]{:S(2)}, u32[]{:S(2)}) %collective-permute-start.1) | collective-permute-done | bytes 8224 | tf_op jit(solution)/shard_map/ppermute | solution.py:397
  20.2 1.1 %shard_map.86 = (f32[16,2,8,128]{3,2,1,0:T(8,128)S(1)}, bf16[256,3072]{1,0:T(8,128)(2,1)S(1)}, bf16[2,512,128]{2,1,0:T(8,128)(2,1)S(1)}, f32[4,4,128]{2,1,0:T(4,128)S(1)}) custom-call(s32[16]{0:T(128)} %rows_ref.5, s32[16]{0:T(128)} %cols_ref.5, s32[16,256]{1,0:T(8,128)} %marker_ref.1, f32[1,4,4,128]{3,2,1,0:T(4,128)S(1)} %bitcast.7, ...), custom_call_target="tpu_custom_call" | custom-call | flops 1000000 | bytes 2000000 | tf_op jit(solution)/shard_map/pallas_call | solution.py:142
  21.3 1.6 %all-to-all-done.jones_ref = f32[16,4,8,128]{3,2,1,0:T(8,128)S(1)} async-done(((f32[16,4,8,128]{3,2,1,0:T(8,128)}), f32[16,4,8,128]{3,2,1,0:T(8,128)S(1)}, u32[]{:S(2)}, u32[]{:S(2)}) %all-to-all-start) | async-done | bytes 262176 | tf_op jit(solution)/shard_map/all_to_all | solution.py:418
  22.9 11.0 %shard_map.87 = f32[16,4,8,128]{3,2,1,0:T(8,128)} custom-call(s32[16]{0:T(128)} %rows_ref.5, s32[16]{0:T(128)} %cols_ref.5, f32[16,4,8,128]{3,2,1,0:T(8,128)S(1)} %all-to-all-done.jones_ref, bf16[16,8,32,256]{3,2,1,0:T(8,128)(2,1)} %bitcast.8, bf16[16,64,256]{2,1,0:T(8,128)(2,1)} %bitcast.10, f32[16,2,8,128]{3,2,1,0:T(8,128)S(1)} %get-tuple-element.18.keep_ref, ...), custom_call_target="tpu_custom_call" | custom-call | flops 40000000 | bytes 4000000 | tf_op jit(solution)/shard_map/pallas_call | solution.py:294
  34.0 5.9 %all-to-all-start.1 = ((f32[16,4,8,128]{3,2,1,0:T(8,128)}), f32[16,4,8,128]{3,2,1,0:T(8,128)S(1)}, u32[]{:S(2)}, u32[]{:S(2)}) async-start(f32[16,4,8,128]{3,2,1,0:T(8,128)} %shard_map.87), calls=%async_computation.1 | async-start | bytes 524288 | tf_op jit(solution)/shard_map/all_to_all | solution.py:424
  39.8 2.8 %collective-permute-start.5 = (f32[4,4,128]{2,1,0:T(4,128)S(1)}, f32[4,4,128]{2,1,0:T(4,128)S(1)}, u32[]{:S(2)}, u32[]{:S(2)}) collective-permute-start(f32[4,4,128]{2,1,0:T(4,128)S(1)} %get-tuple-element.21.refs_3_), channel_id=1, source_target_pairs={{0,6},{1,7},{2,4},{3,5},{4,2},{5,3},{6,0},{7,1},{8,14},{9,15},{10,... | collective-permute-start | bytes 24584 | tf_op jit(solution)/shard_map/ppermute | solution.py:397
  42.7 0.3 collective-permute-start.4
  43.0 0.3 collective-permute-start.3
  43.3 0.4 collective-permute-done.5.refs_6_
  43.7 3.1 %collective-permute-done.4.refs_5_ = f32[4,4,128]{2,1,0:T(4,128)S(1)} collective-permute-done((f32[4,4,128]{2,1,0:T(4,128)S(1)}, f32[4,4,128]{2,1,0:T(4,128)S(1)}, u32[]{:S(2)}, u32[]{:S(2)}) %collective-permute-start.4) | collective-permute-done | bytes 8224 | tf_op jit(solution)/shard_map/ppermute | solution.py:397
  46.8 4.0 %all-to-all-done.1.refs_2_ = f32[16,4,8,128]{3,2,1,0:T(8,128)S(1)} async-done(((f32[16,4,8,128]{3,2,1,0:T(8,128)}), f32[16,4,8,128]{3,2,1,0:T(8,128)S(1)}, u32[]{:S(2)}, u32[]{:S(2)}) %all-to-all-start.1) | async-done | bytes 262176 | tf_op jit(solution)/shard_map/all_to_all | solution.py:424
  50.8 0.1 shard_map.88
  50.9 12.9 %all_to_all.25.jones_ref = f32[16,4,8,128]{3,2,1,0:T(8,128)S(1)} all-to-all(f32[16,4,8,128]{3,2,1,0:T(8,128)S(1)} %get-tuple-element.23), channel_id=1, replica_groups=mesh['pair'=16,'chan'=16] {'pair'}, dimensions={0} | all-to-all | bytes 524288 | tf_op jit(solution)/shard_map/all_to_all | solution.py:428
  63.8 10.3 %shard_map.89 = f32[16,4,8,128]{3,2,1,0:T(8,128)S(1)} custom-call(s32[16]{0:T(128)} %rows_ref.5, s32[16]{0:T(128)} %cols_ref.5, f32[16,4,8,128]{3,2,1,0:T(8,128)S(1)} %all_to_all.25.jones_ref, bf16[16,8,32,256]{3,2,1,0:T(8,128)(2,1)} %bitcast.9, bf16[16,64,256]{2,1,0:T(8,128)(2,1)} %bitcast.11, f32[16,2,8,128]{3,2,1,0:T(8,128)S(1)} %get-tuple-element.18.keep_ref, ...), custom_call_target="tpu_custom_call" | custom-call | flops 40000000 | bytes 4000000 | tf_op jit(solution)/shard_map/pallas_call | solution.py:294
  74.1 12.3 %all_to_all.26.refs_1_ = f32[16,4,8,128]{3,2,1,0:T(8,128)S(1)} all-to-all(f32[16,4,8,128]{3,2,1,0:T(8,128)S(1)} %shard_map.89), channel_id=1, replica_groups=mesh['pair'=16,'chan'=16] {'pair'}, dimensions={0} | all-to-all | bytes 524288 | tf_op jit(solution)/shard_map/all_to_all | solution.py:430
  86.4 0.1 shard_map.90
  86.5 18.3 %all_to_all.27.refs_3_ = f32[16,4,8,128]{3,2,1,0:T(8,128)S(1)} all-to-all(f32[16,4,8,128]{3,2,1,0:T(8,128)S(1)} %get-tuple-element.26), channel_id=1, replica_groups=mesh['pair'=16,'chan'=16] {'chan'}, dimensions={0} | all-to-all | bytes 524288 | tf_op jit(solution)/shard_map/all_to_all | solution.py:438
  104.8 0.9 shard_map.91
  (4 shorter events, 0.0 us)
Async XLA Ops:
  0.6 0.9 copy-start
  2.4 20.6 %all-to-all-start = ((f32[16,4,8,128]{3,2,1,0:T(8,128)}), f32[16,4,8,128]{3,2,1,0:T(8,128)S(1)}, u32[]{:S(2)}, u32[]{:S(2)}) async-start(f32[16,4,8,128]{3,2,1,0:T(8,128)} %get-tuple-element.16), calls=%async_computation | async-start | bytes 524288 | tf_op jit(solution)/shard_map/all_to_all | solution.py:418
  12.4 5.3 %collective-permute-start.2 = (f32[1,4,4,128]{3,2,1,0:T(4,128)S(1)}, f32[1,4,4,128]{3,2,1,0:T(4,128)S(1)}, u32[]{:S(2)}, u32[]{:S(2)}) collective-permute-start(f32[1,4,4,128]{3,2,1,0:T(4,128)S(1)} %bitcast.4), channel_id=1, source_target_pairs={{0,9},{1,8},{2,11},{3,10},{4,13},{5,12},{6,15},{7,14},{8,1},{9,0},... | collective-permute-start | bytes 24584 | tf_op jit(solution)/shard_map/ppermute | solution.py:397
  15.8 4.4 %collective-permute-start.1 = (f32[1,4,4,128]{3,2,1,0:T(4,128)S(1)}, f32[1,4,4,128]{3,2,1,0:T(4,128)S(1)}, u32[]{:S(2)}, u32[]{:S(2)}) collective-permute-start(f32[1,4,4,128]{3,2,1,0:T(4,128)S(1)} %bitcast.5), channel_id=1, source_target_pairs={{0,8},{1,9},{2,10},{3,11},{4,12},{5,13},{6,14},{7,15},{8,0},{9,1},... | collective-permute-start | bytes 24584 | tf_op jit(solution)/shard_map/ppermute | solution.py:397
  16.3 3.9 %collective-permute-start = (f32[1,4,4,128]{3,2,1,0:T(4,128)S(1)}, f32[1,4,4,128]{3,2,1,0:T(4,128)S(1)}, u32[]{:S(2)}, u32[]{:S(2)}) collective-permute-start(f32[1,4,4,128]{3,2,1,0:T(4,128)S(1)} %bitcast.6), channel_id=1, source_target_pairs={{0,1},{1,0},{2,3},{3,2},{4,5},{5,4},{6,7},{7,6},{8,9},{9,8},{10,11... | collective-permute-start | bytes 24584 | tf_op jit(solution)/shard_map/ppermute | solution.py:397
  34.0 16.8 %all-to-all-start.1 = ((f32[16,4,8,128]{3,2,1,0:T(8,128)}), f32[16,4,8,128]{3,2,1,0:T(8,128)S(1)}, u32[]{:S(2)}, u32[]{:S(2)}) async-start(f32[16,4,8,128]{3,2,1,0:T(8,128)} %shard_map.87), calls=%async_computation.1 | async-start | bytes 524288 | tf_op jit(solution)/shard_map/all_to_all | solution.py:424
  39.8 3.9 %collective-permute-start.5 = (f32[4,4,128]{2,1,0:T(4,128)S(1)}, f32[4,4,128]{2,1,0:T(4,128)S(1)}, u32[]{:S(2)}, u32[]{:S(2)}) collective-permute-start(f32[4,4,128]{2,1,0:T(4,128)S(1)} %get-tuple-element.21.refs_3_), channel_id=1, source_target_pairs={{0,6},{1,7},{2,4},{3,5},{4,2},{5,3},{6,0},{7,1},{8,14},{9,15},{10,... | collective-permute-start | bytes 24584 | tf_op jit(solution)/shard_map/ppermute | solution.py:397
  42.7 4.2 %collective-permute-start.4 = (f32[4,4,128]{2,1,0:T(4,128)S(1)}, f32[4,4,128]{2,1,0:T(4,128)S(1)}, u32[]{:S(2)}, u32[]{:S(2)}) collective-permute-start(f32[4,4,128]{2,1,0:T(4,128)S(1)} %get-tuple-element.21.refs_3_), channel_id=1, source_target_pairs={{0,4},{1,5},{2,6},{3,7},{4,0},{5,1},{6,2},{7,3},{8,12},{9,13},{10,... | collective-permute-start | bytes 24584 | tf_op jit(solution)/shard_map/ppermute | solution.py:397
  43.0 3.8 %collective-permute-start.3 = (f32[4,4,128]{2,1,0:T(4,128)S(1)}, f32[4,4,128]{2,1,0:T(4,128)S(1)}, u32[]{:S(2)}, u32[]{:S(2)}) collective-permute-start(f32[4,4,128]{2,1,0:T(4,128)S(1)} %get-tuple-element.21.refs_3_), channel_id=1, source_target_pairs={{0,2},{1,3},{2,0},{3,1},{4,6},{5,7},{6,4},{7,5},{8,10},{9,11},{10,... | collective-permute-start | bytes 24584 | tf_op jit(solution)/shard_map/ppermute | solution.py:397

commit v5 on v4

--- a/solution.py
+++ b/solution.py
@@ -97,6 +97,34 @@
     return item
 
 
+def with_sums(matrix):
+    return [(item[0], item[1] - item[0], item[0] + item[1]) for item in matrix]
+
+
+def three(sums, first, second, third):
+    terms = (first[0] * first[1], second[0] * second[1], third[0] * third[1])
+    return terms if sums is None else tuple(x + y for x, y in zip(sums, terms))
+
+
+def conj_right(x, y, left, right, sums=None):
+    for l, r in zip(left, right):
+        re, im = x[l]
+        sums = three(sums, (y[r][0], re + im), (im, y[r][1]), (re, y[r][2]))
+    return sums
+
+
+def conj_right_value(sums):
+    return (sums[0] + sums[1], sums[0] - sums[2])
+
+
+def conj_left(x, y, left, right):
+    sums = None
+    for l, r in zip(left, right):
+        re, im = x[l]
+        sums = three(sums, (y[r][0], re - im), (im, y[r][2]), (re, y[r][1]))
+    return (sums[0] + sums[1], sums[0] + sums[2])
+
+
 def pairs(list8):
     return [(list8[2 * e], list8[2 * e + 1]) for e in range(4)]
 
@@ -120,9 +148,10 @@
         one = one_hot(source == (n // 3) * BLK + tables[n % 3])
         spread_ref[0:LANES, n * LANES : n * LANES + LANES] = one
         spread_ref[LANES : 2 * LANES, n * LANES : n * LANES + LANES] = one
+    column = source // 64 * BLK + source % BLK
     for n in range(4):
         sums_ref[0, n * LANES : n * LANES + LANES] = one_hot(target == 2 * n * BLK + source // BLK)
-        sums_ref[1, n * LANES : n * LANES + LANES] = one_hot(target == 2 * n * BLK + source % BLK)
+        sums_ref[1, n * LANES : n * LANES + LANES] = one_hot(target == 2 * n * BLK + column)
 
     lane = lane_iota()
     for t in range(rows_ref.shape[0]):
@@ -213,6 +242,16 @@
             ]
         )
 
+    lane = lane_iota()
+
+    def merged(item, dist):
+        low = (lane & dist) == 0
+        kept = jnp.where(low, item[0], item[1])
+        sent = jnp.where(low, item[1], item[0])
+        if dist == LANES // 2:
+            return kept + pltpu.roll(sent, dist, 1)
+        return kept + jnp.take_along_axis(sent, lane ^ dist, axis=1, mode="promise_in_bounds")
+
     def put(ref, part, item):
         ref[0:8, part * LANES : part * LANES + LANES] = item[0]
         ref[8:16, part * LANES : part * LANES + LANES] = item[1]
@@ -235,40 +274,48 @@
                     left_ref[half, k, e] = piece
                 acc = mat_mul(left, expand(b, k, 0), acc, y_herm=True, minus=True)
             keep = keep_ref[t, half]
+            acc = with_sums([(item[0] * keep, item[1] * keep) for item in acc])
             for e, piece in enumerate(flat(acc)):
-                res_ref[half, e] = piece * keep
+                res_ref[half, e] = piece
         for k in range(DIRS):
-            right = expand(b, k, 0)
+            right = with_sums(expand(b, k, 0))
             cols = [None] * 4
             for half in range(2):
-                res = pairs([res_ref[half, e] for e in range(8)])
-                turned = mat_mul(coher_of(t, k, half), right, y_herm=True)
+                res = [tuple(res_ref[half, 3 * e + n] for n in range(3)) for e in range(4)]
+                coher = coher_of(t, k, half)
+                turned = []
+                for i in range(2):
+                    for j in range(2):
+                        sums = conj_right(coher, right, (2 * i, 2 * i + 1), (2 * j, 2 * j + 1))
+                        turned.append(conj_right_value(sums))
                 for e in range(4):
-                    item = mat_entry(res, turned, e // 2, e % 2, y_herm=True)
+                    i, j = e // 2, e % 2
+                    item = conj_left(turned, res, (2 * j, 2 * j + 1), (2 * i, 2 * i + 1))
                     put(row_ref.at[t, k, half], e, item)
                 left = pairs([left_ref[half, k, e] for e in range(8)])
                 for e in range(4):
-                    cols[e] = mat_entry(res, left, e // 2, e % 2, cols[e], x_herm=True)
+                    i, j = e // 2, e % 2
+                    cols[e] = conj_right(left, res, (j, 2 + j), (i, 2 + i), cols[e])
                     if half == 1:
-                        put(col_ref.at[t, k], e, cols[e])
+                        col_ref[t, k, :, e * LANES : e * LANES + LANES] = merged(conj_right_value(cols[e]), 64)
         return carry
 
     lax.fori_loop(0, slots, multiply, 0)
 
-    group = 8
+    group = slots
 
     def total(values, sums):
         high = values.astype(jnp.bfloat16)
-        low = (values - high.astype(jnp.float32)).astype(jnp.bfloat16)
+        low = values - high.astype(jnp.float32)
         out = jnp.dot(high, sums, preferred_element_type=jnp.float32)
-        return out + jnp.dot(low, sums, preferred_element_type=jnp.float32)
+        return out + jnp.dot(low, sums.astype(jnp.float32), preferred_element_type=jnp.float32)
 
     def settle(g, carry):
         t0 = g * group
         rows = total(row_ref[pl.ds(t0, group)].reshape(group * DIRS * 32, 4 * LANES), sums_ref[0])
-        cols = total(col_ref[pl.ds(t0, group)].reshape(group * DIRS * 16, 4 * LANES), sums_ref[1])
+        cols = total(col_ref[pl.ds(t0, group)].reshape(group * DIRS * 8, 4 * LANES), sums_ref[1])
         rows = rows.reshape(group, DIRS, 2, 2, CHANS, LANES)
-        cols = cols.reshape(group, DIRS, 2, CHANS, LANES)
+        cols = cols.reshape(group, DIRS, CHANS, LANES)
         for n in range(group):
             a = jnp.maximum(rows_ref[t0 + n], 0)
             b = jnp.maximum(cols_ref[t0 + n], 0)
@@ -277,8 +324,7 @@
                 row = row[0] + pltpu.roll(row[1], BLK, 1)
                 out_ref[a, k] = out_ref[a, k] + row
             for k in range(DIRS):
-                col = cols[n, k, 0] + pltpu.roll(cols[n, k, 1], BLK, 1)
-                out_ref[b, k] = out_ref[b, k] + col
+                out_ref[b, k] = out_ref[b, k] + cols[n, k]
         return carry
 
     lax.fori_loop(0, slots // group, settle, 0)
@@ -301,9 +347,9 @@
             pltpu.VMEM(seen.shape, jnp.bfloat16),
             pltpu.VMEM((blocks * DIRS, CHANS, 24 * LANES), jnp.float32),
             pltpu.VMEM((2, DIRS, 8, CHANS, LANES), jnp.float32),
-            pltpu.VMEM((2, 8, CHANS, LANES), jnp.float32),
+            pltpu.VMEM((2, 12, CHANS, LANES), jnp.float32),
             pltpu.VMEM((slots, DIRS, 2, 16, 4 * LANES), jnp.float32),
-            pltpu.VMEM((slots, DIRS, 16, 4 * LANES), jnp.float32),
+            pltpu.VMEM((slots, DIRS, CHANS, 4 * LANES), jnp.float32),
             pltpu.SemaphoreType.DMA((slots,)),
             pltpu.SemaphoreType.DMA((slots,)),
         ],

time: 106 us -> 104 us (0.981)
  Pallas kernels: 24.5 us -> 22.6 us
    pallas_call x2, Pallas kernels: 21.4 us -> 19.5 us  [local_descent(): pl.pallas_call(descent_kernel, out_shape=jax.ShapeDtypeStruct((blocks, DI...]
where the time goes in v5:
time: 104 us
  blocking collectives  43.4 us (42%)
  starting transfers between devices  23.3 us (22%)
  Pallas kernels  22.6 us (22%)
  waiting for transfers between devices  12.9 us (12%)
    pallas_call x2, Pallas kernels, local_descent(): pl.pallas_call(descent_kernel, out_shape=jax.ShapeDtypeStruct((blocks, DI...  19.5 us
    all_to_all x1, blocking collectives, local(): sums = lax.all_to_all(sums, 'chan', 0, 0)  18.3 us
    all_to_all x1, blocking collectives, local(): full = lax.all_to_all(sent, 'pair', 0, 0)  12.9 us
    all_to_all x1, blocking collectives, local(): terms = lax.all_to_all(terms, 'pair', 0, 0)  12.3 us
    all_to_all x1, starting transfers between devices, local(): full = lax.all_to_all(sent, 'pair', 0, 0)  10 us
    ppermute x6, starting transfers between devices, flipped(): return lax.ppermute(array, 'chan', [(i, i ^ bits) for i in range(count)])  7.4 us
    ppermute x6, waiting for transfers between devices, flipped(): return lax.ppermute(array, 'chan', [(i, i ^ bits) for i in range(count)])  7.35 us
    all_to_all x1, starting transfers between devices, local(): terms = lax.all_to_all(terms, 'pair', 0, 0)  5.9 us
  transfers between devices with their start and end apart: 8, of which 6 were waited for; matrix products, arithmetic and copies ran while one was open for 0% of the time, Pallas kernels for 1%

profile of v5, /device:TPU:1, one launch (start us, length us, event | category | flops | bytes accessed | tf_op | source)
XLA Modules:
  0.0 103.8 jit_solution(1532371608936553744)
XLA Ops:
  0.6 0.9 copy-done
  1.5 0.8 shard_map.85
  2.4 10.0 %all-to-all-start = ((f32[16,4,8,128]{3,2,1,0:T(8,128)}), f32[16,4,8,128]{3,2,1,0:T(8,128)S(1)}, u32[]{:S(2)}, u32[]{:S(2)}) async-start(f32[16,4,8,128]{3,2,1,0:T(8,128)} %get-tuple-element.16), calls=%async_computation | async-start | bytes 524288 | tf_op jit(solution)/shard_map/all_to_all | solution.py:464
  12.4 3.4 %collective-permute-start.2 = (f32[1,4,4,128]{3,2,1,0:T(4,128)S(1)}, f32[1,4,4,128]{3,2,1,0:T(4,128)S(1)}, u32[]{:S(2)}, u32[]{:S(2)}) collective-permute-start(f32[1,4,4,128]{3,2,1,0:T(4,128)S(1)} %bitcast.4), channel_id=1, source_target_pairs={{0,9},{1,8},{2,11},{3,10},{4,13},{5,12},{6,15},{7,14},{8,1},{9,0},... | collective-permute-start | bytes 24584 | tf_op jit(solution)/shard_map/ppermute | solution.py:443
  15.8 0.5 collective-permute-start.1
  16.3 1.4 %collective-permute-done.2.refs_3_ = f32[1,4,4,128]{3,2,1,0:T(4,128)S(1)} collective-permute-done((f32[1,4,4,128]{3,2,1,0:T(4,128)S(1)}, f32[1,4,4,128]{3,2,1,0:T(4,128)S(1)}, u32[]{:S(2)}, u32[]{:S(2)}) %collective-permute-start.2) | collective-permute-done | bytes 8224 | tf_op jit(solution)/shard_map/ppermute | solution.py:443
  17.7 2.4 %collective-permute-done.1.refs_2_ = f32[1,4,4,128]{3,2,1,0:T(4,128)S(1)} collective-permute-done((f32[1,4,4,128]{3,2,1,0:T(4,128)S(1)}, f32[1,4,4,128]{3,2,1,0:T(4,128)S(1)}, u32[]{:S(2)}, u32[]{:S(2)}) %collective-permute-start.1) | collective-permute-done | bytes 8224 | tf_op jit(solution)/shard_map/ppermute | solution.py:443
  20.2 1.1 %shard_map.86 = (f32[16,2,8,128]{3,2,1,0:T(8,128)S(1)}, bf16[256,3072]{1,0:T(8,128)(2,1)S(1)}, bf16[2,512,128]{2,1,0:T(8,128)(2,1)S(1)}, f32[4,4,128]{2,1,0:T(4,128)S(1)}) custom-call(s32[16]{0:T(128)} %rows_ref.5, s32[16]{0:T(128)} %cols_ref.5, s32[16,256]{1,0:T(8,128)} %marker_ref.1, f32[1,4,4,128]{3,2,1,0:T(4,128)S(1)} %bitcast.7, ...), custom_call_target="tpu_custom_call" | custom-call | flops 1000000 | bytes 2000000 | tf_op jit(solution)/shard_map/pallas_call | solution.py:171
  21.3 1.6 %all-to-all-done.jones_ref = f32[16,4,8,128]{3,2,1,0:T(8,128)S(1)} async-done(((f32[16,4,8,128]{3,2,1,0:T(8,128)}), f32[16,4,8,128]{3,2,1,0:T(8,128)S(1)}, u32[]{:S(2)}, u32[]{:S(2)}) %all-to-all-start) | async-done | bytes 262176 | tf_op jit(solution)/shard_map/all_to_all | solution.py:464
  22.9 10.1 %shard_map.87 = f32[16,4,8,128]{3,2,1,0:T(8,128)} custom-call(s32[16]{0:T(128)} %rows_ref.5, s32[16]{0:T(128)} %cols_ref.5, f32[16,4,8,128]{3,2,1,0:T(8,128)S(1)} %all-to-all-done.jones_ref, bf16[16,8,32,256]{3,2,1,0:T(8,128)(2,1)} %bitcast.8, bf16[16,64,256]{2,1,0:T(8,128)(2,1)} %bitcast.10, f32[16,2,8,128]{3,2,1,0:T(8,128)S(1)} %get-tuple-element.18.keep_ref, ...), custom_call_target="tpu_custom_call" | custom-call | flops 40000000 | bytes 4000000 | tf_op jit(solution)/shard_map/pallas_call | solution.py:340
  33.0 5.9 %all-to-all-start.1 = ((f32[16,4,8,128]{3,2,1,0:T(8,128)}), f32[16,4,8,128]{3,2,1,0:T(8,128)S(1)}, u32[]{:S(2)}, u32[]{:S(2)}) async-start(f32[16,4,8,128]{3,2,1,0:T(8,128)} %shard_map.87), calls=%async_computation.1 | async-start | bytes 524288 | tf_op jit(solution)/shard_map/all_to_all | solution.py:470
  38.9 2.8 %collective-permute-start.5 = (f32[4,4,128]{2,1,0:T(4,128)S(1)}, f32[4,4,128]{2,1,0:T(4,128)S(1)}, u32[]{:S(2)}, u32[]{:S(2)}) collective-permute-start(f32[4,4,128]{2,1,0:T(4,128)S(1)} %get-tuple-element.21.refs_3_), channel_id=1, source_target_pairs={{0,6},{1,7},{2,4},{3,5},{4,2},{5,3},{6,0},{7,1},{8,14},{9,15},{10,... | collective-permute-start | bytes 24584 | tf_op jit(solution)/shard_map/ppermute | solution.py:443
  41.7 0.4 collective-permute-start.4
  42.1 0.3 collective-permute-start.3
  42.4 0.4 collective-permute-done.5.refs_6_
  42.8 3.1 %collective-permute-done.4.refs_5_ = f32[4,4,128]{2,1,0:T(4,128)S(1)} collective-permute-done((f32[4,4,128]{2,1,0:T(4,128)S(1)}, f32[4,4,128]{2,1,0:T(4,128)S(1)}, u32[]{:S(2)}, u32[]{:S(2)}) %collective-permute-start.4) | collective-permute-done | bytes 8224 | tf_op jit(solution)/shard_map/ppermute | solution.py:443
  45.9 4.0 %all-to-all-done.1.refs_2_ = f32[16,4,8,128]{3,2,1,0:T(8,128)S(1)} async-done(((f32[16,4,8,128]{3,2,1,0:T(8,128)}), f32[16,4,8,128]{3,2,1,0:T(8,128)S(1)}, u32[]{:S(2)}, u32[]{:S(2)}) %all-to-all-start.1) | async-done | bytes 262176 | tf_op jit(solution)/shard_map/all_to_all | solution.py:470
  49.9 0.1 shard_map.88
  50.0 12.9 %all_to_all.25.jones_ref = f32[16,4,8,128]{3,2,1,0:T(8,128)S(1)} all-to-all(f32[16,4,8,128]{3,2,1,0:T(8,128)S(1)} %get-tuple-element.23), channel_id=1, replica_groups=mesh['pair'=16,'chan'=16] {'pair'}, dimensions={0} | all-to-all | bytes 524288 | tf_op jit(solution)/shard_map/all_to_all | solution.py:474
  62.9 9.4 %shard_map.89 = f32[16,4,8,128]{3,2,1,0:T(8,128)S(1)} custom-call(s32[16]{0:T(128)} %rows_ref.5, s32[16]{0:T(128)} %cols_ref.5, f32[16,4,8,128]{3,2,1,0:T(8,128)S(1)} %all_to_all.25.jones_ref, bf16[16,8,32,256]{3,2,1,0:T(8,128)(2,1)} %bitcast.9, bf16[16,64,256]{2,1,0:T(8,128)(2,1)} %bitcast.11, f32[16,2,8,128]{3,2,1,0:T(8,128)S(1)} %get-tuple-element.18.keep_ref, ...), custom_call_target="tpu_custom_call" | custom-call | flops 40000000 | bytes 4000000 | tf_op jit(solution)/shard_map/pallas_call | solution.py:340
  72.3 12.3 %all_to_all.26.refs_1_ = f32[16,4,8,128]{3,2,1,0:T(8,128)S(1)} all-to-all(f32[16,4,8,128]{3,2,1,0:T(8,128)S(1)} %shard_map.89), channel_id=1, replica_groups=mesh['pair'=16,'chan'=16] {'pair'}, dimensions={0} | all-to-all | bytes 524288 | tf_op jit(solution)/shard_map/all_to_all | solution.py:476
  84.5 0.1 shard_map.90
  84.6 18.3 %all_to_all.27.refs_3_ = f32[16,4,8,128]{3,2,1,0:T(8,128)S(1)} all-to-all(f32[16,4,8,128]{3,2,1,0:T(8,128)S(1)} %get-tuple-element.26), channel_id=1, replica_groups=mesh['pair'=16,'chan'=16] {'chan'}, dimensions={0} | all-to-all | bytes 524288 | tf_op jit(solution)/shard_map/all_to_all | solution.py:484
  102.9 0.9 shard_map.91
  (4 shorter events, 0.0 us)
Async XLA Ops:
  0.6 0.9 copy-start
  2.4 20.6 %all-to-all-start = ((f32[16,4,8,128]{3,2,1,0:T(8,128)}), f32[16,4,8,128]{3,2,1,0:T(8,128)S(1)}, u32[]{:S(2)}, u32[]{:S(2)}) async-start(f32[16,4,8,128]{3,2,1,0:T(8,128)} %get-tuple-element.16), calls=%async_computation | async-start | bytes 524288 | tf_op jit(solution)/shard_map/all_to_all | solution.py:464
  12.4 5.3 %collective-permute-start.2 = (f32[1,4,4,128]{3,2,1,0:T(4,128)S(1)}, f32[1,4,4,128]{3,2,1,0:T(4,128)S(1)}, u32[]{:S(2)}, u32[]{:S(2)}) collective-permute-start(f32[1,4,4,128]{3,2,1,0:T(4,128)S(1)} %bitcast.4), channel_id=1, source_target_pairs={{0,9},{1,8},{2,11},{3,10},{4,13},{5,12},{6,15},{7,14},{8,1},{9,0},... | collective-permute-start | bytes 24584 | tf_op jit(solution)/shard_map/ppermute | solution.py:443
  15.8 4.4 %collective-permute-start.1 = (f32[1,4,4,128]{3,2,1,0:T(4,128)S(1)}, f32[1,4,4,128]{3,2,1,0:T(4,128)S(1)}, u32[]{:S(2)}, u32[]{:S(2)}) collective-permute-start(f32[1,4,4,128]{3,2,1,0:T(4,128)S(1)} %bitcast.5), channel_id=1, source_target_pairs={{0,8},{1,9},{2,10},{3,11},{4,12},{5,13},{6,14},{7,15},{8,0},{9,1},... | collective-permute-start | bytes 24584 | tf_op jit(solution)/shard_map/ppermute | solution.py:443
  16.3 3.9 %collective-permute-start = (f32[1,4,4,128]{3,2,1,0:T(4,128)S(1)}, f32[1,4,4,128]{3,2,1,0:T(4,128)S(1)}, u32[]{:S(2)}, u32[]{:S(2)}) collective-permute-start(f32[1,4,4,128]{3,2,1,0:T(4,128)S(1)} %bitcast.6), channel_id=1, source_target_pairs={{0,1},{1,0},{2,3},{3,2},{4,5},{5,4},{6,7},{7,6},{8,9},{9,8},{10,11... | collective-permute-start | bytes 24584 | tf_op jit(solution)/shard_map/ppermute | solution.py:443
  33.0 16.9 %all-to-all-start.1 = ((f32[16,4,8,128]{3,2,1,0:T(8,128)}), f32[16,4,8,128]{3,2,1,0:T(8,128)S(1)}, u32[]{:S(2)}, u32[]{:S(2)}) async-start(f32[16,4,8,128]{3,2,1,0:T(8,128)} %shard_map.87), calls=%async_computation.1 | async-start | bytes 524288 | tf_op jit(solution)/shard_map/all_to_all | solution.py:470
  38.9 3.9 %collective-permute-start.5 = (f32[4,4,128]{2,1,0:T(4,128)S(1)}, f32[4,4,128]{2,1,0:T(4,128)S(1)}, u32[]{:S(2)}, u32[]{:S(2)}) collective-permute-start(f32[4,4,128]{2,1,0:T(4,128)S(1)} %get-tuple-element.21.refs_3_), channel_id=1, source_target_pairs={{0,6},{1,7},{2,4},{3,5},{4,2},{5,3},{6,0},{7,1},{8,14},{9,15},{10,... | collective-permute-start | bytes 24584 | tf_op jit(solution)/shard_map/ppermute | solution.py:443
  41.7 4.2 %collective-permute-start.4 = (f32[4,4,128]{2,1,0:T(4,128)S(1)}, f32[4,4,128]{2,1,0:T(4,128)S(1)}, u32[]{:S(2)}, u32[]{:S(2)}) collective-permute-start(f32[4,4,128]{2,1,0:T(4,128)S(1)} %get-tuple-element.21.refs_3_), channel_id=1, source_target_pairs={{0,4},{1,5},{2,6},{3,7},{4,0},{5,1},{6,2},{7,3},{8,12},{9,13},{10,... | collective-permute-start | bytes 24584 | tf_op jit(solution)/shard_map/ppermute | solution.py:443
  42.1 3.8 %collective-permute-start.3 = (f32[4,4,128]{2,1,0:T(4,128)S(1)}, f32[4,4,128]{2,1,0:T(4,128)S(1)}, u32[]{:S(2)}, u32[]{:S(2)}) collective-permute-start(f32[4,4,128]{2,1,0:T(4,128)S(1)} %get-tuple-element.21.refs_3_), channel_id=1, source_target_pairs={{0,2},{1,3},{2,0},{3,1},{4,6},{5,7},{6,4},{7,5},{8,10},{9,11},{10,... | collective-permute-start | bytes 24584 | tf_op jit(solution)/shard_map/ppermute | solution.py:443

commit v6 on v5

--- a/solution.py
+++ b/solution.py
@@ -137,10 +137,12 @@
     return jnp.where(hit, 1.0, 0.0).astype(jnp.bfloat16)
 
 
-def stage_kernel(rows_ref, cols_ref, marker_ref, *refs):
-    part_refs, (keep_ref, spread_ref, sums_ref, total_ref) = refs[:-4], refs[-4:]
-    parts = [ref[n] for ref in part_refs for n in range(ref.shape[0])]
-    total_ref[...] = sum(parts[1:], parts[0])
+def stage_kernel(
+    rows_ref, cols_ref, marker_ref, keep_ref, spread_ref, sums_ref, rows_out, cols_out
+):
+    for t in range(rows_ref.shape[0]):
+        rows_out[t] = rows_ref[t]
+        cols_out[t] = cols_ref[t]
     source = lax.broadcasted_iota(jnp.int32, (LANES, LANES), 0)
     target = lax.broadcasted_iota(jnp.int32, (LANES, LANES), 1)
     tables = [target % BLK, target // BLK, target // BLK + 8]
@@ -164,7 +166,7 @@
             keep_ref[t, half] = keep
 
 
-def stage(marker, rows, cols, parts):
+def stage(marker, rows, cols):
     slots = rows.shape[0]
     vmem = pl.BlockSpec(memory_space=pltpu.VMEM)
     smem = pl.BlockSpec(memory_space=pltpu.SMEM)
@@ -174,13 +176,14 @@
             pltpu.VMEM((slots, 2, CHANS, LANES), jnp.float32),
             pltpu.VMEM((2 * LANES, 24 * LANES), jnp.bfloat16),
             pltpu.VMEM((2, 4 * LANES, LANES), jnp.bfloat16),
-            jax.ShapeDtypeStruct(parts[0].shape[1:], jnp.float32),
+            pltpu.SMEM((slots,), jnp.int32),
+            pltpu.SMEM((slots,), jnp.int32),
         ],
-        in_specs=[smem, smem, vmem] + [vmem] * len(parts),
-        out_specs=[vmem] * 4,
+        in_specs=[smem, smem, vmem],
+        out_specs=[vmem] * 3 + [smem] * 2,
         compiler_params=pltpu.CompilerParams(vmem_limit_bytes=SMALL_LIMIT),
         cost_estimate=pl.CostEstimate(flops=1_000_000, bytes_accessed=2_000_000, transcendentals=0),
-    )(in_hbm(rows), in_hbm(cols), in_hbm(marker), *parts)
+    )(in_hbm(rows), in_hbm(cols), in_hbm(marker))
 
 
 def descent_kernel(
@@ -336,6 +339,9 @@
     vmem = pl.BlockSpec(memory_space=pltpu.VMEM)
     smem = pl.BlockSpec(memory_space=pltpu.SMEM)
     hbm = pl.BlockSpec(memory_space=pltpu.HBM)
+    *staged, rows, cols = staged
+    rows = pltpu.with_memory_space_constraint(rows, pltpu.SMEM)
+    cols = pltpu.with_memory_space_constraint(cols, pltpu.SMEM)
     staged = [pltpu.with_memory_space_constraint(x, pltpu.VMEM) for x in staged]
     return pl.pallas_call(
         descent_kernel,
@@ -357,7 +363,47 @@
         cost_estimate=pl.CostEstimate(
             flops=40_000_000, bytes_accessed=4_000_000, transcendentals=0
         ),
-    )(in_hbm(rows), in_hbm(cols), jones_full, in_hbm(coher), in_hbm(seen), *staged)
+    )(rows, cols, jones_full, in_hbm(coher), in_hbm(seen), *staged)
+
+
+def sum_kernel(count, *refs):
+    refs[-1][...] = sum([ref[...] for ref in refs[1:count]], refs[0][...])
+
+
+def sum_of(parts, after=None):
+    def body(*refs):
+        sum_kernel(len(parts), *refs)
+
+    waited = [] if after is None else [after]
+    vmem = pl.BlockSpec(memory_space=pltpu.VMEM)
+    return pl.pallas_call(
+        body,
+        out_shape=jax.ShapeDtypeStruct(parts[0].shape, parts[0].dtype),
+        in_specs=[vmem] * len(parts) + [pl.BlockSpec(memory_space=pl.ANY)] * len(waited),
+        out_specs=vmem,
+        compiler_params=pltpu.CompilerParams(vmem_limit_bytes=SMALL_LIMIT),
+    )(*parts, *waited)
+
+
+def add_kernel(terms_ref, *refs):
+    part_refs, (passed_ref, total_ref) = refs[:-2], refs[-2:]
+    total_ref[...] = sum([ref[...] for ref in part_refs[1:]], part_refs[0][...])
+
+
+def add_beside(terms, parts):
+    vmem = pl.BlockSpec(memory_space=pltpu.VMEM)
+    whole = pl.BlockSpec(memory_space=pl.ANY)
+    return pl.pallas_call(
+        add_kernel,
+        out_shape=[
+            jax.ShapeDtypeStruct(terms.shape, terms.dtype),
+            jax.ShapeDtypeStruct(parts[0].shape, parts[0].dtype),
+        ],
+        in_specs=[whole] + [vmem] * len(parts),
+        out_specs=[whole, vmem],
+        input_output_aliases={0: 0},
+        compiler_params=pltpu.CompilerParams(vmem_limit_bytes=SMALL_LIMIT),
+    )(terms, *parts)
 
 
 def to_dense_kernel(total, chan_ref, start_ref, dense_ref, sent_ref, part_ref):
@@ -460,16 +506,17 @@
     block = (DIRS, CHANS, LANES)
     blocks = (pair_count,) + block
     poly = (DIRS, NP, LANES)
-    jones, sent, part = small_call(to_dense_kernel, total, chan, [start], [block, blocks, poly])
+    jones, sent, part = small_call(to_dense_kernel, total, chan, [in_hbm(start)], [block, blocks, poly])
     full = lax.all_to_all(sent, "pair", 0, 0)
     bits = [1 << i for i in range(chan_count.bit_length() - 1)]
-    parts = exchanged(part[None], bits[:1] + bits[3:], chan_count)
-    *staged, part = stage(marker, rows, cols, parts)
+    part = sum_of(exchanged(part, bits[:1], chan_count))
+    staged = stage(marker, rows, cols)
+    part = sum_of(exchanged(part, bits[1:3], chan_count), after=staged[0])
     terms = local_descent(full, rows, cols, coher, seen, staged)
-    coeff_parts = exchanged(part, bits[1:3], chan_count)
+    terms, coeffs = add_beside(terms, exchanged(part, bits[3:], chan_count))
     terms = lax.all_to_all(terms, "pair", 0, 0)
     jones, sent, part = small_call(
-        first_update_kernel, total, chan, [jones, terms] + coeff_parts, [block, blocks, poly]
+        first_update_kernel, total, chan, [jones, terms, coeffs], [block, blocks, poly]
     )
     full = lax.all_to_all(sent, "pair", 0, 0)
     terms = local_descent(full, rows, cols, coher, seen, staged)

time: 104 us -> 103 us (level)
  blocking collectives: 43.4 us -> 60.4 us
  waiting for transfers between devices: 12.9 us -> 3.07 us
  starting transfers between devices: 23.3 us -> 17 us
  Pallas kernels: 22.6 us -> 21.4 us
    all_to_all x1 -> x2, blocking collectives: 12.3 us -> 28.8 us  [local(): terms = lax.all_to_all(terms, 'pair', 0, 0)]
    all_to_all x1 -> x0, starting transfers between devices: 5.9 us -> none  [local(): terms = lax.all_to_all(terms, 'pair', 0, 0)]
    ppermute x6 -> x5, waiting for transfers between devices: 7.35 us -> 3.07 us  [flipped(): return lax.ppermute(array, 'chan', [(i, i ^ bits) for i in range(count)])]
    all_to_all x1 -> x0, waiting for transfers between devices: 3.96 us -> none  [local(): terms = lax.all_to_all(terms, 'pair', 0, 0)]
    pallas_call x2, Pallas kernels: 19.5 us -> 17.4 us  [local_descent(): pl.pallas_call(descent_kernel, out_shape=jax.ShapeDtypeStruct((blocks, DI...]
    all_to_all x1, waiting for transfers between devices: 1.58 us -> 0.01 us  [local(): full = lax.all_to_all(sent, 'pair', 0, 0)]
    ppermute x6 -> x5, starting transfers between devices: 7.4 us -> 6.93 us  [flipped(): return lax.ppermute(array, 'chan', [(i, i ^ bits) for i in range(count)])]
  transfers between devices with their start and end apart: 8 -> 6, of which waited for: 6 -> 2; matrix products, arithmetic and copies ran while one was open for 0% -> 0% of each run, Pallas kernels for 1% -> 10%
where the time goes in v6:
time: 103 us; the launch traced here: 102 us
  blocking collectives  60.4 us (59%)
  Pallas kernels  21.4 us (21%)
  starting transfers between devices  17 us (17%)
  waiting for transfers between devices  3.07 us (3%)
    all_to_all x2, blocking collectives, local(): terms = lax.all_to_all(terms, 'pair', 0, 0)  28.8 us
    all_to_all x1, blocking collectives, local(): sums = lax.all_to_all(sums, 'chan', 0, 0)  19.2 us
    pallas_call x2, Pallas kernels, local_descent(): pl.pallas_call(descent_kernel, out_shape=jax.ShapeDtypeStruct((blocks, DI...  17.4 us
    all_to_all x1, blocking collectives, local(): full = lax.all_to_all(sent, 'pair', 0, 0)  12.3 us
    all_to_all x1, starting transfers between devices, local(): full = lax.all_to_all(sent, 'pair', 0, 0)  10 us
    ppermute x5, starting transfers between devices, flipped(): return lax.ppermute(array, 'chan', [(i, i ^ bits) for i in range(count)])  6.93 us
    ppermute x5, waiting for transfers between devices, flipped(): return lax.ppermute(array, 'chan', [(i, i ^ bits) for i in range(count)])  3.07 us
    pallas_call x4, Pallas kernels, small_call(): pl.pallas_call(body, out_shape=[jax.ShapeDtypeStruct(s, jnp.float32) for...  2.84 us
  transfers between devices with their start and end apart: 6, of which 2 were waited for; matrix products, arithmetic and copies ran while one was open for 0% of the time, Pallas kernels for 10%

profile of v6, /device:TPU:1, one launch (start us, length us, event | category | flops | bytes accessed | tf_op | source)
XLA Modules:
  0.0 102.5 jit_solution(13803333385280356241)
XLA Ops:
  0.6 1.7 %shard_map.85 = (f32[4,8,128]{2,1,0:T(8,128)S(1)}, f32[16,4,8,128]{3,2,1,0:T(8,128)}, f32[4,4,128]{2,1,0:T(4,128)S(1)}) custom-call(s32[1]{0:T(128)} %bitcast.refs_0_, f32[8,4,8,16]{3,2,1,0:T(8,128)} %refs_1_.1), custom_call_target="tpu_custom_call" | custom-call | tf_op jit(solution)/shard_map/pallas_call | solution.py:479
  2.4 10.0 %all-to-all-start = ((f32[16,4,8,128]{3,2,1,0:T(8,128)}), f32[16,4,8,128]{3,2,1,0:T(8,128)S(1)}, u32[]{:S(2)}, u32[]{:S(2)}) async-start(f32[16,4,8,128]{3,2,1,0:T(8,128)} %get-tuple-element.21), calls=%async_computation | async-start | bytes 524288 | tf_op jit(solution)/shard_map/all_to_all | solution.py:510
  12.4 1.0 %collective-permute-start = (f32[4,4,128]{2,1,0:T(4,128)S(1)}, f32[4,4,128]{2,1,0:T(4,128)S(1)}, u32[]{:S(2)}, u32[]{:S(2)}) collective-permute-start(f32[4,4,128]{2,1,0:T(4,128)S(1)} %get-tuple-element.25.refs_0_), channel_id=1, source_target_pairs={{0,1},{1,0},{2,3},{3,2},{4,5},{5,4},{6,7},{7,6},{8,9},{9,8},{10,11... | collective-permute-start | bytes 24584 | tf_op jit(solution)/shard_map/ppermute | solution.py:489
  13.5 0.8 collective-permute-done.refs_1_
  14.3 2.7 %collective-permute-start.3 = (f32[4,4,128]{2,1,0:T(4,128)S(1)}, f32[4,4,128]{2,1,0:T(4,128)S(1)}, u32[]{:S(2)}, u32[]{:S(2)}) collective-permute-start(f32[4,4,128]{2,1,0:T(4,128)S(1)} %shard_map.88.refs_0_), channel_id=1, source_target_pairs={{0,6},{1,7},{2,4},{3,5},{4,2},{5,3},{6,0},{7,1},{8,14},{9,15},{10,... | collective-permute-start | bytes 24584 | tf_op jit(solution)/shard_map/ppermute | solution.py:489
  17.0 0.3 collective-permute-start.2
  17.4 0.3 collective-permute-start.1
  17.7 1.1 %shard_map.86 = (f32[16,2,8,128]{3,2,1,0:T(8,128)S(1)}, bf16[256,3072]{1,0:T(8,128)(2,1)S(1)}, bf16[2,512,128]{2,1,0:T(8,128)(2,1)S(1)}, s32[16]{0:T(128)S(4)}, s32[16]{0:T(128)S(4)}) custom-call(s32[16]{0:T(128)} %rows_ref.1, s32[16]{0:T(128)} %cols_ref.1, s32[16,256]{1,0:T(8,128)} %marker_ref.1), custom_call_target="tpu_custom_call" | custom-call | flops 1000000 | bytes 2000000 | tf_op jit(solution)/shard_map/pallas_call | solution.py:173
  18.8 0.0 collective-permute-done.3.refs_3_
  18.8 2.2 %collective-permute-done.2.refs_2_ = f32[4,4,128]{2,1,0:T(4,128)S(1)} collective-permute-done((f32[4,4,128]{2,1,0:T(4,128)S(1)}, f32[4,4,128]{2,1,0:T(4,128)S(1)}, u32[]{:S(2)}, u32[]{:S(2)}) %collective-permute-start.2) | collective-permute-done | bytes 8224 | tf_op jit(solution)/shard_map/ppermute | solution.py:489
  21.0 0.0 collective-permute-done.1.refs_1_
  21.1 2.5 %collective-permute-start.4 = (f32[4,4,128]{2,1,0:T(4,128)S(1)}, f32[4,4,128]{2,1,0:T(4,128)S(1)}, u32[]{:S(2)}, u32[]{:S(2)}) collective-permute-start(f32[4,4,128]{2,1,0:T(4,128)S(1)} %shard_map.89.refs_0_), channel_id=1, source_target_pairs={{0,8},{1,9},{2,10},{3,11},{4,12},{5,13},{6,14},{7,15},{8,0},{9,1},... | collective-permute-start | bytes 24584 | tf_op jit(solution)/shard_map/ppermute | solution.py:489
  23.6 0.0 all-to-all-done.jones_ref
  23.6 8.7 %shard_map.87.terms_ref = f32[16,4,8,128]{3,2,1,0:T(8,128)S(1)} custom-call(s32[16]{0:T(128)S(4)} %get-tuple-element.19.rows_ref, s32[16]{0:T(128)S(4)} %get-tuple-element.20.cols_ref, f32[16,4,8,128]{3,2,1,0:T(8,128)S(1)} %all-to-all-done.jones_ref, bf16[16,8,32,256]{3,2,1,0:T(8,128)(2,1)} %bitcast.3, bf16[16,64,256]{2,1,0:T(8,128)(2,1)} %bitcast.5, ...), custom_call_target="tpu_custom_call" | custom-call | flops 40000000 | bytes 4000000 | tf_op jit(solution)/shard_map/pallas_call | solution.py:346
  32.3 0.0 collective-permute-done.4.refs_1_
  32.3 16.6 %all_to_all.25.refs_2_ = f32[16,4,8,128]{3,2,1,0:T(8,128)S(1)} all-to-all(f32[16,4,8,128]{3,2,1,0:T(8,128)S(1)} %get-tuple-element.26), channel_id=1, replica_groups=mesh['pair'=16,'chan'=16] {'pair'}, dimensions={0} | all-to-all | bytes 524288 | tf_op jit(solution)/shard_map/all_to_all | solution.py:517
  48.9 0.1 shard_map.91
  49.0 12.3 %all_to_all.26.jones_ref = f32[16,4,8,128]{3,2,1,0:T(8,128)S(1)} all-to-all(f32[16,4,8,128]{3,2,1,0:T(8,128)S(1)} %get-tuple-element.29), channel_id=1, replica_groups=mesh['pair'=16,'chan'=16] {'pair'}, dimensions={0} | all-to-all | bytes 524288 | tf_op jit(solution)/shard_map/all_to_all | solution.py:521
  61.4 8.7 %shard_map.92 = f32[16,4,8,128]{3,2,1,0:T(8,128)S(1)} custom-call(s32[16]{0:T(128)S(4)} %get-tuple-element.19.rows_ref, s32[16]{0:T(128)S(4)} %get-tuple-element.20.cols_ref, f32[16,4,8,128]{3,2,1,0:T(8,128)S(1)} %all_to_all.26.jones_ref, bf16[16,8,32,256]{3,2,1,0:T(8,128)(2,1)} %bitcast.4, bf16[16,64,256]{2,1,0:T(8,128)(2,1)} %bitcast.6, ...), custom_call_target="tpu_custom_call" | custom-call | flops 40000000 | bytes 4000000 | tf_op jit(solution)/shard_map/pallas_call | solution.py:346
  70.1 12.2 %all_to_all.27.refs_1_ = f32[16,4,8,128]{3,2,1,0:T(8,128)S(1)} all-to-all(f32[16,4,8,128]{3,2,1,0:T(8,128)S(1)} %shard_map.92), channel_id=1, replica_groups=mesh['pair'=16,'chan'=16] {'pair'}, dimensions={0} | all-to-all | bytes 524288 | tf_op jit(solution)/shard_map/all_to_all | solution.py:523
  82.3 0.1 shard_map.93
  82.4 19.2 %all_to_all.28.refs_3_ = f32[16,4,8,128]{3,2,1,0:T(8,128)S(1)} all-to-all(f32[16,4,8,128]{3,2,1,0:T(8,128)S(1)} %get-tuple-element.32), channel_id=1, replica_groups=mesh['pair'=16,'chan'=16] {'chan'}, dimensions={0} | all-to-all | bytes 524288 | tf_op jit(solution)/shard_map/all_to_all | solution.py:531
  101.6 0.9 shard_map.94
  (3 shorter events, 0.0 us)
Async XLA Ops:
  2.4 21.2 %all-to-all-start = ((f32[16,4,8,128]{3,2,1,0:T(8,128)}), f32[16,4,8,128]{3,2,1,0:T(8,128)S(1)}, u32[]{:S(2)}, u32[]{:S(2)}) async-start(f32[16,4,8,128]{3,2,1,0:T(8,128)} %get-tuple-element.21), calls=%async_computation | async-start | bytes 524288 | tf_op jit(solution)/shard_map/all_to_all | solution.py:510
  12.4 1.9 %collective-permute-start = (f32[4,4,128]{2,1,0:T(4,128)S(1)}, f32[4,4,128]{2,1,0:T(4,128)S(1)}, u32[]{:S(2)}, u32[]{:S(2)}) collective-permute-start(f32[4,4,128]{2,1,0:T(4,128)S(1)} %get-tuple-element.25.refs_0_), channel_id=1, source_target_pairs={{0,1},{1,0},{2,3},{3,2},{4,5},{5,4},{6,7},{7,6},{8,9},{9,8},{10,11... | collective-permute-start | bytes 24584 | tf_op jit(solution)/shard_map/ppermute | solution.py:489
  14.3 4.5 %collective-permute-start.3 = (f32[4,4,128]{2,1,0:T(4,128)S(1)}, f32[4,4,128]{2,1,0:T(4,128)S(1)}, u32[]{:S(2)}, u32[]{:S(2)}) collective-permute-start(f32[4,4,128]{2,1,0:T(4,128)S(1)} %shard_map.88.refs_0_), channel_id=1, source_target_pairs={{0,6},{1,7},{2,4},{3,5},{4,2},{5,3},{6,0},{7,1},{8,14},{9,15},{10,... | collective-permute-start | bytes 24584 | tf_op jit(solution)/shard_map/ppermute | solution.py:489
  17.0 4.0 %collective-permute-start.2 = (f32[4,4,128]{2,1,0:T(4,128)S(1)}, f32[4,4,128]{2,1,0:T(4,128)S(1)}, u32[]{:S(2)}, u32[]{:S(2)}) collective-permute-start(f32[4,4,128]{2,1,0:T(4,128)S(1)} %shard_map.88.refs_0_), channel_id=1, source_target_pairs={{0,4},{1,5},{2,6},{3,7},{4,0},{5,1},{6,2},{7,3},{8,12},{9,13},{10,... | collective-permute-start | bytes 24584 | tf_op jit(solution)/shard_map/ppermute | solution.py:489
  17.4 3.7 %collective-permute-start.1 = (f32[4,4,128]{2,1,0:T(4,128)S(1)}, f32[4,4,128]{2,1,0:T(4,128)S(1)}, u32[]{:S(2)}, u32[]{:S(2)}) collective-permute-start(f32[4,4,128]{2,1,0:T(4,128)S(1)} %shard_map.88.refs_0_), channel_id=1, source_target_pairs={{0,2},{1,3},{2,0},{3,1},{4,6},{5,7},{6,4},{7,5},{8,10},{9,11},{10,... | collective-permute-start | bytes 24584 | tf_op jit(solution)/shard_map/ppermute | solution.py:489
  21.1 11.2 %collective-permute-start.4 = (f32[4,4,128]{2,1,0:T(4,128)S(1)}, f32[4,4,128]{2,1,0:T(4,128)S(1)}, u32[]{:S(2)}, u32[]{:S(2)}) collective-permute-start(f32[4,4,128]{2,1,0:T(4,128)S(1)} %shard_map.89.refs_0_), channel_id=1, source_target_pairs={{0,8},{1,9},{2,10},{3,11},{4,12},{5,13},{6,14},{7,15},{8,0},{9,1},... | collective-permute-start | bytes 24584 | tf_op jit(solution)/shard_map/ppermute | solution.py:489

commit v7 on v6

--- a/solution.py
+++ b/solution.py
@@ -264,43 +264,47 @@
         b = jnp.maximum(cols_ref[t], 0)
         for copy in copies(t):
             copy.wait()
-        for half in range(2):
-            acc = []
-            for e in range(4):
-                both = seen_ref[
-                    t, 16 * e : 16 * e + 16, LANES * half : LANES * half + LANES
-                ].astype(jnp.float32)
-                acc.append((both[0:8], both[8:16]))
+
+        @pl.when(rows_ref[t] >= 0)
+        def _():
+            for half in range(2):
+                acc = []
+                for e in range(4):
+                    both = seen_ref[
+                        t, 16 * e : 16 * e + 16, LANES * half : LANES * half + LANES
+                    ].astype(jnp.float32)
+                    acc.append((both[0:8], both[8:16]))
+                for k in range(DIRS):
+                    left = mat_mul(expand(a, k, 1 + half), coher_of(t, k, half))
+                    for e, piece in enumerate(flat(left)):
+                        left_ref[half, k, e] = piece
+                    acc = mat_mul(left, expand(b, k, 0), acc, y_herm=True, minus=True)
+                keep = keep_ref[t, half]
+                acc = with_sums([(item[0] * keep, item[1] * keep) for item in acc])
+                for e, piece in enumerate(flat(acc)):
+                    res_ref[half, e] = piece
             for k in range(DIRS):
-                left = mat_mul(expand(a, k, 1 + half), coher_of(t, k, half))
-                for e, piece in enumerate(flat(left)):
-                    left_ref[half, k, e] = piece
-                acc = mat_mul(left, expand(b, k, 0), acc, y_herm=True, minus=True)
-            keep = keep_ref[t, half]
-            acc = with_sums([(item[0] * keep, item[1] * keep) for item in acc])
-            for e, piece in enumerate(flat(acc)):
-                res_ref[half, e] = piece
-        for k in range(DIRS):
-            right = with_sums(expand(b, k, 0))
-            cols = [None] * 4
-            for half in range(2):
-                res = [tuple(res_ref[half, 3 * e + n] for n in range(3)) for e in range(4)]
-                coher = coher_of(t, k, half)
-                turned = []
-                for i in range(2):
-                    for j in range(2):
-                        sums = conj_right(coher, right, (2 * i, 2 * i + 1), (2 * j, 2 * j + 1))
-                        turned.append(conj_right_value(sums))
-                for e in range(4):
-                    i, j = e // 2, e % 2
-                    item = conj_left(turned, res, (2 * j, 2 * j + 1), (2 * i, 2 * i + 1))
-                    put(row_ref.at[t, k, half], e, item)
-                left = pairs([left_ref[half, k, e] for e in range(8)])
-                for e in range(4):
-                    i, j = e // 2, e % 2
-                    cols[e] = conj_right(left, res, (j, 2 + j), (i, 2 + i), cols[e])
-                    if half == 1:
-                        col_ref[t, k, :, e * LANES : e * LANES + LANES] = merged(conj_right_value(cols[e]), 64)
+                right = with_sums(expand(b, k, 0))
+                cols = [None] * 4
+                for half in range(2):
+                    res = [tuple(res_ref[half, 3 * e + n] for n in range(3)) for e in range(4)]
+                    coher = coher_of(t, k, half)
+                    turned = []
+                    for i in range(2):
+                        for j in range(2):
+                            sums = conj_right(coher, right, (2 * i, 2 * i + 1), (2 * j, 2 * j + 1))
+                            turned.append(conj_right_value(sums))
+                    for e in range(4):
+                        i, j = e // 2, e % 2
+                        item = conj_left(turned, res, (2 * j, 2 * j + 1), (2 * i, 2 * i + 1))
+                        put(row_ref.at[t, k, half], e, item)
+                    left = pairs([left_ref[half, k, e] for e in range(8)])
+                    for e in range(4):
+                        i, j = e // 2, e % 2
+                        cols[e] = conj_right(left, res, (j, 2 + j), (i, 2 + i), cols[e])
+                        if half == 1:
+                            col_ref[t, k, :, e * LANES : e * LANES + LANES] = merged(conj_right_value(cols[e]), 64)
+
         return carry
 
     lax.fori_loop(0, slots, multiply, 0)
@@ -322,12 +326,13 @@
         for n in range(group):
             a = jnp.maximum(rows_ref[t0 + n], 0)
             b = jnp.maximum(cols_ref[t0 + n], 0)
+            live = rows_ref[t0 + n] >= 0
             for k in range(DIRS):
                 row = [rows[n, k, 0, c] + pltpu.roll(rows[n, k, 1, c], 8, 1) for c in range(2)]
                 row = row[0] + pltpu.roll(row[1], BLK, 1)
-                out_ref[a, k] = out_ref[a, k] + row
+                out_ref[a, k] = out_ref[a, k] + jnp.where(live, row, 0.0)
             for k in range(DIRS):
-                out_ref[b, k] = out_ref[b, k] + cols[n, k]
+                out_ref[b, k] = out_ref[b, k] + jnp.where(live, cols[n, k], 0.0)
         return carry
 
     lax.fori_loop(0, slots // group, settle, 0)

time: 103 us -> 101 us (0.981)
  Pallas kernels: 21.4 us -> 17.3 us
  blocking collectives: 60.4 us -> 62.9 us
    pallas_call x2, Pallas kernels: 17.4 us -> 13.3 us  [local_descent(): pl.pallas_call(descent_kernel, out_shape=jax.ShapeDtypeStruct((blocks, DI...]
    all_to_all x2, blocking collectives: 28.8 us -> 32.4 us  [local(): terms = lax.all_to_all(terms, 'pair', 0, 0)]
    all_to_all x1, blocking collectives: 19.2 us -> 18.1 us  [local(): sums = lax.all_to_all(sums, 'chan', 0, 0)]
  transfers between devices with their start and end apart: 6 -> 6, of which waited for: 2 -> 2; matrix products, arithmetic and copies ran while one was open for 0% -> 0% of each run, Pallas kernels for 10% -> 8%
where the time goes in v7:
time: 101 us
  blocking collectives  62.9 us (62%)
  Pallas kernels  17.3 us (17%)
  starting transfers between devices  17 us (17%)
  waiting for transfers between devices  3.07 us (3%)
    all_to_all x2, blocking collectives, local(): terms = lax.all_to_all(terms, 'pair', 0, 0)  32.4 us
    all_to_all x1, blocking collectives, local(): sums = lax.all_to_all(sums, 'chan', 0, 0)  18.1 us
    pallas_call x2, Pallas kernels, local_descent(): pl.pallas_call(descent_kernel, out_shape=jax.ShapeDtypeStruct((blocks, DI...  13.3 us
    all_to_all x1, blocking collectives, local(): full = lax.all_to_all(sent, 'pair', 0, 0)  12.3 us
    all_to_all x1, starting transfers between devices, local(): full = lax.all_to_all(sent, 'pair', 0, 0)  10 us
    ppermute x5, starting transfers between devices, flipped(): return lax.ppermute(array, 'chan', [(i, i ^ bits) for i in range(count)])  6.93 us
    ppermute x5, waiting for transfers between devices, flipped(): return lax.ppermute(array, 'chan', [(i, i ^ bits) for i in range(count)])  3.07 us
    pallas_call x4, Pallas kernels, small_call(): pl.pallas_call(body, out_shape=[jax.ShapeDtypeStruct(s, jnp.float32) for...  2.84 us
  transfers between devices with their start and end apart: 6, of which 2 were waited for; matrix products, arithmetic and copies ran while one was open for 0% of the time, Pallas kernels for 8%

profile of v7, /device:TPU:1, one launch (start us, length us, event | category | flops | bytes accessed | tf_op | source)
XLA Modules:
  0.0 100.9 jit_solution(4452834813674033151)
XLA Ops:
  0.6 1.7 %shard_map.85 = (f32[4,8,128]{2,1,0:T(8,128)S(1)}, f32[16,4,8,128]{3,2,1,0:T(8,128)}, f32[4,4,128]{2,1,0:T(4,128)S(1)}) custom-call(s32[1]{0:T(128)} %bitcast.refs_0_, f32[8,4,8,16]{3,2,1,0:T(8,128)} %refs_1_.1), custom_call_target="tpu_custom_call" | custom-call | tf_op jit(solution)/shard_map/pallas_call | solution.py:484
  2.4 10.0 %all-to-all-start = ((f32[16,4,8,128]{3,2,1,0:T(8,128)}), f32[16,4,8,128]{3,2,1,0:T(8,128)S(1)}, u32[]{:S(2)}, u32[]{:S(2)}) async-start(f32[16,4,8,128]{3,2,1,0:T(8,128)} %get-tuple-element.21), calls=%async_computation | async-start | bytes 524288 | tf_op jit(solution)/shard_map/all_to_all | solution.py:515
  12.4 1.0 %collective-permute-start = (f32[4,4,128]{2,1,0:T(4,128)S(1)}, f32[4,4,128]{2,1,0:T(4,128)S(1)}, u32[]{:S(2)}, u32[]{:S(2)}) collective-permute-start(f32[4,4,128]{2,1,0:T(4,128)S(1)} %get-tuple-element.25.refs_0_), channel_id=1, source_target_pairs={{0,1},{1,0},{2,3},{3,2},{4,5},{5,4},{6,7},{7,6},{8,9},{9,8},{10,11... | collective-permute-start | bytes 24584 | tf_op jit(solution)/shard_map/ppermute | solution.py:494
  13.5 0.8 collective-permute-done.refs_1_
  14.3 2.7 %collective-permute-start.3 = (f32[4,4,128]{2,1,0:T(4,128)S(1)}, f32[4,4,128]{2,1,0:T(4,128)S(1)}, u32[]{:S(2)}, u32[]{:S(2)}) collective-permute-start(f32[4,4,128]{2,1,0:T(4,128)S(1)} %shard_map.88.refs_0_), channel_id=1, source_target_pairs={{0,6},{1,7},{2,4},{3,5},{4,2},{5,3},{6,0},{7,1},{8,14},{9,15},{10,... | collective-permute-start | bytes 24584 | tf_op jit(solution)/shard_map/ppermute | solution.py:494
  17.0 0.3 collective-permute-start.2
  17.4 0.3 collective-permute-start.1
  17.7 1.1 %shard_map.86 = (f32[16,2,8,128]{3,2,1,0:T(8,128)S(1)}, bf16[256,3072]{1,0:T(8,128)(2,1)S(1)}, bf16[2,512,128]{2,1,0:T(8,128)(2,1)S(1)}, s32[16]{0:T(128)S(4)}, s32[16]{0:T(128)S(4)}) custom-call(s32[16]{0:T(128)} %rows_ref.1, s32[16]{0:T(128)} %cols_ref.1, s32[16,256]{1,0:T(8,128)} %marker_ref.1), custom_call_target="tpu_custom_call" | custom-call | flops 1000000 | bytes 2000000 | tf_op jit(solution)/shard_map/pallas_call | solution.py:173
  18.8 0.0 collective-permute-done.3.refs_3_
  18.8 2.2 %collective-permute-done.2.refs_2_ = f32[4,4,128]{2,1,0:T(4,128)S(1)} collective-permute-done((f32[4,4,128]{2,1,0:T(4,128)S(1)}, f32[4,4,128]{2,1,0:T(4,128)S(1)}, u32[]{:S(2)}, u32[]{:S(2)}) %collective-permute-start.2) | collective-permute-done | bytes 8224 | tf_op jit(solution)/shard_map/ppermute | solution.py:494
  21.0 0.0 collective-permute-done.1.refs_1_
  21.1 2.5 %collective-permute-start.4 = (f32[4,4,128]{2,1,0:T(4,128)S(1)}, f32[4,4,128]{2,1,0:T(4,128)S(1)}, u32[]{:S(2)}, u32[]{:S(2)}) collective-permute-start(f32[4,4,128]{2,1,0:T(4,128)S(1)} %shard_map.89.refs_0_), channel_id=1, source_target_pairs={{0,8},{1,9},{2,10},{3,11},{4,12},{5,13},{6,14},{7,15},{8,0},{9,1},... | collective-permute-start | bytes 24584 | tf_op jit(solution)/shard_map/ppermute | solution.py:494
  23.6 0.0 all-to-all-done.jones_ref
  23.6 6.6 %shard_map.87.terms_ref = f32[16,4,8,128]{3,2,1,0:T(8,128)S(1)} custom-call(s32[16]{0:T(128)S(4)} %get-tuple-element.19.rows_ref, s32[16]{0:T(128)S(4)} %get-tuple-element.20.cols_ref, f32[16,4,8,128]{3,2,1,0:T(8,128)S(1)} %all-to-all-done.jones_ref, bf16[16,8,32,256]{3,2,1,0:T(8,128)(2,1)} %bitcast.3, bf16[16,64,256]{2,1,0:T(8,128)(2,1)} %bitcast.5, ...), custom_call_target="tpu_custom_call" | custom-call | flops 40000000 | bytes 4000000 | tf_op jit(solution)/shard_map/pallas_call | solution.py:351
  30.2 0.0 collective-permute-done.4.refs_1_
  30.3 18.5 %all_to_all.25.refs_2_ = f32[16,4,8,128]{3,2,1,0:T(8,128)S(1)} all-to-all(f32[16,4,8,128]{3,2,1,0:T(8,128)S(1)} %get-tuple-element.26), channel_id=1, replica_groups=mesh['pair'=16,'chan'=16] {'pair'}, dimensions={0} | all-to-all | bytes 524288 | tf_op jit(solution)/shard_map/all_to_all | solution.py:522
  48.7 0.1 shard_map.91
  48.8 12.3 %all_to_all.26.jones_ref = f32[16,4,8,128]{3,2,1,0:T(8,128)S(1)} all-to-all(f32[16,4,8,128]{3,2,1,0:T(8,128)S(1)} %get-tuple-element.29), channel_id=1, replica_groups=mesh['pair'=16,'chan'=16] {'pair'}, dimensions={0} | all-to-all | bytes 524288 | tf_op jit(solution)/shard_map/all_to_all | solution.py:526
  61.2 6.6 %shard_map.92 = f32[16,4,8,128]{3,2,1,0:T(8,128)S(1)} custom-call(s32[16]{0:T(128)S(4)} %get-tuple-element.19.rows_ref, s32[16]{0:T(128)S(4)} %get-tuple-element.20.cols_ref, f32[16,4,8,128]{3,2,1,0:T(8,128)S(1)} %all_to_all.26.jones_ref, bf16[16,8,32,256]{3,2,1,0:T(8,128)(2,1)} %bitcast.4, bf16[16,64,256]{2,1,0:T(8,128)(2,1)} %bitcast.6, ...), custom_call_target="tpu_custom_call" | custom-call | flops 40000000 | bytes 4000000 | tf_op jit(solution)/shard_map/pallas_call | solution.py:351
  67.8 13.9 %all_to_all.27.refs_1_ = f32[16,4,8,128]{3,2,1,0:T(8,128)S(1)} all-to-all(f32[16,4,8,128]{3,2,1,0:T(8,128)S(1)} %shard_map.92), channel_id=1, replica_groups=mesh['pair'=16,'chan'=16] {'pair'}, dimensions={0} | all-to-all | bytes 524288 | tf_op jit(solution)/shard_map/all_to_all | solution.py:528
  81.8 0.1 shard_map.93
  81.9 18.1 %all_to_all.28.refs_3_ = f32[16,4,8,128]{3,2,1,0:T(8,128)S(1)} all-to-all(f32[16,4,8,128]{3,2,1,0:T(8,128)S(1)} %get-tuple-element.32), channel_id=1, replica_groups=mesh['pair'=16,'chan'=16] {'chan'}, dimensions={0} | all-to-all | bytes 524288 | tf_op jit(solution)/shard_map/all_to_all | solution.py:536
  100.0 0.9 shard_map.94
  (3 shorter events, 0.0 us)
Async XLA Ops:
  2.4 21.2 %all-to-all-start = ((f32[16,4,8,128]{3,2,1,0:T(8,128)}), f32[16,4,8,128]{3,2,1,0:T(8,128)S(1)}, u32[]{:S(2)}, u32[]{:S(2)}) async-start(f32[16,4,8,128]{3,2,1,0:T(8,128)} %get-tuple-element.21), calls=%async_computation | async-start | bytes 524288 | tf_op jit(solution)/shard_map/all_to_all | solution.py:515
  12.4 1.9 %collective-permute-start = (f32[4,4,128]{2,1,0:T(4,128)S(1)}, f32[4,4,128]{2,1,0:T(4,128)S(1)}, u32[]{:S(2)}, u32[]{:S(2)}) collective-permute-start(f32[4,4,128]{2,1,0:T(4,128)S(1)} %get-tuple-element.25.refs_0_), channel_id=1, source_target_pairs={{0,1},{1,0},{2,3},{3,2},{4,5},{5,4},{6,7},{7,6},{8,9},{9,8},{10,11... | collective-permute-start | bytes 24584 | tf_op jit(solution)/shard_map/ppermute | solution.py:494
  14.3 4.5 %collective-permute-start.3 = (f32[4,4,128]{2,1,0:T(4,128)S(1)}, f32[4,4,128]{2,1,0:T(4,128)S(1)}, u32[]{:S(2)}, u32[]{:S(2)}) collective-permute-start(f32[4,4,128]{2,1,0:T(4,128)S(1)} %shard_map.88.refs_0_), channel_id=1, source_target_pairs={{0,6},{1,7},{2,4},{3,5},{4,2},{5,3},{6,0},{7,1},{8,14},{9,15},{10,... | collective-permute-start | bytes 24584 | tf_op jit(solution)/shard_map/ppermute | solution.py:494
  17.0 4.0 %collective-permute-start.2 = (f32[4,4,128]{2,1,0:T(4,128)S(1)}, f32[4,4,128]{2,1,0:T(4,128)S(1)}, u32[]{:S(2)}, u32[]{:S(2)}) collective-permute-start(f32[4,4,128]{2,1,0:T(4,128)S(1)} %shard_map.88.refs_0_), channel_id=1, source_target_pairs={{0,4},{1,5},{2,6},{3,7},{4,0},{5,1},{6,2},{7,3},{8,12},{9,13},{10,... | collective-permute-start | bytes 24584 | tf_op jit(solution)/shard_map/ppermute | solution.py:494
  17.4 3.7 %collective-permute-start.1 = (f32[4,4,128]{2,1,0:T(4,128)S(1)}, f32[4,4,128]{2,1,0:T(4,128)S(1)}, u32[]{:S(2)}, u32[]{:S(2)}) collective-permute-start(f32[4,4,128]{2,1,0:T(4,128)S(1)} %shard_map.88.refs_0_), channel_id=1, source_target_pairs={{0,2},{1,3},{2,0},{3,1},{4,6},{5,7},{6,4},{7,5},{8,10},{9,11},{10,... | collective-permute-start | bytes 24584 | tf_op jit(solution)/shard_map/ppermute | solution.py:494
  21.1 9.2 %collective-permute-start.4 = (f32[4,4,128]{2,1,0:T(4,128)S(1)}, f32[4,4,128]{2,1,0:T(4,128)S(1)}, u32[]{:S(2)}, u32[]{:S(2)}) collective-permute-start(f32[4,4,128]{2,1,0:T(4,128)S(1)} %shard_map.89.refs_0_), channel_id=1, source_target_pairs={{0,8},{1,9},{2,10},{3,11},{4,12},{5,13},{6,14},{7,15},{8,0},{9,1},... | collective-permute-start | bytes 24584 | tf_op jit(solution)/shard_map/ppermute | solution.py:494

commit v8 on v7

--- a/solution.py
+++ b/solution.py
@@ -267,6 +267,7 @@
 
         @pl.when(rows_ref[t] >= 0)
         def _():
+            accs = []
             for half in range(2):
                 acc = []
                 for e in range(4):
@@ -274,13 +275,17 @@
                         t, 16 * e : 16 * e + 16, LANES * half : LANES * half + LANES
                     ].astype(jnp.float32)
                     acc.append((both[0:8], both[8:16]))
-                for k in range(DIRS):
+                accs.append(acc)
+            for k in range(DIRS):
+                right = expand(b, k, 0)
+                for half in range(2):
                     left = mat_mul(expand(a, k, 1 + half), coher_of(t, k, half))
                     for e, piece in enumerate(flat(left)):
                         left_ref[half, k, e] = piece
-                    acc = mat_mul(left, expand(b, k, 0), acc, y_herm=True, minus=True)
+                    accs[half] = mat_mul(left, right, accs[half], y_herm=True, minus=True)
+            for half in range(2):
                 keep = keep_ref[t, half]
-                acc = with_sums([(item[0] * keep, item[1] * keep) for item in acc])
+                acc = with_sums([(item[0] * keep, item[1] * keep) for item in accs[half]])
                 for e, piece in enumerate(flat(acc)):
                     res_ref[half, e] = piece
             for k in range(DIRS):

time: 101 us -> 101 us (level)
  blocking collectives: 62.9 us -> 68.1 us
  Pallas kernels: 17.3 us -> 12.6 us
    pallas_call x2, Pallas kernels: 13.3 us -> 8.61 us  [local_descent(): pl.pallas_call(descent_kernel, out_shape=jax.ShapeDtypeStruct((blocks, DI...]
    all_to_all x2, blocking collectives: 32.4 us -> 36.4 us  [local(): terms = lax.all_to_all(terms, 'pair', 0, 0)]
    all_to_all x1, blocking collectives: 18.1 us -> 19.3 us  [local(): sums = lax.all_to_all(sums, 'chan', 0, 0)]
  transfers between devices with their start and end apart: 6 -> 6, of which waited for: 2 -> 2; matrix products, arithmetic and copies ran while one was open for 0% -> 0% of each run, Pallas kernels for 8% -> 5%
where the time goes in v8:
time: 101 us
  blocking collectives  68.1 us (67%)
  starting transfers between devices  17 us (17%)
  Pallas kernels  12.6 us (12%)
  waiting for transfers between devices  3.07 us (3%)
    all_to_all x2, blocking collectives, local(): terms = lax.all_to_all(terms, 'pair', 0, 0)  36.4 us
    all_to_all x1, blocking collectives, local(): sums = lax.all_to_all(sums, 'chan', 0, 0)  19.3 us
    all_to_all x1, blocking collectives, local(): full = lax.all_to_all(sent, 'pair', 0, 0)  12.3 us
    all_to_all x1, starting transfers between devices, local(): full = lax.all_to_all(sent, 'pair', 0, 0)  10 us
    pallas_call x2, Pallas kernels, local_descent(): pl.pallas_call(descent_kernel, out_shape=jax.ShapeDtypeStruct((blocks, DI...  8.61 us
    ppermute x5, starting transfers between devices, flipped(): return lax.ppermute(array, 'chan', [(i, i ^ bits) for i in range(count)])  6.93 us
    ppermute x5, waiting for transfers between devices, flipped(): return lax.ppermute(array, 'chan', [(i, i ^ bits) for i in range(count)])  3.07 us
    pallas_call x4, Pallas kernels, small_call(): pl.pallas_call(body, out_shape=[jax.ShapeDtypeStruct(s, jnp.float32) for...  2.84 us
  transfers between devices with their start and end apart: 6, of which 2 were waited for; matrix products, arithmetic and copies ran while one was open for 0% of the time, Pallas kernels for 5%

profile of v8, /device:TPU:1, one launch (start us, length us, event | category | flops | bytes accessed | tf_op | source)
XLA Modules:
  0.0 101.5 jit_solution(5575201959279238217)
XLA Ops:
  0.6 1.7 %shard_map.85 = (f32[4,8,128]{2,1,0:T(8,128)S(1)}, f32[16,4,8,128]{3,2,1,0:T(8,128)}, f32[4,4,128]{2,1,0:T(4,128)S(1)}) custom-call(s32[1]{0:T(128)} %bitcast.refs_0_, f32[8,4,8,16]{3,2,1,0:T(8,128)} %refs_1_.1), custom_call_target="tpu_custom_call" | custom-call | tf_op jit(solution)/shard_map/pallas_call | solution.py:489
  2.4 10.0 %all-to-all-start = ((f32[16,4,8,128]{3,2,1,0:T(8,128)}), f32[16,4,8,128]{3,2,1,0:T(8,128)S(1)}, u32[]{:S(2)}, u32[]{:S(2)}) async-start(f32[16,4,8,128]{3,2,1,0:T(8,128)} %get-tuple-element.21), calls=%async_computation | async-start | bytes 524288 | tf_op jit(solution)/shard_map/all_to_all | solution.py:520
  12.4 1.0 %collective-permute-start = (f32[4,4,128]{2,1,0:T(4,128)S(1)}, f32[4,4,128]{2,1,0:T(4,128)S(1)}, u32[]{:S(2)}, u32[]{:S(2)}) collective-permute-start(f32[4,4,128]{2,1,0:T(4,128)S(1)} %get-tuple-element.25.refs_0_), channel_id=1, source_target_pairs={{0,1},{1,0},{2,3},{3,2},{4,5},{5,4},{6,7},{7,6},{8,9},{9,8},{10,11... | collective-permute-start | bytes 24584 | tf_op jit(solution)/shard_map/ppermute | solution.py:499
  13.5 0.8 collective-permute-done.refs_1_
  14.3 2.7 %collective-permute-start.3 = (f32[4,4,128]{2,1,0:T(4,128)S(1)}, f32[4,4,128]{2,1,0:T(4,128)S(1)}, u32[]{:S(2)}, u32[]{:S(2)}) collective-permute-start(f32[4,4,128]{2,1,0:T(4,128)S(1)} %shard_map.88.refs_0_), channel_id=1, source_target_pairs={{0,6},{1,7},{2,4},{3,5},{4,2},{5,3},{6,0},{7,1},{8,14},{9,15},{10,... | collective-permute-start | bytes 24584 | tf_op jit(solution)/shard_map/ppermute | solution.py:499
  17.0 0.3 collective-permute-start.2
  17.4 0.3 collective-permute-start.1
  17.7 1.1 %shard_map.86 = (f32[16,2,8,128]{3,2,1,0:T(8,128)S(1)}, bf16[256,3072]{1,0:T(8,128)(2,1)S(1)}, bf16[2,512,128]{2,1,0:T(8,128)(2,1)S(1)}, s32[16]{0:T(128)S(4)}, s32[16]{0:T(128)S(4)}) custom-call(s32[16]{0:T(128)} %rows_ref.1, s32[16]{0:T(128)} %cols_ref.1, s32[16,256]{1,0:T(8,128)} %marker_ref.1), custom_call_target="tpu_custom_call" | custom-call | flops 1000000 | bytes 2000000 | tf_op jit(solution)/shard_map/pallas_call | solution.py:173
  18.8 0.0 collective-permute-done.3.refs_3_
  18.8 2.2 %collective-permute-done.2.refs_2_ = f32[4,4,128]{2,1,0:T(4,128)S(1)} collective-permute-done((f32[4,4,128]{2,1,0:T(4,128)S(1)}, f32[4,4,128]{2,1,0:T(4,128)S(1)}, u32[]{:S(2)}, u32[]{:S(2)}) %collective-permute-start.2) | collective-permute-done | bytes 8224 | tf_op jit(solution)/shard_map/ppermute | solution.py:499
  21.0 0.0 collective-permute-done.1.refs_1_
  21.1 2.5 %collective-permute-start.4 = (f32[4,4,128]{2,1,0:T(4,128)S(1)}, f32[4,4,128]{2,1,0:T(4,128)S(1)}, u32[]{:S(2)}, u32[]{:S(2)}) collective-permute-start(f32[4,4,128]{2,1,0:T(4,128)S(1)} %shard_map.89.refs_0_), channel_id=1, source_target_pairs={{0,8},{1,9},{2,10},{3,11},{4,12},{5,13},{6,14},{7,15},{8,0},{9,1},... | collective-permute-start | bytes 24584 | tf_op jit(solution)/shard_map/ppermute | solution.py:499
  23.6 0.0 all-to-all-done.jones_ref
  23.6 4.3 %shard_map.87.terms_ref = f32[16,4,8,128]{3,2,1,0:T(8,128)S(1)} custom-call(s32[16]{0:T(128)S(4)} %get-tuple-element.19.rows_ref, s32[16]{0:T(128)S(4)} %get-tuple-element.20.cols_ref, f32[16,4,8,128]{3,2,1,0:T(8,128)S(1)} %all-to-all-done.jones_ref, bf16[16,8,32,256]{3,2,1,0:T(8,128)(2,1)} %bitcast.3, bf16[16,64,256]{2,1,0:T(8,128)(2,1)} %bitcast.5, ...), custom_call_target="tpu_custom_call" | custom-call | flops 40000000 | bytes 4000000 | tf_op jit(solution)/shard_map/pallas_call | solution.py:356
  27.9 0.0 collective-permute-done.4.refs_1_
  27.9 20.2 %all_to_all.25.refs_2_ = f32[16,4,8,128]{3,2,1,0:T(8,128)S(1)} all-to-all(f32[16,4,8,128]{3,2,1,0:T(8,128)S(1)} %get-tuple-element.26), channel_id=1, replica_groups=mesh['pair'=16,'chan'=16] {'pair'}, dimensions={0} | all-to-all | bytes 524288 | tf_op jit(solution)/shard_map/all_to_all | solution.py:527
  48.1 0.1 shard_map.91
  48.2 12.3 %all_to_all.26.jones_ref = f32[16,4,8,128]{3,2,1,0:T(8,128)S(1)} all-to-all(f32[16,4,8,128]{3,2,1,0:T(8,128)S(1)} %get-tuple-element.29), channel_id=1, replica_groups=mesh['pair'=16,'chan'=16] {'pair'}, dimensions={0} | all-to-all | bytes 524288 | tf_op jit(solution)/shard_map/all_to_all | solution.py:531
  60.6 4.3 %shard_map.92 = f32[16,4,8,128]{3,2,1,0:T(8,128)S(1)} custom-call(s32[16]{0:T(128)S(4)} %get-tuple-element.19.rows_ref, s32[16]{0:T(128)S(4)} %get-tuple-element.20.cols_ref, f32[16,4,8,128]{3,2,1,0:T(8,128)S(1)} %all_to_all.26.jones_ref, bf16[16,8,32,256]{3,2,1,0:T(8,128)(2,1)} %bitcast.4, bf16[16,64,256]{2,1,0:T(8,128)(2,1)} %bitcast.6, ...), custom_call_target="tpu_custom_call" | custom-call | flops 40000000 | bytes 4000000 | tf_op jit(solution)/shard_map/pallas_call | solution.py:356
  64.9 16.2 %all_to_all.27.refs_1_ = f32[16,4,8,128]{3,2,1,0:T(8,128)S(1)} all-to-all(f32[16,4,8,128]{3,2,1,0:T(8,128)S(1)} %shard_map.92), channel_id=1, replica_groups=mesh['pair'=16,'chan'=16] {'pair'}, dimensions={0} | all-to-all | bytes 524288 | tf_op jit(solution)/shard_map/all_to_all | solution.py:533
  81.1 0.1 shard_map.93
  81.2 19.3 %all_to_all.28.refs_3_ = f32[16,4,8,128]{3,2,1,0:T(8,128)S(1)} all-to-all(f32[16,4,8,128]{3,2,1,0:T(8,128)S(1)} %get-tuple-element.32), channel_id=1, replica_groups=mesh['pair'=16,'chan'=16] {'chan'}, dimensions={0} | all-to-all | bytes 524288 | tf_op jit(solution)/shard_map/all_to_all | solution.py:541
  100.6 0.9 shard_map.94
  (3 shorter events, 0.0 us)
Async XLA Ops:
  2.4 21.2 %all-to-all-start = ((f32[16,4,8,128]{3,2,1,0:T(8,128)}), f32[16,4,8,128]{3,2,1,0:T(8,128)S(1)}, u32[]{:S(2)}, u32[]{:S(2)}) async-start(f32[16,4,8,128]{3,2,1,0:T(8,128)} %get-tuple-element.21), calls=%async_computation | async-start | bytes 524288 | tf_op jit(solution)/shard_map/all_to_all | solution.py:520
  12.4 1.9 %collective-permute-start = (f32[4,4,128]{2,1,0:T(4,128)S(1)}, f32[4,4,128]{2,1,0:T(4,128)S(1)}, u32[]{:S(2)}, u32[]{:S(2)}) collective-permute-start(f32[4,4,128]{2,1,0:T(4,128)S(1)} %get-tuple-element.25.refs_0_), channel_id=1, source_target_pairs={{0,1},{1,0},{2,3},{3,2},{4,5},{5,4},{6,7},{7,6},{8,9},{9,8},{10,11... | collective-permute-start | bytes 24584 | tf_op jit(solution)/shard_map/ppermute | solution.py:499
  14.3 4.5 %collective-permute-start.3 = (f32[4,4,128]{2,1,0:T(4,128)S(1)}, f32[4,4,128]{2,1,0:T(4,128)S(1)}, u32[]{:S(2)}, u32[]{:S(2)}) collective-permute-start(f32[4,4,128]{2,1,0:T(4,128)S(1)} %shard_map.88.refs_0_), channel_id=1, source_target_pairs={{0,6},{1,7},{2,4},{3,5},{4,2},{5,3},{6,0},{7,1},{8,14},{9,15},{10,... | collective-permute-start | bytes 24584 | tf_op jit(solution)/shard_map/ppermute | solution.py:499
  17.0 4.0 %collective-permute-start.2 = (f32[4,4,128]{2,1,0:T(4,128)S(1)}, f32[4,4,128]{2,1,0:T(4,128)S(1)}, u32[]{:S(2)}, u32[]{:S(2)}) collective-permute-start(f32[4,4,128]{2,1,0:T(4,128)S(1)} %shard_map.88.refs_0_), channel_id=1, source_target_pairs={{0,4},{1,5},{2,6},{3,7},{4,0},{5,1},{6,2},{7,3},{8,12},{9,13},{10,... | collective-permute-start | bytes 24584 | tf_op jit(solution)/shard_map/ppermute | solution.py:499
  17.4 3.7 %collective-permute-start.1 = (f32[4,4,128]{2,1,0:T(4,128)S(1)}, f32[4,4,128]{2,1,0:T(4,128)S(1)}, u32[]{:S(2)}, u32[]{:S(2)}) collective-permute-start(f32[4,4,128]{2,1,0:T(4,128)S(1)} %shard_map.88.refs_0_), channel_id=1, source_target_pairs={{0,2},{1,3},{2,0},{3,1},{4,6},{5,7},{6,4},{7,5},{8,10},{9,11},{10,... | collective-permute-start | bytes 24584 | tf_op jit(solution)/shard_map/ppermute | solution.py:499
  21.1 6.9 %collective-permute-start.4 = (f32[4,4,128]{2,1,0:T(4,128)S(1)}, f32[4,4,128]{2,1,0:T(4,128)S(1)}, u32[]{:S(2)}, u32[]{:S(2)}) collective-permute-start(f32[4,4,128]{2,1,0:T(4,128)S(1)} %shard_map.89.refs_0_), channel_id=1, source_target_pairs={{0,8},{1,9},{2,10},{3,11},{4,12},{5,13},{6,14},{7,15},{8,0},{9,1},... | collective-permute-start | bytes 24584 | tf_op jit(solution)/shard_map/ppermute | solution.py:499

commit v9 on v8

--- a/solution.py
+++ b/solution.py
@@ -464,6 +464,7 @@
 
 def finish_kernel(total, chan_ref, jones_ref, descent_ref, sums_ref, sol_ref, du_ref, co_ref):
     basis = basis_rows(chan_ref[0], total)
+    held = []
     for k in range(DIRS):
         both = descent_sum(sums_ref, k)
         coeffs = both[0:NP]
@@ -476,7 +477,13 @@
             part = slice(e * BLK, e * BLK + BLK)
             sol_ref[e, k] = now[:, part]
             du_ref[e, k] = dual[:, part]
-            co_ref[e, k] = coeffs[:, part]
+        held.append(coeffs)
+    for k in range(0, DIRS, 2):
+        two = jnp.concatenate(held[k : k + 2], axis=0)
+        for e in range(8):
+            part = two[:, e * BLK : e * BLK + BLK]
+            co_ref[e, k] = part[0:NP]
+            co_ref[e, k + 1] = part[NP : 2 * NP]
 
 
 def small_call(kernel, total, chan, arrays, shapes):

time: 101 us -> 102 us (level); the launches traced: 101 us -> 101 us
    all_to_all x1, blocking collectives: 19.3 us -> 18.1 us  [local(): sums = lax.all_to_all(sums, 'chan', 0, 0)]
where the time goes in v9:
time: 102 us; the launch traced here: 101 us
  blocking collectives  67.5 us (66%)
  starting transfers between devices  17 us (17%)
  Pallas kernels  12.6 us (12%)
  waiting for transfers between devices  3.07 us (3%)
    all_to_all x2, blocking collectives, local(): terms = lax.all_to_all(terms, 'pair', 0, 0)  37 us
    all_to_all x1, blocking collectives, local(): sums = lax.all_to_all(sums, 'chan', 0, 0)  18.1 us
    all_to_all x1, blocking collectives, local(): full = lax.all_to_all(sent, 'pair', 0, 0)  12.3 us
    all_to_all x1, starting transfers between devices, local(): full = lax.all_to_all(sent, 'pair', 0, 0)  10 us
    pallas_call x2, Pallas kernels, local_descent(): pl.pallas_call(descent_kernel, out_shape=jax.ShapeDtypeStruct((blocks, DI...  8.61 us
    ppermute x5, starting transfers between devices, flipped(): return lax.ppermute(array, 'chan', [(i, i ^ bits) for i in range(count)])  6.93 us
    ppermute x5, waiting for transfers between devices, flipped(): return lax.ppermute(array, 'chan', [(i, i ^ bits) for i in range(count)])  3.07 us
    pallas_call x4, Pallas kernels, small_call(): pl.pallas_call(body, out_shape=[jax.ShapeDtypeStruct(s, jnp.float32) for...  2.83 us
  transfers between devices with their start and end apart: 6, of which 2 were waited for; matrix products, arithmetic and copies ran while one was open for 0% of the time, Pallas kernels for 5%

profile of v9, /device:TPU:1, one launch (start us, length us, event | category | flops | bytes accessed | tf_op | source)
XLA Modules:
  0.0 100.9 jit_solution(3573992291671785288)
XLA Ops:
  0.6 1.7 %shard_map.85 = (f32[4,8,128]{2,1,0:T(8,128)S(1)}, f32[16,4,8,128]{3,2,1,0:T(8,128)}, f32[4,4,128]{2,1,0:T(4,128)S(1)}) custom-call(s32[1]{0:T(128)} %bitcast.refs_0_, f32[8,4,8,16]{3,2,1,0:T(8,128)} %refs_1_.1), custom_call_target="tpu_custom_call" | custom-call | tf_op jit(solution)/shard_map/pallas_call | solution.py:496
  2.4 10.0 %all-to-all-start = ((f32[16,4,8,128]{3,2,1,0:T(8,128)}), f32[16,4,8,128]{3,2,1,0:T(8,128)S(1)}, u32[]{:S(2)}, u32[]{:S(2)}) async-start(f32[16,4,8,128]{3,2,1,0:T(8,128)} %get-tuple-element.21), calls=%async_computation | async-start | bytes 524288 | tf_op jit(solution)/shard_map/all_to_all | solution.py:527
  12.4 1.0 %collective-permute-start = (f32[4,4,128]{2,1,0:T(4,128)S(1)}, f32[4,4,128]{2,1,0:T(4,128)S(1)}, u32[]{:S(2)}, u32[]{:S(2)}) collective-permute-start(f32[4,4,128]{2,1,0:T(4,128)S(1)} %get-tuple-element.25.refs_0_), channel_id=1, source_target_pairs={{0,1},{1,0},{2,3},{3,2},{4,5},{5,4},{6,7},{7,6},{8,9},{9,8},{10,11... | collective-permute-start | bytes 24584 | tf_op jit(solution)/shard_map/ppermute | solution.py:506
  13.5 0.8 collective-permute-done.refs_1_
  14.3 2.7 %collective-permute-start.3 = (f32[4,4,128]{2,1,0:T(4,128)S(1)}, f32[4,4,128]{2,1,0:T(4,128)S(1)}, u32[]{:S(2)}, u32[]{:S(2)}) collective-permute-start(f32[4,4,128]{2,1,0:T(4,128)S(1)} %shard_map.88.refs_0_), channel_id=1, source_target_pairs={{0,6},{1,7},{2,4},{3,5},{4,2},{5,3},{6,0},{7,1},{8,14},{9,15},{10,... | collective-permute-start | bytes 24584 | tf_op jit(solution)/shard_map/ppermute | solution.py:506
  17.0 0.3 collective-permute-start.2
  17.4 0.3 collective-permute-start.1
  17.7 1.1 %shard_map.86 = (f32[16,2,8,128]{3,2,1,0:T(8,128)S(1)}, bf16[256,3072]{1,0:T(8,128)(2,1)S(1)}, bf16[2,512,128]{2,1,0:T(8,128)(2,1)S(1)}, s32[16]{0:T(128)S(4)}, s32[16]{0:T(128)S(4)}) custom-call(s32[16]{0:T(128)} %rows_ref.1, s32[16]{0:T(128)} %cols_ref.1, s32[16,256]{1,0:T(8,128)} %marker_ref.1), custom_call_target="tpu_custom_call" | custom-call | flops 1000000 | bytes 2000000 | tf_op jit(solution)/shard_map/pallas_call | solution.py:173
  18.8 0.0 collective-permute-done.3.refs_3_
  18.8 2.2 %collective-permute-done.2.refs_2_ = f32[4,4,128]{2,1,0:T(4,128)S(1)} collective-permute-done((f32[4,4,128]{2,1,0:T(4,128)S(1)}, f32[4,4,128]{2,1,0:T(4,128)S(1)}, u32[]{:S(2)}, u32[]{:S(2)}) %collective-permute-start.2) | collective-permute-done | bytes 8224 | tf_op jit(solution)/shard_map/ppermute | solution.py:506
  21.0 0.0 collective-permute-done.1.refs_1_
  21.1 2.5 %collective-permute-start.4 = (f32[4,4,128]{2,1,0:T(4,128)S(1)}, f32[4,4,128]{2,1,0:T(4,128)S(1)}, u32[]{:S(2)}, u32[]{:S(2)}) collective-permute-start(f32[4,4,128]{2,1,0:T(4,128)S(1)} %shard_map.89.refs_0_), channel_id=1, source_target_pairs={{0,8},{1,9},{2,10},{3,11},{4,12},{5,13},{6,14},{7,15},{8,0},{9,1},... | collective-permute-start | bytes 24584 | tf_op jit(solution)/shard_map/ppermute | solution.py:506
  23.6 0.0 all-to-all-done.jones_ref
  23.6 4.3 %shard_map.87.terms_ref = f32[16,4,8,128]{3,2,1,0:T(8,128)S(1)} custom-call(s32[16]{0:T(128)S(4)} %get-tuple-element.19.rows_ref, s32[16]{0:T(128)S(4)} %get-tuple-element.20.cols_ref, f32[16,4,8,128]{3,2,1,0:T(8,128)S(1)} %all-to-all-done.jones_ref, bf16[16,8,32,256]{3,2,1,0:T(8,128)(2,1)} %bitcast.3, bf16[16,64,256]{2,1,0:T(8,128)(2,1)} %bitcast.5, ...), custom_call_target="tpu_custom_call" | custom-call | flops 40000000 | bytes 4000000 | tf_op jit(solution)/shard_map/pallas_call | solution.py:356
  27.9 0.0 collective-permute-done.4.refs_1_
  27.9 20.8 %all_to_all.25.refs_2_ = f32[16,4,8,128]{3,2,1,0:T(8,128)S(1)} all-to-all(f32[16,4,8,128]{3,2,1,0:T(8,128)S(1)} %get-tuple-element.26), channel_id=1, replica_groups=mesh['pair'=16,'chan'=16] {'pair'}, dimensions={0} | all-to-all | bytes 524288 | tf_op jit(solution)/shard_map/all_to_all | solution.py:534
  48.7 0.1 shard_map.91
  48.8 12.3 %all_to_all.26.jones_ref = f32[16,4,8,128]{3,2,1,0:T(8,128)S(1)} all-to-all(f32[16,4,8,128]{3,2,1,0:T(8,128)S(1)} %get-tuple-element.29), channel_id=1, replica_groups=mesh['pair'=16,'chan'=16] {'pair'}, dimensions={0} | all-to-all | bytes 524288 | tf_op jit(solution)/shard_map/all_to_all | solution.py:538
  61.2 4.3 %shard_map.92 = f32[16,4,8,128]{3,2,1,0:T(8,128)S(1)} custom-call(s32[16]{0:T(128)S(4)} %get-tuple-element.19.rows_ref, s32[16]{0:T(128)S(4)} %get-tuple-element.20.cols_ref, f32[16,4,8,128]{3,2,1,0:T(8,128)S(1)} %all_to_all.26.jones_ref, bf16[16,8,32,256]{3,2,1,0:T(8,128)(2,1)} %bitcast.4, bf16[16,64,256]{2,1,0:T(8,128)(2,1)} %bitcast.6, ...), custom_call_target="tpu_custom_call" | custom-call | flops 40000000 | bytes 4000000 | tf_op jit(solution)/shard_map/pallas_call | solution.py:356
  65.5 16.3 %all_to_all.27.refs_1_ = f32[16,4,8,128]{3,2,1,0:T(8,128)S(1)} all-to-all(f32[16,4,8,128]{3,2,1,0:T(8,128)S(1)} %shard_map.92), channel_id=1, replica_groups=mesh['pair'=16,'chan'=16] {'pair'}, dimensions={0} | all-to-all | bytes 524288 | tf_op jit(solution)/shard_map/all_to_all | solution.py:540
  81.7 0.1 shard_map.93
  81.8 18.1 %all_to_all.28.refs_3_ = f32[16,4,8,128]{3,2,1,0:T(8,128)S(1)} all-to-all(f32[16,4,8,128]{3,2,1,0:T(8,128)S(1)} %get-tuple-element.32), channel_id=1, replica_groups=mesh['pair'=16,'chan'=16] {'chan'}, dimensions={0} | all-to-all | bytes 524288 | tf_op jit(solution)/shard_map/all_to_all | solution.py:548
  100.0 0.9 shard_map.94
  (3 shorter events, 0.0 us)
Async XLA Ops:
  2.4 21.2 %all-to-all-start = ((f32[16,4,8,128]{3,2,1,0:T(8,128)}), f32[16,4,8,128]{3,2,1,0:T(8,128)S(1)}, u32[]{:S(2)}, u32[]{:S(2)}) async-start(f32[16,4,8,128]{3,2,1,0:T(8,128)} %get-tuple-element.21), calls=%async_computation | async-start | bytes 524288 | tf_op jit(solution)/shard_map/all_to_all | solution.py:527
  12.4 1.9 %collective-permute-start = (f32[4,4,128]{2,1,0:T(4,128)S(1)}, f32[4,4,128]{2,1,0:T(4,128)S(1)}, u32[]{:S(2)}, u32[]{:S(2)}) collective-permute-start(f32[4,4,128]{2,1,0:T(4,128)S(1)} %get-tuple-element.25.refs_0_), channel_id=1, source_target_pairs={{0,1},{1,0},{2,3},{3,2},{4,5},{5,4},{6,7},{7,6},{8,9},{9,8},{10,11... | collective-permute-start | bytes 24584 | tf_op jit(solution)/shard_map/ppermute | solution.py:506
  14.3 4.5 %collective-permute-start.3 = (f32[4,4,128]{2,1,0:T(4,128)S(1)}, f32[4,4,128]{2,1,0:T(4,128)S(1)}, u32[]{:S(2)}, u32[]{:S(2)}) collective-permute-start(f32[4,4,128]{2,1,0:T(4,128)S(1)} %shard_map.88.refs_0_), channel_id=1, source_target_pairs={{0,6},{1,7},{2,4},{3,5},{4,2},{5,3},{6,0},{7,1},{8,14},{9,15},{10,... | collective-permute-start | bytes 24584 | tf_op jit(solution)/shard_map/ppermute | solution.py:506
  17.0 4.0 %collective-permute-start.2 = (f32[4,4,128]{2,1,0:T(4,128)S(1)}, f32[4,4,128]{2,1,0:T(4,128)S(1)}, u32[]{:S(2)}, u32[]{:S(2)}) collective-permute-start(f32[4,4,128]{2,1,0:T(4,128)S(1)} %shard_map.88.refs_0_), channel_id=1, source_target_pairs={{0,4},{1,5},{2,6},{3,7},{4,0},{5,1},{6,2},{7,3},{8,12},{9,13},{10,... | collective-permute-start | bytes 24584 | tf_op jit(solution)/shard_map/ppermute | solution.py:506
  17.4 3.7 %collective-permute-start.1 = (f32[4,4,128]{2,1,0:T(4,128)S(1)}, f32[4,4,128]{2,1,0:T(4,128)S(1)}, u32[]{:S(2)}, u32[]{:S(2)}) collective-permute-start(f32[4,4,128]{2,1,0:T(4,128)S(1)} %shard_map.88.refs_0_), channel_id=1, source_target_pairs={{0,2},{1,3},{2,0},{3,1},{4,6},{5,7},{6,4},{7,5},{8,10},{9,11},{10,... | collective-permute-start | bytes 24584 | tf_op jit(solution)/shard_map/ppermute | solution.py:506
  21.1 6.9 %collective-permute-start.4 = (f32[4,4,128]{2,1,0:T(4,128)S(1)}, f32[4,4,128]{2,1,0:T(4,128)S(1)}, u32[]{:S(2)}, u32[]{:S(2)}) collective-permute-start(f32[4,4,128]{2,1,0:T(4,128)S(1)} %shard_map.89.refs_0_), channel_id=1, source_target_pairs={{0,8},{1,9},{2,10},{3,11},{4,12},{5,13},{6,14},{7,15},{8,0},{9,1},... | collective-permute-start | bytes 24584 | tf_op jit(solution)/shard_map/ppermute | solution.py:506
